TPU v7x, 128 devices: a whole 4x4x4 slice. The times are simulated.
128 devices in a mesh: hull: 8 (over y, core), blk: 16 (over x, z).
Axes of the slice: x: 4, y: 4, z: 4, core: 2. Of those that a mesh axis runs over, the one named last changes fastest.
Arguments:
- source: float32 [7, 64, 32768], P(None, 'hull', 'blk'), may hold values from -500 to 500
- jacobian: float32 [7, 7, 64, 32768], P(None, None, 'hull', 'blk'), may hold values from -0.03 to 0.5, as said below
- face_coef: float32 [4, 7, 64, 32768], P(None, None, 'hull', 'blk'), may hold values from 0.1 to 1.5
- active: int32 [64, 32768], P('hull', 'blk'), may hold values 0 or 1
Outputs:
- adjoint: float32 [7, 64, 32768], P(None, 'hull', 'blk')
- residual: float32 [7, 64, 32768], P(None, 'hull', 'blk')
- level_rms: float32 [3], replicated
Inputs may be any that keep to these rules, and one draw needn't show every extreme that they name: `jacobian`: in each tile the diagonal entry exceeds the sum of magnitudes of the other entries of its row.
All inputs are finite; a program needn't handle non-finite values. No bound on the sum of `active` on one device may be relied on, other than what follows from the above.
Results may differ from a plain program's by a relative error of at most 0.0003.
Values sent between devices are 32-bit elements; how exact they have to be, the bound alone decides.
No kernel may reach another device: no remote copies, remote signals or barrier semaphores. Data moves between devices by JAX's collectives and lax.ppermute only.
A program may use at most 128 MiB of HBM per device.

v0:
```python
import jax
import jax.numpy as jnp
from jax import lax
from jax.sharding import PartitionSpec as P

LEVELS = 2
SWEEPS = 2
COARSE_SWEEPS = 4


damping = 0.7


def with_halo(cells, sides, width):
    for axis, dim in sides:
        count = lax.axis_size(axis)
        ends = count - 1
        head = lax.slice_in_dim(cells, 0, width, axis=dim)
        tail = lax.slice_in_dim(cells, cells.shape[dim] - width, cells.shape[dim], axis=dim)
        cells = jnp.concatenate(
            [
                lax.ppermute(tail, axis, [(i, (i + 1) % count) for i in range(ends)]),
                cells,
                lax.ppermute(head, axis, [((i + 1) % count, i) for i in range(ends)]),
            ],
            axis=dim,
        )
    return cells


def shifted(block, axis, distance):
    devices = range(lax.axis_size(axis))
    route = [(i - distance, i) for i in devices if i - distance in devices]
    return lax.ppermute(block, axis, route)


def partner_2(block, axis, distance):
    count = lax.axis_size(axis)
    route = []
    for low in range(count):
        high = low | 1 << distance
        if high != low and high < count:
            route += [(low, high), (high, low)]
    return lax.ppermute(block, axis, route)


def diagonal_of(jacobian, couple):
    return jnp.stack([jacobian[field, field] for field in range(jacobian.shape[0])]) + couple[0]


def block_width(columns):
    return min(columns, 256)


def pair_sum(array):
    columns = array.shape[-1]
    width = block_width(columns)
    rows_idx = lax.broadcasted_iota(jnp.int32, (width, width // 2), 0)
    cols_idx = lax.broadcasted_iota(jnp.int32, (width, width // 2), 1)
    pairing = (rows_idx // 2 == cols_idx).astype(jnp.float32)
    blocks = array.reshape(array.shape[:-1] + (columns // width, width))
    summed = jnp.einsum("...kw,wh->...kh", blocks, pairing, precision=lax.Precision.HIGHEST)
    return summed.reshape(array.shape[:-1] + (columns // 2,))


def expand(array):
    columns = array.shape[-1] * 2
    width = block_width(columns)
    rows_idx = lax.broadcasted_iota(jnp.int32, (width // 2, width), 0)
    cols_idx = lax.broadcasted_iota(jnp.int32, (width // 2, width), 1)
    spread = (cols_idx // 2 == rows_idx).astype(jnp.float32)
    blocks = array.reshape(array.shape[:-1] + (columns // width, width // 2))
    copied = jnp.einsum("...kh,hw->...kw", blocks, spread, precision=lax.Precision.HIGHEST)
    return copied.reshape(array.shape[:-1] + (columns,))


def coarsen_couple(couple):
    face_sum = pair_sum(couple[0])
    columns = couple.shape[-1]
    even_mask = (lax.broadcasted_iota(jnp.int32, (columns,), 0) % 2 == 0).astype(jnp.float32)
    east_even = pair_sum(couple[1] * even_mask)
    west_odd = pair_sum(couple[2] * (1.0 - even_mask))
    west_even = pair_sum(couple[2] * even_mask)
    east_odd = pair_sum(couple[1] * (1.0 - even_mask))
    north = pair_sum(couple[3])
    south = pair_sum(couple[4])
    return jnp.stack([face_sum - west_even - east_odd, east_even, west_odd, north, south])


def join(mine, partner, bitnum):
    lower = lax.axis_index("blk") // 2**bitnum % 2 == 0
    return jnp.where(
        lower, jnp.concatenate([mine, partner], axis=-1), jnp.concatenate([partner, mine], axis=-1)
    )


def apply_span(vector, level, jacobian, couple):
    span = 2**level
    row_padded = with_halo(vector, (("hull", 1),), 1)
    left = shifted(vector[..., -1:], "blk", span)
    right = shifted(vector[..., :1], "blk", -span)
    before = jnp.concatenate([left, vector[..., :-1]], axis=-1)
    after = jnp.concatenate([vector[..., 1:], right], axis=-1)
    upper = row_padded[:, :-2, :]
    lower_rows = row_padded[:, 2:, :]
    result = couple[0] * vector
    result = result - couple[1] * before
    result = result - couple[2] * after
    result = result - couple[3] * upper
    result = result - couple[4] * lower_rows
    for field in range(jacobian.shape[0]):
        result = result + jacobian[field] * vector[field]
    return result


def operate(vector, level, level_ops):
    return apply_span(vector, level, level_ops[0], level_ops[1])


def smooth(vector, target, level, level_ops, diagonal):
    return vector + damping * (target - operate(vector, level, level_ops)) / diagonal


def prolong(coarse, level):
    half = coarse.shape[-1] // 2
    start = lax.axis_index("blk") // 2**level % 2 * half
    return expand(lax.dynamic_slice_in_dim(coarse, start, half, 2))


def record(local_sum):
    return lax.psum(local_sum, ("hull", "blk"))


def on_device(source, jacobian, face_coef, active):
    fields = source.shape[0]
    rows_here = source.shape[1]
    columns = source.shape[2]
    padded = with_halo(face_coef, (("hull", 2), ("blk", 3)), 1)
    east = padded[0][:, 1:-1, 0:columns]
    west = padded[1][:, 1:-1, 2:]
    north = padded[2][:, 0:rows_here, 1:-1]
    south = padded[3][:, 2:, 1:-1]
    face_sum = face_coef[0] + face_coef[1] + face_coef[2] + face_coef[3]
    couple = jnp.stack([face_sum, east, west, north, south])
    cell_mask = active.astype(jnp.float32)
    diagonal = diagonal_of(jacobian, couple)
    fine_ops = (jacobian, couple)
    level_ops = [fine_ops]
    diagonals = [diagonal]
    targets = [source]
    adjoint = jnp.zeros(source.shape, jnp.float32)
    for sweep in range(SWEEPS):
        adjoint = smooth(adjoint, source, 0, fine_ops, diagonal) * cell_mask
    residual = (source - operate(adjoint, 0, fine_ops)) * cell_mask
    squares = [record(jnp.sum(residual * residual))]
    corrections = [adjoint]
    jac_level, couple_level = (jacobian, couple)
    for level in range(1, LEVELS + 1):
        bitnum = level - 1
        jac_coarse = pair_sum(jac_level)
        couple_coarse = coarsen_couple(couple_level)
        partner = partner_2((jac_coarse, couple_coarse), "blk", bitnum)
        jac_level = join(jac_coarse, partner[0], bitnum)
        couple_level = join(couple_coarse, partner[1], bitnum)
        diagonal = diagonal_of(jac_level, couple_level)
        current_ops = (jac_level, couple_level)
        restricted = pair_sum(residual)
        level_target = join(restricted, partner_2(restricted, "blk", bitnum), bitnum)
        correction = jnp.zeros(level_target.shape, jnp.float32)
        count = SWEEPS if level < LEVELS else COARSE_SWEEPS
        for sweep in range(count):
            correction = smooth(correction, level_target, level, current_ops, diagonal)
        level_ops.append(current_ops)
        diagonals.append(diagonal)
        targets.append(level_target)
        corrections.append(correction)
        if level < LEVELS:
            residual = level_target - operate(correction, level, current_ops)
            squares.append(record(jnp.sum(residual * residual)))
    level = 1
    correction = corrections[level] + prolong(corrections[level + 1], level)
    for sweep in range(SWEEPS):
        correction = smooth(correction, targets[level], level, level_ops[level], diagonals[level])
    corrections[level] = correction
    adjoint = adjoint + prolong(corrections[1], 0) * cell_mask
    for sweep in range(SWEEPS):
        adjoint = smooth(adjoint, source, 0, fine_ops, diagonals[0]) * cell_mask
    residual = (source - operate(adjoint, 0, fine_ops)) * cell_mask
    squares.append(record(jnp.sum(residual * residual)))
    stacked = jnp.stack(squares)
    cell_count = fields * rows_here * columns * lax.axis_size("hull") * lax.axis_size("blk")
    level_rms = jnp.sqrt(stacked / float(cell_count))
    return (adjoint, residual, level_rms)


def solution(mesh):
    return jax.shard_map(
        on_device,
        mesh=mesh,
        in_specs=(
            P(None, "hull", "blk"),
            P(None, None, "hull", "blk"),
            P(None, None, "hull", "blk"),
            P("hull", "blk"),
        ),
        out_specs=(P(None, "hull", "blk"), P(None, "hull", "blk"), P()),
        check_vma=False,
    )
```

profile of v0, /device:TPU:0, one launch (start us, length us, event | category | flops | bytes accessed | tf_op | source)
XLA Modules:
  0.0 494.6 jit_solution(13115578030521415145)
XLA Ops:
  1.2 4.5 collective-permute-start.4
  7.0 3.2 fusion.352
  14.3 4.0 collective-permute-start.6
  25.0 4.5 fusion.9
  33.3 4.6 collective-permute-start.2
  44.4 3.4 collective-permute-done.3
  47.8 5.1 %concatenate.236 = f32[4,7,10,2050]{3,2,1,0:T(8,128)} concatenate(f32[4,7,10,1]{3,2,1,0:T(8,128)S(1)} %collective-permute-done.2, f32[4,7,10,2048]{3,2,1,0:T(8,128)} %copy-done.18, f32[4,7,10,1]{3,2,1,0:T(8,128)S(1)} %collective-permute-done.3), dimensions={3} | concatenate | bytes 4592000 | tf_op jit(solution)/shard_map/concatenate | solution.py:20
  52.9 2.5 slice_bitcast_fusion.1
  57.8 2.5 fusion.230
  65.5 2.7 collective-permute-start.10
  69.5 3.8 collective-permute-start.8
  81.6 2.3 fusion.245
  85.6 2.3 fusion.243
  89.5 2.3 fusion.24
  93.4 2.3 fusion.21
  104.0 2.6 collective-permute-start.17
  106.6 5.1 %broadcast_multiply_fusion = (f32[7,8,2048]{2,1,0:T(8,128)S(1)}, f32[7,8,2048]{2,1,0:T(8,128)}) fusion(f32[8,2048]{1,0:T(8,128)S(1)} %convert_element_type.50, f32[7,8,2048]{2,1,0:T(8,128)} %copy-done.24, f32[7,8,2048]{2,1,0:T(8,128)} %get-tuple-element.21, f32[7,8,2048]{2,1,0:T(8,128)} %param.4, f32[8,2048]{1,0:T(8,128)} %get-tuple-element.194, ...), kind=kLoop, calls=%fused_computation.446 | loop fusion | flops 3670016 | bytes 9355264 | tf_op jit(solution)/shard_map/mul | solution.py:153
  112.1 2.7 collective-permute-start.14
  119.6 13.4 %collective-permute-done.12 = f32[7,8,1]{2,1,0:T(8,128)S(1)} collective-permute-done((f32[7,8,1]{2,1,0:T(8,128)S(1)}, f32[7,8,1]{2,1,0:T(8,128)S(1)}, u32[]{:S(2)}, u32[]{:S(2)}) %collective-permute-start.12) | collective-permute-done | bytes 256 | tf_op jit(solution)/shard_map/ppermute | solution.py:34
  133.0 7.3 %collective-permute-start.18 = (f32[7,8,1]{2,1,0:T(8,128)}, f32[7,8,1]{2,1,0:T(8,128)S(1)}, u32[]{:S(2)}, u32[]{:S(2)}) collective-permute-start(f32[7,8,1]{2,1,0:T(8,128)} %broadcast.156), channel_id=1, source_target_pairs={{0,2},{1,3},{2,4},{3,5},{4,6},{5,7},{6,8},{7,9},{8,10},{9,11},{10,... | collective-permute-start | bytes 680 | tf_op jit(solution)/shard_map/ppermute | solution.py:34
  143.6 3.6 multiply_reduce_fusion.2
  148.9 2.9 maximum_select_fusion.4
  160.9 4.6 collective-permute-start.30
  165.6 15.1 %collective-permute-done.20 = f32[7,7,8,1024]{3,2,1,0:T(8,128)} collective-permute-done((f32[7,7,8,1024]{3,2,1,0:T(8,128)}, f32[7,7,8,1024]{3,2,1,0:T(8,128)}, u32[]{:S(2)}, u32[]{:S(2)}) %collective-permute-start.20) | collective-permute-done | bytes 1605664 | tf_op jit(solution)/shard_map/ppermute | solution.py:44
  180.6 3.6 maximum_select_fusion
  185.6 2.9 fusion.222
  197.9 6.4 %collective-permute-start.21 = (f32[7,8,1]{2,1,0:T(8,128)}, f32[7,8,1]{2,1,0:T(8,128)S(1)}, u32[]{:S(2)}, u32[]{:S(2)}) collective-permute-start(f32[7,8,1]{2,1,0:T(8,128)} %get-tuple-element.167), channel_id=1, source_target_pairs={{0,2},{1,3},{2,4},{3,5},{4,6},{5,7},{6,8},{7,9},{8,10},{9,11},{10,... | collective-permute-start | bytes 680 | tf_op jit(solution)/shard_map/ppermute | solution.py:34
  205.6 3.9 fusion
  209.5 2.6 reshape.175
  212.1 4.5 collective-permute-start.33
  216.7 3.5 fusion.157
  222.6 3.8 collective-permute-start.27
  227.7 24.0 %collective-permute-done.25 = f32[7,8,1]{2,1,0:T(8,128)S(1)} collective-permute-done((f32[7,8,1]{2,1,0:T(8,128)S(1)}, f32[7,8,1]{2,1,0:T(8,128)S(1)}, u32[]{:S(2)}, u32[]{:S(2)}) %collective-permute-start.25) | collective-permute-done | bytes 256 | tf_op jit(solution)/shard_map/ppermute | solution.py:34
  253.0 6.4 %collective-permute-done.26 = f32[7,8,1]{2,1,0:T(8,128)S(1)} collective-permute-done((f32[7,8,1]{2,1,0:T(8,128)S(1)}, f32[7,8,1]{2,1,0:T(8,128)S(1)}, u32[]{:S(2)}, u32[]{:S(2)}) %collective-permute-start.26) | collective-permute-done | bytes 256 | tf_op jit(solution)/shard_map/ppermute | solution.py:34
  259.4 3.4 collective-permute-start.31
  268.7 4.6 collective-permute-start.29
  273.3 2.8 maximum_select_fusion.5
  276.1 2.6 maximum_select_fusion.3
  282.9 4.3 collective-permute-start.34
  288.7 4.2 collective-permute-done.35
  294.3 4.7 collective-permute-start.40
  300.2 3.3 collective-permute-start.38
  305.1 4.2 collective-permute-done.39
  310.7 4.3 collective-permute-start.44
  320.0 4.2 collective-permute-done.43
  329.9 4.0 collective-permute-start.48
  335.1 4.1 collective-permute-start.46
  340.8 5.7 %collective-permute-done.47 = f32[7,8,1]{2,1,0:T(8,128)S(1)} collective-permute-done((f32[7,8,1]{2,1,0:T(8,128)S(1)}, f32[7,8,1]{2,1,0:T(8,128)S(1)}, u32[]{:S(2)}, u32[]{:S(2)}) %collective-permute-start.47) | collective-permute-done | bytes 256 | tf_op jit(solution)/shard_map/ppermute | solution.py:34
  348.0 4.3 collective-permute-start.52
  353.5 3.6 collective-permute-start.50
  358.7 5.7 %collective-permute-done.51 = f32[7,8,1]{2,1,0:T(8,128)S(1)} collective-permute-done((f32[7,8,1]{2,1,0:T(8,128)S(1)}, f32[7,8,1]{2,1,0:T(8,128)S(1)}, u32[]{:S(2)}, u32[]{:S(2)}) %collective-permute-start.51) | collective-permute-done | bytes 256 | tf_op jit(solution)/shard_map/ppermute | solution.py:34
  370.3 4.3 collective-permute-start.56
  375.9 3.5 collective-permute-start.54
  380.9 4.2 collective-permute-done.55
  385.2 2.8 fusion.260
  388.4 4.4 collective-permute-start.60
  394.1 2.9 collective-permute-start.58
  398.5 4.2 collective-permute-done.59
  404.3 4.3 collective-permute-start.64
  409.9 4.0 collective-permute-start.62
  415.4 4.2 collective-permute-done.63
  419.7 2.4 multiply_reduce_fusion
  422.1 69.8 %all-reduce.8 = (f32[1]{0:T(128)}, f32[1]{0:T(128)}, f32[1]{0:T(128)}) all-reduce(f32[1]{0:T(128)} %bitcast.163, f32[1]{0:T(128)} %bitcast.162, f32[1]{0:T(128)} %bitcast.161), channel_id=1, replica_groups=mesh['hull'=8,'blk'=16] {'hull','blk'}, use_global_device_ids=true, to_apply=%region_5.6 | all-reduce | flops 3 | bytes 24 | tf_op jit(solution)/shard_map/psum | solution.py:131
  491.9 2.5 fusion.327
  (312 shorter events, 140.0 us)
Async XLA Ops:
  1.2 54.2 %collective-permute-start.4 = (f32[7,8,1]{2,1,0:T(8,128)}, f32[7,8,1]{2,1,0:T(8,128)}, u32[]{:S(2)}, u32[]{:S(2)}) collective-permute-start(f32[7,8,1]{2,1,0:T(8,128)} %broadcast.156), channel_id=1, source_target_pairs={{0,1},{1,2},{2,3},{3,4},{4,5},{5,6},{6,7},{7,8},{8,9},{9,10},{10,1... | collective-permute-start | bytes 680 | tf_op jit(solution)/shard_map/ppermute | solution.py:34
  5.7 49.7 %collective-permute-start.5 = (f32[7,8,1]{2,1,0:T(8,128)}, f32[7,8,1]{2,1,0:T(8,128)}, u32[]{:S(2)}, u32[]{:S(2)}) collective-permute-start(f32[7,8,1]{2,1,0:T(8,128)} %broadcast.156), channel_id=1, source_target_pairs={{1,0},{2,1},{3,2},{4,3},{5,4},{6,5},{7,6},{8,7},{9,8},{10,9},{11,1... | collective-permute-start | bytes 680 | tf_op jit(solution)/shard_map/ppermute | solution.py:34
  10.2 19.4 %collective-permute-start = (f32[4,7,1,2048]{3,2,1,0:T(1,128)}, f32[4,7,1,2048]{3,2,1,0:T(1,128)}, u32[]{:S(2)}, u32[]{:S(2)}) collective-permute-start(f32[4,7,1,2048]{3,2,1,0:T(1,128)} %get-tuple-element.34), channel_id=1, source_target_pairs={{0,16},{16,32},{32,48},{48,64},{64,80},{80,96},{96,112},{1,17},{17... | collective-permute-start | bytes 688136 | tf_op jit(solution)/shard_map/ppermute | solution.py:22
  12.4 17.2 %collective-permute-start.1 = (f32[4,7,1,2048]{3,2,1,0:T(1,128)}, f32[4,7,1,2048]{3,2,1,0:T(1,128)}, u32[]{:S(2)}, u32[]{:S(2)}) collective-permute-start(f32[4,7,1,2048]{3,2,1,0:T(1,128)} %get-tuple-element.35), channel_id=1, source_target_pairs={{16,0},{32,16},{48,32},{64,48},{80,64},{96,80},{112,96},{17,1},{33... | collective-permute-start | bytes 688136 | tf_op jit(solution)/shard_map/ppermute | solution.py:24
  14.3 41.2 %collective-permute-start.6 = (f32[7,1,2048]{2,1,0:T(1,128)}, f32[7,1,2048]{2,1,0:T(1,128)S(1)}, u32[]{:S(2)}, u32[]{:S(2)}) collective-permute-start(f32[7,1,2048]{2,1,0:T(1,128)} %broadcast.157), channel_id=1, source_target_pairs={{0,16},{16,32},{32,48},{48,64},{64,80},{80,96},{96,112},{1,17},{17... | collective-permute-start | bytes 172040 | tf_op jit(solution)/shard_map/ppermute | solution.py:22
  33.3 9.8 %collective-permute-start.2 = (f32[4,7,10,1]{3,2,1,0:T(8,128)S(1)}, f32[4,7,10,1]{3,2,1,0:T(8,128)S(1)}, u32[]{:S(2)}, u32[]{:S(2)}) collective-permute-start(f32[4,7,10,1]{3,2,1,0:T(8,128)S(1)} %get-tuple-element.28), channel_id=1, source_target_pairs={{0,1},{1,2},{2,3},{3,4},{4,5},{5,6},{6,7},{7,8},{8,9},{9,10},{10,1... | collective-permute-start | bytes 3368 | tf_op jit(solution)/shard_map/ppermute | solution.py:22
  37.9 10.0 %collective-permute-start.3 = (f32[4,7,10,1]{3,2,1,0:T(8,128)S(1)}, f32[4,7,10,1]{3,2,1,0:T(8,128)S(1)}, u32[]{:S(2)}, u32[]{:S(2)}) collective-permute-start(f32[4,7,10,1]{3,2,1,0:T(8,128)S(1)} %get-tuple-element.27), channel_id=1, source_target_pairs={{1,0},{2,1},{3,2},{4,3},{5,4},{6,5},{7,6},{8,7},{9,8},{10,9},{11,1... | collective-permute-start | bytes 3368 | tf_op jit(solution)/shard_map/ppermute | solution.py:24
  43.1 12.4 %collective-permute-start.7 = (f32[7,1,2048]{2,1,0:T(1,128)}, f32[7,1,2048]{2,1,0:T(1,128)S(1)}, u32[]{:S(2)}, u32[]{:S(2)}) collective-permute-start(f32[7,1,2048]{2,1,0:T(1,128)} %broadcast.157), channel_id=1, source_target_pairs={{16,0},{32,16},{48,32},{64,48},{80,64},{96,80},{112,96},{17,1},{33... | collective-permute-start | bytes 172040 | tf_op jit(solution)/shard_map/ppermute | solution.py:24
  65.5 41.1 %collective-permute-start.10 = (f32[7,1,2048]{2,1,0:T(1,128)}, f32[7,1,2048]{2,1,0:T(1,128)}, u32[]{:S(2)}, u32[]{:S(2)}) collective-permute-start(f32[7,1,2048]{2,1,0:T(1,128)} %get-tuple-element.187), channel_id=1, source_target_pairs={{0,16},{16,32},{32,48},{48,64},{64,80},{80,96},{96,112},{1,17},{17... | collective-permute-start | bytes 172040 | tf_op jit(solution)/shard_map/ppermute | solution.py:22
  68.2 38.4 %collective-permute-start.11 = (f32[7,1,2048]{2,1,0:T(1,128)}, f32[7,1,2048]{2,1,0:T(1,128)}, u32[]{:S(2)}, u32[]{:S(2)}) collective-permute-start(f32[7,1,2048]{2,1,0:T(1,128)} %get-tuple-element.188), channel_id=1, source_target_pairs={{16,0},{32,16},{48,32},{64,48},{80,64},{96,80},{112,96},{17,1},{33... | collective-permute-start | bytes 172040 | tf_op jit(solution)/shard_map/ppermute | solution.py:24
  69.5 37.1 %collective-permute-start.8 = (f32[7,8,1]{2,1,0:T(8,128)}, f32[7,8,1]{2,1,0:T(8,128)}, u32[]{:S(2)}, u32[]{:S(2)}) collective-permute-start(f32[7,8,1]{2,1,0:T(8,128)} %get-tuple-element.183), channel_id=1, source_target_pairs={{0,1},{1,2},{2,3},{3,4},{4,5},{5,6},{6,7},{7,8},{8,9},{9,10},{10,1... | collective-permute-start | bytes 680 | tf_op jit(solution)/shard_map/ppermute | solution.py:34
  73.4 33.2 %collective-permute-start.9 = (f32[7,8,1]{2,1,0:T(8,128)S(1)}, f32[7,8,1]{2,1,0:T(8,128)}, u32[]{:S(2)}, u32[]{:S(2)}) collective-permute-start(f32[7,8,1]{2,1,0:T(8,128)S(1)} %get-tuple-element.184), channel_id=1, source_target_pairs={{1,0},{2,1},{3,2},{4,3},{5,4},{6,5},{7,6},{8,7},{9,8},{10,9},{11,1... | collective-permute-start | bytes 680 | tf_op jit(solution)/shard_map/ppermute | solution.py:34
  104.0 44.9 %collective-permute-start.17 = (f32[5,7,8,1024]{3,2,1,0:T(8,128)}, f32[5,7,8,1024]{3,2,1,0:T(8,128)}, u32[]{:S(2)}, u32[]{:S(2)}) collective-permute-start(f32[5,7,8,1024]{3,2,1,0:T(8,128)} %constant_dynamic-update-slice_fusion.7), channel_id=1, source_target_pairs={{0,1},{1,0},{2,3},{3,2},{4,5},{5,4},{6,7},{7,6},{8,9},{9,8},{10,11... | collective-permute-start | bytes 3440648 | tf_op jit(solution)/shard_map/ppermute | solution.py:44
  112.1 29.6 %collective-permute-start.14 = (f32[7,1,2048]{2,1,0:T(1,128)S(1)}, f32[7,1,2048]{2,1,0:T(1,128)S(1)}, u32[]{:S(2)}, u32[]{:S(2)}) collective-permute-start(f32[7,1,2048]{2,1,0:T(1,128)S(1)} %get-tuple-element.174), channel_id=1, source_target_pairs={{0,16},{16,32},{32,48},{48,64},{64,80},{80,96},{96,112},{1,17},{17... | collective-permute-start | bytes 172040 | tf_op jit(solution)/shard_map/ppermute | solution.py:22
  114.8 28.9 %collective-permute-start.15 = (f32[7,1,2048]{2,1,0:T(1,128)S(1)}, f32[7,1,2048]{2,1,0:T(1,128)S(1)}, u32[]{:S(2)}, u32[]{:S(2)}) collective-permute-start(f32[7,1,2048]{2,1,0:T(1,128)S(1)} %get-tuple-element.175), channel_id=1, source_target_pairs={{16,0},{32,16},{48,32},{64,48},{80,64},{96,80},{112,96},{17,1},{33... | collective-permute-start | bytes 172040 | tf_op jit(solution)/shard_map/ppermute | solution.py:24
  116.1 16.9 %collective-permute-start.12 = (f32[7,8,1]{2,1,0:T(8,128)S(1)}, f32[7,8,1]{2,1,0:T(8,128)S(1)}, u32[]{:S(2)}, u32[]{:S(2)}) collective-permute-start(f32[7,8,1]{2,1,0:T(8,128)S(1)} %get-tuple-element.170), channel_id=1, source_target_pairs={{0,1},{1,2},{2,3},{3,4},{4,5},{5,6},{6,7},{7,8},{8,9},{9,10},{10,1... | collective-permute-start | bytes 680 | tf_op jit(solution)/shard_map/ppermute | solution.py:34
  118.3 22.1 %collective-permute-start.13 = (f32[7,8,1]{2,1,0:T(8,128)S(1)}, f32[7,8,1]{2,1,0:T(8,128)S(1)}, u32[]{:S(2)}, u32[]{:S(2)}) collective-permute-start(f32[7,8,1]{2,1,0:T(8,128)S(1)} %get-tuple-element.171), channel_id=1, source_target_pairs={{1,0},{2,1},{3,2},{4,3},{5,4},{6,5},{7,6},{8,7},{9,8},{10,9},{11,1... | collective-permute-start | bytes 680 | tf_op jit(solution)/shard_map/ppermute | solution.py:34
  133.0 51.3 %collective-permute-start.18 = (f32[7,8,1]{2,1,0:T(8,128)}, f32[7,8,1]{2,1,0:T(8,128)S(1)}, u32[]{:S(2)}, u32[]{:S(2)}) collective-permute-start(f32[7,8,1]{2,1,0:T(8,128)} %broadcast.156), channel_id=1, source_target_pairs={{0,2},{1,3},{2,4},{3,5},{4,6},{5,7},{6,8},{7,9},{8,10},{9,11},{10,... | collective-permute-start | bytes 680 | tf_op jit(solution)/shard_map/ppermute | solution.py:34
  140.3 44.0 %collective-permute-start.19 = (f32[7,8,1]{2,1,0:T(8,128)}, f32[7,8,1]{2,1,0:T(8,128)}, u32[]{:S(2)}, u32[]{:S(2)}) collective-permute-start(f32[7,8,1]{2,1,0:T(8,128)} %broadcast.156), channel_id=1, source_target_pairs={{2,0},{3,1},{4,2},{5,3},{6,4},{7,5},{8,6},{9,7},{10,8},{11,9},{12,... | collective-permute-start | bytes 680 | tf_op jit(solution)/shard_map/ppermute | solution.py:34
  141.7 39.0 %collective-permute-start.20 = (f32[7,7,8,1024]{3,2,1,0:T(8,128)}, f32[7,7,8,1024]{3,2,1,0:T(8,128)}, u32[]{:S(2)}, u32[]{:S(2)}) collective-permute-start(f32[7,7,8,1024]{3,2,1,0:T(8,128)} %reshape.172), channel_id=1, source_target_pairs={{0,1},{1,0},{2,3},{3,2},{4,5},{5,4},{6,7},{7,6},{8,9},{9,8},{10,11... | collective-permute-start | bytes 4816904 | tf_op jit(solution)/shard_map/ppermute | solution.py:44
  148.5 37.0 %collective-permute-start.16 = (f32[7,8,1024]{2,1,0:T(8,128)}, f32[7,8,1024]{2,1,0:T(8,128)}, u32[]{:S(2)}, u32[]{:S(2)}) collective-permute-start(f32[7,8,1024]{2,1,0:T(8,128)} %reshape.166), channel_id=1, source_target_pairs={{0,1},{1,0},{2,3},{3,2},{4,5},{5,4},{6,7},{7,6},{8,9},{9,8},{10,11... | collective-permute-start | bytes 688136 | tf_op jit(solution)/shard_map/ppermute | solution.py:44
  160.9 112.4 %collective-permute-start.30 = (f32[5,7,8,1024]{3,2,1,0:T(8,128)}, f32[5,7,8,1024]{3,2,1,0:T(8,128)}, u32[]{:S(2)}, u32[]{:S(2)}) collective-permute-start(f32[5,7,8,1024]{3,2,1,0:T(8,128)} %constant_dynamic-update-slice_fusion.12), channel_id=1, source_target_pairs={{0,2},{2,0},{1,3},{3,1},{4,6},{6,4},{5,7},{7,5},{8,10},{10,8},{9,1... | collective-permute-start | bytes 3440648 | tf_op jit(solution)/shard_map/ppermute | solution.py:44
  194.7 22.0 %collective-permute-start.23 = (f32[7,1,2048]{2,1,0:T(1,128)}, f32[7,1,2048]{2,1,0:T(1,128)}, u32[]{:S(2)}, u32[]{:S(2)}) collective-permute-start(f32[7,1,2048]{2,1,0:T(1,128)} %get-tuple-element.168), channel_id=1, source_target_pairs={{0,16},{16,32},{32,48},{48,64},{64,80},{80,96},{96,112},{1,17},{17... | collective-permute-start | bytes 172040 | tf_op jit(solution)/shard_map/ppermute | solution.py:22
  196.6 20.0 %collective-permute-start.24 = (f32[7,1,2048]{2,1,0:T(1,128)}, f32[7,1,2048]{2,1,0:T(1,128)}, u32[]{:S(2)}, u32[]{:S(2)}) collective-permute-start(f32[7,1,2048]{2,1,0:T(1,128)} %get-tuple-element.169), channel_id=1, source_target_pairs={{16,0},{32,16},{48,32},{64,48},{80,64},{96,80},{112,96},{17,1},{33... | collective-permute-start | bytes 172040 | tf_op jit(solution)/shard_map/ppermute | solution.py:24
  197.9 14.2 %collective-permute-start.21 = (f32[7,8,1]{2,1,0:T(8,128)}, f32[7,8,1]{2,1,0:T(8,128)S(1)}, u32[]{:S(2)}, u32[]{:S(2)}) collective-permute-start(f32[7,8,1]{2,1,0:T(8,128)} %get-tuple-element.167), channel_id=1, source_target_pairs={{0,2},{1,3},{2,4},{3,5},{4,6},{5,7},{6,8},{7,9},{8,10},{9,11},{10,... | collective-permute-start | bytes 680 | tf_op jit(solution)/shard_map/ppermute | solution.py:34
  204.3 12.3 %collective-permute-start.22 = (f32[7,8,1]{2,1,0:T(8,128)}, f32[7,8,1]{2,1,0:T(8,128)S(1)}, u32[]{:S(2)}, u32[]{:S(2)}) collective-permute-start(f32[7,8,1]{2,1,0:T(8,128)} %get-tuple-element.166), channel_id=1, source_target_pairs={{2,0},{3,1},{4,2},{5,3},{6,4},{7,5},{8,6},{9,7},{10,8},{11,9},{12,... | collective-permute-start | bytes 680 | tf_op jit(solution)/shard_map/ppermute | solution.py:34
  212.1 64.0 %collective-permute-start.33 = (f32[7,7,8,1024]{3,2,1,0:T(8,128)}, f32[7,7,8,1024]{3,2,1,0:T(8,128)}, u32[]{:S(2)}, u32[]{:S(2)}) collective-permute-start(f32[7,7,8,1024]{3,2,1,0:T(8,128)} %reshape.175), channel_id=1, source_target_pairs={{0,2},{2,0},{1,3},{3,1},{4,6},{6,4},{5,7},{7,5},{8,10},{10,8},{9,1... | collective-permute-start | bytes 4816904 | tf_op jit(solution)/shard_map/ppermute | solution.py:44
  220.5 31.2 %collective-permute-start.25 = (f32[7,8,1]{2,1,0:T(8,128)S(1)}, f32[7,8,1]{2,1,0:T(8,128)S(1)}, u32[]{:S(2)}, u32[]{:S(2)}) collective-permute-start(f32[7,8,1]{2,1,0:T(8,128)S(1)} %get-tuple-element.144), channel_id=1, source_target_pairs={{0,2},{1,3},{2,4},{3,5},{4,6},{5,7},{6,8},{7,9},{8,10},{9,11},{10,... | collective-permute-start | bytes 680 | tf_op jit(solution)/shard_map/ppermute | solution.py:34
  222.6 40.2 %collective-permute-start.27 = (f32[7,1,2048]{2,1,0:T(1,128)S(1)}, f32[7,1,2048]{2,1,0:T(1,128)S(1)}, u32[]{:S(2)}, u32[]{:S(2)}) collective-permute-start(f32[7,1,2048]{2,1,0:T(1,128)S(1)} %get-tuple-element.148), channel_id=1, source_target_pairs={{0,16},{16,32},{32,48},{48,64},{64,80},{80,96},{96,112},{1,17},{17... | collective-permute-start | bytes 172040 | tf_op jit(solution)/shard_map/ppermute | solution.py:22
  226.4 37.7 %collective-permute-start.28 = (f32[7,1,2048]{2,1,0:T(1,128)S(1)}, f32[7,1,2048]{2,1,0:T(1,128)S(1)}, u32[]{:S(2)}, u32[]{:S(2)}) collective-permute-start(f32[7,1,2048]{2,1,0:T(1,128)S(1)} %get-tuple-element.149), channel_id=1, source_target_pairs={{16,0},{32,16},{48,32},{64,48},{80,64},{96,80},{112,96},{17,1},{33... | collective-permute-start | bytes 172040 | tf_op jit(solution)/shard_map/ppermute | solution.py:24
  251.7 7.7 %collective-permute-start.26 = (f32[7,8,1]{2,1,0:T(8,128)S(1)}, f32[7,8,1]{2,1,0:T(8,128)S(1)}, u32[]{:S(2)}, u32[]{:S(2)}) collective-permute-start(f32[7,8,1]{2,1,0:T(8,128)S(1)} %get-tuple-element.145), channel_id=1, source_target_pairs={{2,0},{3,1},{4,2},{5,3},{6,4},{7,5},{8,6},{9,7},{10,8},{11,9},{12,... | collective-permute-start | bytes 680 | tf_op jit(solution)/shard_map/ppermute | solution.py:34
  259.4 19.4 %collective-permute-start.31 = (f32[7,8,1]{2,1,0:T(8,128)}, f32[7,8,1]{2,1,0:T(8,128)S(1)}, u32[]{:S(2)}, u32[]{:S(2)}) collective-permute-start(f32[7,8,1]{2,1,0:T(8,128)} %broadcast.156), channel_id=1, source_target_pairs={{0,4},{1,5},{2,6},{3,7},{4,8},{5,9},{6,10},{7,11},{8,12},{9,13},{1... | collective-permute-start | bytes 680 | tf_op jit(solution)/shard_map/ppermute | solution.py:34
  262.8 16.0 %collective-permute-start.32 = (f32[7,8,1]{2,1,0:T(8,128)}, f32[7,8,1]{2,1,0:T(8,128)S(1)}, u32[]{:S(2)}, u32[]{:S(2)}) collective-permute-start(f32[7,8,1]{2,1,0:T(8,128)} %broadcast.156), channel_id=1, source_target_pairs={{4,0},{5,1},{6,2},{7,3},{8,4},{9,5},{10,6},{11,7},{12,8},{13,9},{1... | collective-permute-start | bytes 680 | tf_op jit(solution)/shard_map/ppermute | solution.py:34
  268.7 10.4 %collective-permute-start.29 = (f32[7,8,1024]{2,1,0:T(8,128)}, f32[7,8,1024]{2,1,0:T(8,128)S(1)}, u32[]{:S(2)}, u32[]{:S(2)}) collective-permute-start(f32[7,8,1024]{2,1,0:T(8,128)} %reshape.174), channel_id=1, source_target_pairs={{0,2},{2,0},{1,3},{3,1},{4,6},{6,4},{5,7},{7,5},{8,10},{10,8},{9,1... | collective-permute-start | bytes 688136 | tf_op jit(solution)/shard_map/ppermute | solution.py:44
  280.3 12.6 %collective-permute-start.36 = (f32[7,1,2048]{2,1,0:T(1,128)S(1)}, f32[7,1,2048]{2,1,0:T(1,128)S(1)}, u32[]{:S(2)}, u32[]{:S(2)}) collective-permute-start(f32[7,1,2048]{2,1,0:T(1,128)S(1)} %get-tuple-element.142), channel_id=1, source_target_pairs={{0,16},{16,32},{32,48},{48,64},{64,80},{80,96},{96,112},{1,17},{17... | collective-permute-start | bytes 172040 | tf_op jit(solution)/shard_map/ppermute | solution.py:22
  281.6 11.3 %collective-permute-start.37 = (f32[7,1,2048]{2,1,0:T(1,128)S(1)}, f32[7,1,2048]{2,1,0:T(1,128)S(1)}, u32[]{:S(2)}, u32[]{:S(2)}) collective-permute-start(f32[7,1,2048]{2,1,0:T(1,128)S(1)} %get-tuple-element.143), channel_id=1, source_target_pairs={{16,0},{32,16},{48,32},{64,48},{80,64},{96,80},{112,96},{17,1},{33... | collective-permute-start | bytes 172040 | tf_op jit(solution)/shard_map/ppermute | solution.py:24
  282.9 5.8 %collective-permute-start.34 = (f32[7,8,1]{2,1,0:T(8,128)S(1)}, f32[7,8,1]{2,1,0:T(8,128)S(1)}, u32[]{:S(2)}, u32[]{:S(2)}) collective-permute-start(f32[7,8,1]{2,1,0:T(8,128)S(1)} %get-tuple-element.141), channel_id=1, source_target_pairs={{0,4},{1,5},{2,6},{3,7},{4,8},{5,9},{6,10},{7,11},{8,12},{9,13},{1... | collective-permute-start | bytes 680 | tf_op jit(solution)/shard_map/ppermute | solution.py:34
  287.1 5.8 %collective-permute-start.35 = (f32[7,8,1]{2,1,0:T(8,128)S(1)}, f32[7,8,1]{2,1,0:T(8,128)S(1)}, u32[]{:S(2)}, u32[]{:S(2)}) collective-permute-start(f32[7,8,1]{2,1,0:T(8,128)S(1)} %get-tuple-element.140), channel_id=1, source_target_pairs={{4,0},{5,1},{6,2},{7,3},{8,4},{9,5},{10,6},{11,7},{12,8},{13,9},{1... | collective-permute-start | bytes 680 | tf_op jit(solution)/shard_map/ppermute | solution.py:34
  294.3 15.0 %collective-permute-start.40 = (f32[7,1,2048]{2,1,0:T(1,128)S(1)}, f32[7,1,2048]{2,1,0:T(1,128)S(1)}, u32[]{:S(2)}, u32[]{:S(2)}) collective-permute-start(f32[7,1,2048]{2,1,0:T(1,128)S(1)} %get-tuple-element.129), channel_id=1, source_target_pairs={{0,16},{16,32},{32,48},{48,64},{64,80},{80,96},{96,112},{1,17},{17... | collective-permute-start | bytes 172040 | tf_op jit(solution)/shard_map/ppermute | solution.py:22
  298.9 10.4 %collective-permute-start.41 = (f32[7,1,2048]{2,1,0:T(1,128)S(1)}, f32[7,1,2048]{2,1,0:T(1,128)S(1)}, u32[]{:S(2)}, u32[]{:S(2)}) collective-permute-start(f32[7,1,2048]{2,1,0:T(1,128)S(1)} %get-tuple-element.130), channel_id=1, source_target_pairs={{16,0},{32,16},{48,32},{64,48},{80,64},{96,80},{112,96},{17,1},{33... | collective-permute-start | bytes 172040 | tf_op jit(solution)/shard_map/ppermute | solution.py:24
  300.2 4.8 collective-permute-start.38
  303.5 5.8 %collective-permute-start.39 = (f32[7,8,1]{2,1,0:T(8,128)S(1)}, f32[7,8,1]{2,1,0:T(8,128)S(1)}, u32[]{:S(2)}, u32[]{:S(2)}) collective-permute-start(f32[7,8,1]{2,1,0:T(8,128)S(1)} %get-tuple-element.127), channel_id=1, source_target_pairs={{4,0},{5,1},{6,2},{7,3},{8,4},{9,5},{10,6},{11,7},{12,8},{13,9},{1... | collective-permute-start | bytes 680 | tf_op jit(solution)/shard_map/ppermute | solution.py:34
  310.7 13.5 %collective-permute-start.44 = (f32[7,1,2048]{2,1,0:T(1,128)S(1)}, f32[7,1,2048]{2,1,0:T(1,128)S(1)}, u32[]{:S(2)}, u32[]{:S(2)}) collective-permute-start(f32[7,1,2048]{2,1,0:T(1,128)S(1)} %get-tuple-element.116), channel_id=1, source_target_pairs={{0,16},{16,32},{32,48},{48,64},{64,80},{80,96},{96,112},{1,17},{17... | collective-permute-start | bytes 172040 | tf_op jit(solution)/shard_map/ppermute | solution.py:22
  315.0 9.3 %collective-permute-start.45 = (f32[7,1,2048]{2,1,0:T(1,128)S(1)}, f32[7,1,2048]{2,1,0:T(1,128)S(1)}, u32[]{:S(2)}, u32[]{:S(2)}) collective-permute-start(f32[7,1,2048]{2,1,0:T(1,128)S(1)} %get-tuple-element.117), channel_id=1, source_target_pairs={{16,0},{32,16},{48,32},{64,48},{80,64},{96,80},{112,96},{17,1},{33... | collective-permute-start | bytes 172040 | tf_op jit(solution)/shard_map/ppermute | solution.py:24
  318.5 5.8 %collective-permute-start.43 = (f32[7,8,1]{2,1,0:T(8,128)S(1)}, f32[7,8,1]{2,1,0:T(8,128)S(1)}, u32[]{:S(2)}, u32[]{:S(2)}) collective-permute-start(f32[7,8,1]{2,1,0:T(8,128)S(1)} %get-tuple-element.114), channel_id=1, source_target_pairs={{4,0},{5,1},{6,2},{7,3},{8,4},{9,5},{10,6},{11,7},{12,8},{13,9},{1... | collective-permute-start | bytes 680 | tf_op jit(solution)/shard_map/ppermute | solution.py:34
  329.9 16.7 %collective-permute-start.48 = (f32[7,1,2048]{2,1,0:T(1,128)S(1)}, f32[7,1,2048]{2,1,0:T(1,128)S(1)}, u32[]{:S(2)}, u32[]{:S(2)}) collective-permute-start(f32[7,1,2048]{2,1,0:T(1,128)S(1)} %get-tuple-element.103), channel_id=1, source_target_pairs={{0,16},{16,32},{32,48},{48,64},{64,80},{80,96},{96,112},{1,17},{17... | collective-permute-start | bytes 172040 | tf_op jit(solution)/shard_map/ppermute | solution.py:22
  333.8 12.7 %collective-permute-start.49 = (f32[7,1,2048]{2,1,0:T(1,128)S(1)}, f32[7,1,2048]{2,1,0:T(1,128)S(1)}, u32[]{:S(2)}, u32[]{:S(2)}) collective-permute-start(f32[7,1,2048]{2,1,0:T(1,128)S(1)} %get-tuple-element.104), channel_id=1, source_target_pairs={{16,0},{32,16},{48,32},{64,48},{80,64},{96,80},{112,96},{17,1},{33... | collective-permute-start | bytes 172040 | tf_op jit(solution)/shard_map/ppermute | solution.py:24
  335.1 5.7 %collective-permute-start.46 = (f32[7,8,1]{2,1,0:T(8,128)S(1)}, f32[7,8,1]{2,1,0:T(8,128)S(1)}, u32[]{:S(2)}, u32[]{:S(2)}) collective-permute-start(f32[7,8,1]{2,1,0:T(8,128)S(1)} %get-tuple-element.102), channel_id=1, source_target_pairs={{0,2},{1,3},{2,4},{3,5},{4,6},{5,7},{6,8},{7,9},{8,10},{9,11},{10,... | collective-permute-start | bytes 680 | tf_op jit(solution)/shard_map/ppermute | solution.py:34
  339.3 7.3 %collective-permute-start.47 = (f32[7,8,1]{2,1,0:T(8,128)S(1)}, f32[7,8,1]{2,1,0:T(8,128)S(1)}, u32[]{:S(2)}, u32[]{:S(2)}) collective-permute-start(f32[7,8,1]{2,1,0:T(8,128)S(1)} %get-tuple-element.101), channel_id=1, source_target_pairs={{2,0},{3,1},{4,2},{5,3},{6,4},{7,5},{8,6},{9,7},{10,8},{11,9},{12,... | collective-permute-start | bytes 680 | tf_op jit(solution)/shard_map/ppermute | solution.py:34
  348.0 16.4 %collective-permute-start.52 = (f32[7,1,2048]{2,1,0:T(1,128)S(1)}, f32[7,1,2048]{2,1,0:T(1,128)S(1)}, u32[]{:S(2)}, u32[]{:S(2)}) collective-permute-start(f32[7,1,2048]{2,1,0:T(1,128)S(1)} %get-tuple-element.90), channel_id=1, source_target_pairs={{0,16},{16,32},{32,48},{48,64},{64,80},{80,96},{96,112},{1,17},{17... | collective-permute-start | bytes 172040 | tf_op jit(solution)/shard_map/ppermute | solution.py:22
  352.2 12.2 %collective-permute-start.53 = (f32[7,1,2048]{2,1,0:T(1,128)S(1)}, f32[7,1,2048]{2,1,0:T(1,128)S(1)}, u32[]{:S(2)}, u32[]{:S(2)}) collective-permute-start(f32[7,1,2048]{2,1,0:T(1,128)S(1)} %get-tuple-element.91), channel_id=1, source_target_pairs={{16,0},{32,16},{48,32},{64,48},{80,64},{96,80},{112,96},{17,1},{33... | collective-permute-start | bytes 172040 | tf_op jit(solution)/shard_map/ppermute | solution.py:24
  353.5 5.1 %collective-permute-start.50 = (f32[7,8,1]{2,1,0:T(8,128)S(1)}, f32[7,8,1]{2,1,0:T(8,128)S(1)}, u32[]{:S(2)}, u32[]{:S(2)}) collective-permute-start(f32[7,8,1]{2,1,0:T(8,128)S(1)} %get-tuple-element.89), channel_id=1, source_target_pairs={{0,2},{1,3},{2,4},{3,5},{4,6},{5,7},{6,8},{7,9},{8,10},{9,11},{10,... | collective-permute-start | bytes 680 | tf_op jit(solution)/shard_map/ppermute | solution.py:34
  357.1 7.3 %collective-permute-start.51 = (f32[7,8,1]{2,1,0:T(8,128)S(1)}, f32[7,8,1]{2,1,0:T(8,128)S(1)}, u32[]{:S(2)}, u32[]{:S(2)}) collective-permute-start(f32[7,8,1]{2,1,0:T(8,128)S(1)} %get-tuple-element.88), channel_id=1, source_target_pairs={{2,0},{3,1},{4,2},{5,3},{6,4},{7,5},{8,6},{9,7},{10,8},{11,9},{12,... | collective-permute-start | bytes 680 | tf_op jit(solution)/shard_map/ppermute | solution.py:34
  370.3 14.8 %collective-permute-start.56 = (f32[7,1,2048]{2,1,0:T(1,128)S(1)}, f32[7,1,2048]{2,1,0:T(1,128)S(1)}, u32[]{:S(2)}, u32[]{:S(2)}) collective-permute-start(f32[7,1,2048]{2,1,0:T(1,128)S(1)} %get-tuple-element.77), channel_id=1, source_target_pairs={{0,16},{16,32},{32,48},{48,64},{64,80},{80,96},{96,112},{1,17},{17... | collective-permute-start | bytes 172040 | tf_op jit(solution)/shard_map/ppermute | solution.py:22
  374.6 10.6 %collective-permute-start.57 = (f32[7,1,2048]{2,1,0:T(1,128)S(1)}, f32[7,1,2048]{2,1,0:T(1,128)S(1)}, u32[]{:S(2)}, u32[]{:S(2)}) collective-permute-start(f32[7,1,2048]{2,1,0:T(1,128)S(1)} %get-tuple-element.78), channel_id=1, source_target_pairs={{16,0},{32,16},{48,32},{64,48},{80,64},{96,80},{112,96},{17,1},{33... | collective-permute-start | bytes 172040 | tf_op jit(solution)/shard_map/ppermute | solution.py:24
  375.9 5.0 %collective-permute-start.54 = (f32[7,8,1]{2,1,0:T(8,128)S(1)}, f32[7,8,1]{2,1,0:T(8,128)S(1)}, u32[]{:S(2)}, u32[]{:S(2)}) collective-permute-start(f32[7,8,1]{2,1,0:T(8,128)S(1)} %get-tuple-element.73), channel_id=1, source_target_pairs={{0,1},{1,2},{2,3},{3,4},{4,5},{5,6},{6,7},{7,8},{8,9},{9,10},{10,1... | collective-permute-start | bytes 680 | tf_op jit(solution)/shard_map/ppermute | solution.py:34
  379.4 5.8 %collective-permute-start.55 = (f32[7,8,1]{2,1,0:T(8,128)S(1)}, f32[7,8,1]{2,1,0:T(8,128)S(1)}, u32[]{:S(2)}, u32[]{:S(2)}) collective-permute-start(f32[7,8,1]{2,1,0:T(8,128)S(1)} %get-tuple-element.74), channel_id=1, source_target_pairs={{1,0},{2,1},{3,2},{4,3},{5,4},{6,5},{7,6},{8,7},{9,8},{10,9},{11,1... | collective-permute-start | bytes 680 | tf_op jit(solution)/shard_map/ppermute | solution.py:34
  388.4 14.4 %collective-permute-start.60 = (f32[7,1,2048]{2,1,0:T(1,128)S(1)}, f32[7,1,2048]{2,1,0:T(1,128)S(1)}, u32[]{:S(2)}, u32[]{:S(2)}) collective-permute-start(f32[7,1,2048]{2,1,0:T(1,128)S(1)} %get-tuple-element.64), channel_id=1, source_target_pairs={{0,16},{16,32},{32,48},{48,64},{64,80},{80,96},{96,112},{1,17},{17... | collective-permute-start | bytes 172040 | tf_op jit(solution)/shard_map/ppermute | solution.py:22
  392.8 10.0 %collective-permute-start.61 = (f32[7,1,2048]{2,1,0:T(1,128)S(1)}, f32[7,1,2048]{2,1,0:T(1,128)S(1)}, u32[]{:S(2)}, u32[]{:S(2)}) collective-permute-start(f32[7,1,2048]{2,1,0:T(1,128)S(1)} %get-tuple-element.65), channel_id=1, source_target_pairs={{16,0},{32,16},{48,32},{64,48},{80,64},{96,80},{112,96},{17,1},{33... | collective-permute-start | bytes 172040 | tf_op jit(solution)/shard_map/ppermute | solution.py:24
  397.0 5.8 %collective-permute-start.59 = (f32[7,8,1]{2,1,0:T(8,128)S(1)}, f32[7,8,1]{2,1,0:T(8,128)S(1)}, u32[]{:S(2)}, u32[]{:S(2)}) collective-permute-start(f32[7,8,1]{2,1,0:T(8,128)S(1)} %get-tuple-element.61), channel_id=1, source_target_pairs={{1,0},{2,1},{3,2},{4,3},{5,4},{6,5},{7,6},{8,7},{9,8},{10,9},{11,1... | collective-permute-start | bytes 680 | tf_op jit(solution)/shard_map/ppermute | solution.py:34
  404.3 15.4 %collective-permute-start.64 = (f32[7,1,2048]{2,1,0:T(1,128)S(1)}, f32[7,1,2048]{2,1,0:T(1,128)S(1)}, u32[]{:S(2)}, u32[]{:S(2)}) collective-permute-start(f32[7,1,2048]{2,1,0:T(1,128)S(1)} %get-tuple-element.44), channel_id=1, source_target_pairs={{0,16},{16,32},{32,48},{48,64},{64,80},{80,96},{96,112},{1,17},{17... | collective-permute-start | bytes 172040 | tf_op jit(solution)/shard_map/ppermute | solution.py:22
  408.6 11.1 %collective-permute-start.65 = (f32[7,1,2048]{2,1,0:T(1,128)S(1)}, f32[7,1,2048]{2,1,0:T(1,128)S(1)}, u32[]{:S(2)}, u32[]{:S(2)}) collective-permute-start(f32[7,1,2048]{2,1,0:T(1,128)S(1)} %get-tuple-element.45), channel_id=1, source_target_pairs={{16,0},{32,16},{48,32},{64,48},{80,64},{96,80},{112,96},{17,1},{33... | collective-permute-start | bytes 172040 | tf_op jit(solution)/shard_map/ppermute | solution.py:24
  409.9 5.6 %collective-permute-start.62 = (f32[7,8,1]{2,1,0:T(8,128)S(1)}, f32[7,8,1]{2,1,0:T(8,128)S(1)}, u32[]{:S(2)}, u32[]{:S(2)}) collective-permute-start(f32[7,8,1]{2,1,0:T(8,128)S(1)} %get-tuple-element.40), channel_id=1, source_target_pairs={{0,1},{1,2},{2,3},{3,4},{4,5},{5,6},{6,7},{7,8},{8,9},{9,10},{10,1... | collective-permute-start | bytes 680 | tf_op jit(solution)/shard_map/ppermute | solution.py:34
  413.9 5.8 %collective-permute-start.63 = (f32[7,8,1]{2,1,0:T(8,128)S(1)}, f32[7,8,1]{2,1,0:T(8,128)S(1)}, u32[]{:S(2)}, u32[]{:S(2)}) collective-permute-start(f32[7,8,1]{2,1,0:T(8,128)S(1)} %get-tuple-element.41), channel_id=1, source_target_pairs={{1,0},{2,1},{3,2},{4,3},{5,4},{6,5},{7,6},{8,7},{9,8},{10,9},{11,1... | collective-permute-start | bytes 680 | tf_op jit(solution)/shard_map/ppermute | solution.py:34
  (41 other events, 596.7 us)
where the time goes:
time: 504 us; the launch traced here: 495 us
  starting transfers between devices  169 us (34%)
  waiting for transfers between devices  103 us (20%)
  local copies, waits for them, and re-layouts  72.3 us (14%)
  blocking collectives  69.8 us (14%)
  other arithmetic  51.1 us (10%)
  matrix products  27.7 us (5%)
    ppermute x30, waiting for transfers between devices, shifted(): return lax.ppermute(block, axis, route)  82 us
    ppermute x30, starting transfers between devices, shifted(): return lax.ppermute(block, axis, route)  77.3 us
    psum x1, blocking collectives, record(): return lax.psum(local_sum, ('hull', 'blk'))  69.8 us
    ppermute x15, starting transfers between devices, with_halo(): lax.ppermute(tail, axis, [(i, (i + 1) % count) for i in range(ends)])  53.2 us
    dot_general x18, matrix products, pair_sum(): jnp.einsum('...kw,wh->...kh', blocks, pairing, precision=lax.Precision.HI...  25.5 us
    unnamed x104, local copies, waits for them, and re-layouts  21.1 us
    ppermute x15, starting transfers between devices, with_halo(): lax.ppermute(head, axis, [((i + 1) % count, i) for i in range(ends)])  19.3 us
    ppermute x6, starting transfers between devices, partner_2(): return lax.ppermute(block, axis, route)  18.7 us
  transfers between devices with their start and end apart: 66, of which 23 were waited for; matrix products, arithmetic and copies ran while one was open for 22% of the time, Pallas kernels for 0%

commit v1 on v0

v1 whole, which is shorter than its diff:
```python
import jax
import jax.numpy as jnp
from jax import lax
from jax.experimental import pallas as pl
from jax.experimental.pallas import tpu as pltpu
from jax.sharding import PartitionSpec as P

FIELDS = 7
ROWS = 8
WIDE = 2
T = 128
HALF = 64
DAMP = 0.7
PLANES = 12
SWEEP_W = 11
F32 = jnp.float32
LIMIT = 12 * 2**20


def iota(shape, dim):
    return lax.broadcasted_iota(jnp.int32, shape, dim)


def tile(j):
    return pl.ds(pl.multiple_of(j * T, T), T)


def each_tile(count, body):
    def step(j, carry):
        body(j)
        return carry

    lax.fori_loop(0, count, step, 0)


def swap(x, span):
    low = (iota(x.shape, 1) // span) % 2 == 0
    return jnp.where(low, pltpu.roll(x, T - span, 1), pltpu.roll(x, span, 1))


def lower_half(x, span):
    low = (iota(x.shape, 1) // span) % 2 == 0
    return jnp.where(low, x, pltpu.roll(x, span, 1))


def upper_half(x, span):
    low = (iota(x.shape, 1) // span) % 2 == 0
    return jnp.where(low, pltpu.roll(x, T - span, 1), x)


def diagonal(planes):
    sub = iota(planes[0].shape, 0)
    out = planes[FIELDS - 1]
    for f in range(FIELDS - 1):
        out = jnp.where(sub == f, planes[f], out)
    return out


def coarser(planes, span):
    low_j = [p + swap(p, span) for p in planes[:FIELDS]]
    f0, f1, f2, f3 = planes[FIELDS : FIELDS + 4]
    f0_low, f0_up = lower_half(f0, span), upper_half(f0, span)
    f1_low, f1_up = lower_half(f1, span), upper_half(f1, span)
    inner = f1_up + f0_low
    sub = iota(f0.shape, 0)
    low_j = [jnp.where(sub == f, p - inner, p) for f, p in enumerate(low_j)]
    return low_j + [f0_up, f1_low, f2 + swap(f2, span), f3 + swap(f3, span)]


def split_kernel(jac, face, src, act, c0, t0, top, bottom, left, right, buf):
    columns = src.shape[-1]
    last = columns // T - 1

    def body(j):
        sl = tile(j)
        for f in range(FIELDS):
            buf[f] = jac[f, :, sl]
        for k in range(4):
            buf[FIELDS + k] = face[k, :, sl]
        buf[PLANES - 1] = src[:, sl]
        for r in range(ROWS):
            pick = pl.ds(r, FIELDS, stride=ROWS)
            planes = [buf[f, pick, :] for f in range(FIELDS)]
            faces = [buf[FIELDS + k, pick, :] for k in range(4)]
            total = faces[0] + faces[1] + faces[2] + faces[3]
            sub = iota(total.shape, 0)
            planes = [jnp.where(sub == f, p + total, p) for f, p in enumerate(planes)]
            mask = act[r : r + 1, sl].astype(F32)
            for k, p in enumerate(planes + faces):
                c0[r + WIDE, k, 0:FIELDS, sl] = p
            c0[r + WIDE, SWEEP_W, 0:FIELDS, sl] = DAMP * mask / diagonal(planes)
            t0[r + WIDE, 0:FIELDS, sl] = buf[PLANES - 1, pick, :]
            t0[r + WIDE, FIELDS : FIELDS + 1, sl] = mask

    each_tile(columns // T, body)

    def rows(j):
        sl = tile(j)
        for out, first in ((top, 0), (bottom, ROWS - WIDE)):
            for w in range(WIDE):
                for k in range(PLANES - 1):
                    out[w, k, :, sl] = c0[first + w + WIDE, k, :, sl]
                out[w, PLANES - 1, :, sl] = t0[first + w + WIDE, :, sl]

    each_tile(columns // T, rows)

    def cols(r):
        for out, j in ((left, 0), (right, last)):
            sl = slice(j * T, j * T + T)
            for k in range(PLANES - 1):
                out[r, k] = c0[r + WIDE, k, :, sl]
            out[r, PLANES - 1] = t0[r + WIDE, :, sl]

    each_tile(ROWS, cols)


def build_levels(c0, c1, c2, r, sl, domain):
    planes = [c0[r, k, :, sl] for k in range(PLANES - 1)]
    for out, span in ((c1, 1), (c2, 2)):
        planes = coarser(planes, span)
        for k, p in enumerate(planes):
            out[r, k, :, sl] = p
        weight = DAMP / diagonal(planes[:FIELDS])
        out[r, SWEEP_W, :, sl] = weight if domain is None else weight * domain


def own_levels_kernel(c0, c1, c2):
    def body(j):
        for r in range(ROWS):
            build_levels(c0, c1, c2, r + WIDE, tile(j), None)

    each_tile(c0.shape[-1] // T - 1, body)


def side_domain(flags):
    lane = iota((8, T), 1)
    return jnp.where(lane < HALF, flags[3], flags[2])


def row_flag(flags, r):
    if r < WIDE:
        return flags[0]
    if r >= WIDE + ROWS:
        return flags[1]
    return None


HALO_ROWS = list(range(WIDE)) + list(range(WIDE + ROWS, 2 * WIDE + ROWS))


def halo_levels_kernel(flags, c0, c1_in, c2_in, c1, c2):
    tiles = c0.shape[-1] // T

    def body(j):
        for r in HALO_ROWS:
            build_levels(c0, c1, c2, r, tile(j), row_flag(flags, r))

    each_tile(tiles - 1, body)
    sides = side_domain(flags)
    sl = slice((tiles - 1) * T, tiles * T)
    for r in range(2 * WIDE + ROWS):
        flag = row_flag(flags, r)
        build_levels(c0, c1, c2, r, sl, sides if flag is None else sides * flag)


def apply_at(c, r, v, vi, j, tiles, span, above=None, below=None):
    sl = tile(j)
    before = tile(lax.rem(j + tiles - 1, tiles))
    after = tile(lax.rem(j + 1, tiles))
    lane = iota((8, T), 1)
    here = v[vi, :, sl]
    out = c[r, 0, :, sl] * v[vi, 0:1, sl]
    for f in range(1, FIELDS):
        out = out + c[r, f, :, sl] * v[vi, f : f + 1, sl]
    k = FIELDS
    from_left = jnp.where(lane >= T - span, c[r, k, :, before] * v[vi, :, before], c[r, k, :, sl] * here)
    out = out - pltpu.roll(from_left, span, 1)
    from_right = jnp.where(lane < span, c[r, k + 1, :, after] * v[vi, :, after], c[r, k + 1, :, sl] * here)
    out = out - pltpu.roll(from_right, T - span, 1)
    out = out - (c[r - 1, k + 2, :, sl] * v[vi - 1, :, sl] if above is None else above)
    out = out - (c[r + 1, k + 3, :, sl] * v[vi + 1, :, sl] if below is None else below)
    return out


def first_kernel(flags, c0_in, t0_in, rows_above, rows_below, side, side_above, side_below, c0, t0, v2, t1, t1_top, t1_bottom, sums, va, vb):
    tiles = c0.shape[-1] // T
    last = slice((tiles - 1) * T, tiles * T)

    def put(r, planes, sl, domain):
        for k in range(PLANES - 1):
            c0[r, k, :, sl] = planes[k]
        source = planes[PLANES - 1]
        t0[r, :, sl] = source
        weight = DAMP * source[FIELDS : FIELDS + 1] / diagonal(planes[:FIELDS])
        weight = weight if domain is None else jnp.where(domain > 0.0, weight, 0.0)
        c0[r, SWEEP_W, :, sl] = weight
        va[r, :, sl] = weight * source

    def fill(j):
        sl = tile(j)
        for w in range(WIDE):
            put(w, [rows_above[w, k, :, sl] for k in range(PLANES)], sl, flags[0])
            put(WIDE + ROWS + w, [rows_below[w, k, :, sl] for k in range(PLANES)], sl, flags[1])
        for r in range(WIDE, WIDE + ROWS):
            va[r, :, sl] = c0[r, SWEEP_W, :, sl] * t0[r, :, sl]

    each_tile(tiles - 1, fill)
    sides = side_domain(flags)
    for r in range(ROWS):
        put(r + WIDE, [side[r, k] for k in range(PLANES)], last, sides)
    for w in range(WIDE):
        put(w, [side_above[w, k] for k in range(PLANES)], last, sides * flags[0])
        put(WIDE + ROWS + w, [side_below[w, k] for k in range(PLANES)], last, sides * flags[1])

    def sweep(j):
        sl = tile(j)
        for r in range(1, ROWS + 2 * WIDE - 1):
            diff = t0[r, :, sl] - apply_at(c0, r, va, r, j, tiles, 1)
            vb[r, :, sl] = va[r, :, sl] + diff * c0[r, SWEEP_W, :, sl]

    each_tile(tiles, sweep)
    sums[...] = jnp.zeros_like(sums)

    def rest(j):
        sl = tile(j)
        total = jnp.zeros((8, T), F32)
        for r in range(WIDE, WIDE + ROWS):
            diff = t0[r, :, sl] - apply_at(c0, r, vb, r, j, tiles, 1)
            res = jnp.where(c0[r, SWEEP_W, :, sl] != 0.0, diff, 0.0)
            total = total + res * res
            t1[r - WIDE, :, sl] = res + swap(res, 1)
            v2[r - WIDE, :, sl] = vb[r, :, sl]
        sums[...] += jnp.where(j < tiles - 1, total, 0.0)

    each_tile(tiles, rest)
    t1_top[...] = t1[0:WIDE]
    t1_bottom[...] = t1[ROWS - WIDE : ROWS]


def second_kernel(c1, c2, t1_own, t1_above, t1_below, t1, e1, t2, send_top, send_bottom, sums, va, vb):
    tiles = c1.shape[-1] // T

    def fill(j):
        sl = tile(j)
        for r in range(ROWS + 2 * WIDE):
            if r < WIDE:
                val = t1_above[r, :, sl]
            elif r < WIDE + ROWS:
                val = t1_own[r - WIDE, :, sl]
            else:
                val = t1_below[r - WIDE - ROWS, :, sl]
            t1[r, :, sl] = val
            va[r, :, sl] = c1[r, SWEEP_W, :, sl] * val

    each_tile(tiles, fill)

    def sweep(j):
        sl = tile(j)
        for r in range(1, ROWS + 2 * WIDE - 1):
            diff = t1[r, :, sl] - apply_at(c1, r, va, r, j, tiles, 2)
            vb[r, :, sl] = va[r, :, sl] + diff * c1[r, SWEEP_W, :, sl]

    each_tile(tiles, sweep)
    sums[...] = jnp.zeros_like(sums)

    def rest(j):
        sl = tile(j)
        total = jnp.zeros((8, T), F32)
        for r in range(WIDE, WIDE + ROWS):
            res = t1[r, :, sl] - apply_at(c1, r, vb, r, j, tiles, 2)
            total = total + res * res
            val = res + swap(res, 2)
            t2[r - WIDE, :, sl] = val
            e1[r - WIDE, :, sl] = vb[r, :, sl]
            row = r - WIDE
            if row < WIDE:
                send_top[row, :, sl] = val
            if row == WIDE:
                send_top[WIDE, :, sl] = c2[r, FIELDS + 3, :, sl] * c2[r, SWEEP_W, :, sl] * val
            if row == ROWS - WIDE - 1:
                send_bottom[WIDE, :, sl] = c2[r, FIELDS + 2, :, sl] * c2[r, SWEEP_W, :, sl] * val
            if row >= ROWS - WIDE:
                send_bottom[row - ROWS + WIDE, :, sl] = val
        sums[...] += jnp.where(j < tiles - 1, total, 0.0)

    each_tile(tiles, rest)


def third_kernel(c2, t2_own, above, below, e1_in, e1, send_top, send_bottom, t2, va, vb):
    tiles = c2.shape[-1] // T
    high = ROWS + 2 * WIDE

    def fill(j):
        sl = tile(j)
        for r in range(high):
            if r < WIDE:
                val = above[r, :, sl]
            elif r < WIDE + ROWS:
                val = t2_own[r - WIDE, :, sl]
            else:
                val = below[r - WIDE - ROWS, :, sl]
            t2[r, :, sl] = val
            va[r, :, sl] = c2[r, SWEEP_W, :, sl] * val

    each_tile(tiles, fill)

    def value(j, r, v):
        sl = tile(j)
        up = above[WIDE, :, sl] if r == 0 else None
        down = below[WIDE, :, sl] if r == high - 1 else None
        diff = t2[r, :, sl] - apply_at(c2, r, v, r, j, tiles, 4, up, down)
        return v[r, :, sl] + diff * c2[r, SWEEP_W, :, sl]

    def sweep2(j):
        for r in range(high):
            vb[r, :, tile(j)] = value(j, r, va)

    def sweep3(j):
        for r in range(1, high - 1):
            va[r, :, tile(j)] = value(j, r, vb)

    def sweep4(j):
        sl = tile(j)
        for r in range(WIDE, WIDE + ROWS):
            row = r - WIDE
            val = e1_in[row, :, sl] + value(j, r, va)
            e1[row, :, sl] = val
            if row < WIDE:
                send_top[row, :, sl] = val
            if row >= ROWS - WIDE:
                send_bottom[row - ROWS + WIDE, :, sl] = val

    each_tile(tiles, sweep2)
    each_tile(tiles, sweep3)
    each_tile(tiles, sweep4)


def fourth_kernel(c1, c0, t1, e1, above, below, v2, v, send_top, send_bottom, va, vb):
    tiles = c1.shape[-1] // T

    def fill(j):
        sl = tile(j)
        for r in range(ROWS + 2 * WIDE):
            if WIDE <= r < WIDE + ROWS:
                va[r, :, sl] = e1[r - WIDE, :, sl]
            else:
                val = above[r, :, sl] if r < WIDE else below[r - WIDE - ROWS, :, sl]
                va[r, :, sl] = jnp.where(c1[r, SWEEP_W, :, sl] != 0.0, val, 0.0)

    each_tile(tiles, fill)

    def value(j, r, x):
        sl = tile(j)
        diff = t1[r, :, sl] - apply_at(c1, r, x, r, j, tiles, 2)
        return x[r, :, sl] + diff * c1[r, SWEEP_W, :, sl]

    def sweep(j):
        for r in range(1, ROWS + 2 * WIDE - 1):
            vb[r, :, tile(j)] = value(j, r, va)

    def last(j):
        sl = tile(j)
        for r in range(WIDE, WIDE + ROWS):
            row = r - WIDE
            val = v2[row, :, sl] + jnp.where(c0[r, SWEEP_W, :, sl] != 0.0, value(j, r, vb), 0.0)
            v[row, :, sl] = val
            if row < WIDE:
                send_top[row, :, sl] = val
            if row == WIDE:
                send_top[WIDE, :, sl] = c0[r, FIELDS + 3, :, sl] * val
            if row == ROWS - WIDE - 1:
                send_bottom[WIDE, :, sl] = c0[r, FIELDS + 2, :, sl] * val
            if row >= ROWS - WIDE:
                send_bottom[row - ROWS + WIDE, :, sl] = val

    each_tile(tiles, sweep)
    each_tile(tiles, last)


def fifth_kernel(c0, t0, v, above, below, adjoint, residual, sums, va, vb, buf):
    tiles = c0.shape[-1] // T
    high = ROWS + 2 * WIDE

    def fill(j):
        sl = tile(j)
        for r in range(high):
            if WIDE <= r < WIDE + ROWS:
                va[r, :, sl] = v[r - WIDE, :, sl]
            else:
                val = above[r, :, sl] if r < WIDE else below[r - WIDE - ROWS, :, sl]
                va[r, :, sl] = jnp.where(c0[r, SWEEP_W, :, sl] != 0.0, val, 0.0)

    each_tile(tiles, fill)

    def value(j, r, x):
        sl = tile(j)
        up = above[WIDE, :, sl] if r == 0 else None
        down = below[WIDE, :, sl] if r == high - 1 else None
        diff = t0[r, :, sl] - apply_at(c0, r, x, r, j, tiles, 1, up, down)
        return x[r, :, sl] + diff * c0[r, SWEEP_W, :, sl]

    def sweep1(j):
        for r in range(high):
            vb[r, :, tile(j)] = value(j, r, va)

    def sweep2(j):
        for r in range(1, high - 1):
            va[r, :, tile(j)] = value(j, r, vb)

    each_tile(tiles, sweep1)
    each_tile(tiles, sweep2)
    sums[...] = jnp.zeros_like(sums)

    def rest(j):
        sl = tile(j)
        total = jnp.zeros((8, T), F32)
        for r in range(WIDE, WIDE + ROWS):
            diff = t0[r, :, sl] - apply_at(c0, r, va, r, j, tiles, 1)
            res = jnp.where(c0[r, SWEEP_W, :, sl] != 0.0, diff, 0.0)
            total = total + res * res
            pick = pl.ds(r - WIDE, FIELDS, stride=ROWS)
            buf[0, pick, :] = res[0:FIELDS]
            buf[1, pick, :] = va[r, 0:FIELDS, sl]
        residual[:, sl] = buf[0]
        adjoint[:, sl] = buf[1]
        sums[...] += total

    each_tile(tiles - 1, rest)


def call(kernel, outs, args, scratch=(), alias=None, flags=False, flops=0, size=0):
    vmem = pl.BlockSpec(memory_space=pltpu.VMEM)
    in_specs = [vmem] * len(args)
    if flags:
        in_specs[0] = pl.BlockSpec(memory_space=pltpu.SMEM)
    return pl.pallas_call(
        kernel,
        out_shape=[jax.ShapeDtypeStruct(s, F32) for s in outs],
        in_specs=in_specs,
        out_specs=[vmem] * len(outs),
        scratch_shapes=[pltpu.VMEM(s, F32) for s in scratch],
        input_output_aliases=alias or {},
        compiler_params=pltpu.CompilerParams(vmem_limit_bytes=LIMIT),
        cost_estimate=pl.CostEstimate(flops=flops, bytes_accessed=size, transcendentals=0),
        name=kernel.__name__,
    )(*args)


def ring(x, axis, step):
    count = lax.axis_size(axis)
    return lax.ppermute(x, axis, [(i, (i + step) % count) for i in range(count)])


def xor(x, axis, bits):
    count = lax.axis_size(axis)
    return lax.ppermute(x, axis, [(i, i ^ bits) for i in range(count)])


def total_over_devices(x):
    x = x + xor(x, "hull", 1)
    for axis, unit in (("hull", 2), ("blk", 1), ("blk", 4)):
        x = x + xor(x, axis, unit) + xor(x, axis, 2 * unit) + xor(x, axis, 3 * unit)
    return x


def on_device(source, jacobian, face_coef, active):
    columns = source.shape[2]
    wide = columns + T
    hull, blk = lax.axis_index("hull"), lax.axis_index("blk")
    flags = jnp.stack([hull > 0, hull < lax.axis_size("hull") - 1, blk > 0, blk < lax.axis_size("blk") - 1]).astype(F32)
    ext = ROWS + 2 * WIDE
    c_shape = (ext, PLANES, 8, wide)
    row_shape = (ext, 8, wide)
    own = (ROWS, 8, wide)
    two, three = (WIDE, 8, wide), (WIDE + 1, 8, wide)
    tile_shape = (8, T)

    c0, t0, top, bottom, left, right = call(
        split_kernel,
        [c_shape, row_shape, (WIDE, PLANES, 8, columns), (WIDE, PLANES, 8, columns), (ROWS, PLANES, 8, T), (ROWS, PLANES, 8, T)],
        [
            jacobian.reshape(FIELDS, FIELDS * ROWS, columns),
            face_coef.reshape(4, FIELDS * ROWS, columns),
            source.reshape(FIELDS * ROWS, columns),
            active,
        ],
        [(PLANES, FIELDS * ROWS, T)],
    )
    from_right = ring(left, "blk", -1)
    from_left = ring(right, "blk", 1)
    rows_below = ring(top, "hull", -1)
    rows_above = ring(bottom, "hull", 1)
    c1, c2 = call(own_levels_kernel, [c_shape, c_shape], [c0], size=10**7)
    side = jnp.where(lax.broadcasted_iota(jnp.int32, from_right.shape, 3) < HALF, from_right, from_left)
    side_below = ring(side[0:WIDE], "hull", -1)
    side_above = ring(side[ROWS - WIDE : ROWS], "hull", 1)
    c0, t0, v2, t1, t1_top, t1_bottom, sum0 = call(
        first_kernel,
        [c_shape, row_shape, own, own, two, two, tile_shape],
        [flags, c0, t0, rows_above, rows_below, side, side_above, side_below],
        [row_shape, row_shape],
        {1: 0, 2: 1},
        True,
    )
    t1_below = ring(t1_top, "hull", -1)
    t1_above = ring(t1_bottom, "hull", 1)
    c1, c2 = call(halo_levels_kernel, [c_shape, c_shape], [flags, c0, c1, c2], alias={2: 0, 3: 1}, flags=True, size=10**7)
    t1, e1, t2, send_top, send_bottom, sum1 = call(
        second_kernel, [row_shape, own, own, three, three, tile_shape], [c1, c2, t1, t1_above, t1_below], [row_shape, row_shape]
    )
    below = ring(send_top, "hull", -1)
    above = ring(send_bottom, "hull", 1)
    e1, send_top, send_bottom = call(
        third_kernel, [own, two, two], [c2, t2, above, below, e1], [row_shape] * 3
    )
    below = ring(send_top, "hull", -1)
    above = ring(send_bottom, "hull", 1)
    v, send_top, send_bottom = call(
        fourth_kernel, [own, three, three], [c1, c0, t1, e1, above, below, v2], [row_shape, row_shape]
    )
    below = ring(send_top, "hull", -1)
    above = ring(send_bottom, "hull", 1)
    adjoint, residual, sum2 = call(
        fifth_kernel, [(FIELDS * ROWS, columns)] * 2 + [tile_shape], [c0, t0, v, above, below],
        [row_shape, row_shape, (2, FIELDS * ROWS, T)],
    )
    squares = total_over_devices(jnp.stack([sum0, sum1, sum2]))
    squares = jnp.sum(squares[:, :FIELDS], axis=(1, 2))
    cells = source.size * lax.axis_size("hull") * lax.axis_size("blk")
    level_rms = jnp.sqrt(squares / float(cells))
    return adjoint.reshape(source.shape), residual.reshape(source.shape), level_rms


def solution(mesh):
    return jax.shard_map(
        on_device,
        mesh=mesh,
        in_specs=(
            P(None, "hull", "blk"),
            P(None, None, "hull", "blk"),
            P(None, None, "hull", "blk"),
            P("hull", "blk"),
        ),
        out_specs=(P(None, "hull", "blk"), P(None, "hull", "blk"), P()),
        check_vma=False,
    )
```

time: 504 us -> 138 us (0.27); the launches traced: 495 us -> 137 us
  starting transfers between devices: 169 us -> 34.8 us
  waiting for transfers between devices: 103 us -> 25.7 us
  blocking collectives: 69.8 us -> 0 us
  Pallas kernels: 0 us -> 53.5 us
  local copies, waits for them, and re-layouts: 72.3 us -> 20.7 us
  other arithmetic: 51.1 us -> 1.9 us
  matrix products: 27.7 us -> 0 us
    ppermute x66 -> x24, starting transfers between devices: 169 us -> 34.8 us  [the longest x14 21.7 us: ring(): lax.ppermute(x, axis, [(i, (i + step) % count) for i in range(count)])]
    ppermute x66 -> x24, waiting for transfers between devices: 103 us -> 25.7 us  [the longest x14 14.4 us: ring(): lax.ppermute(x, axis, [(i, (i + step) % count) for i in range(count)])]
    psum x1 -> x0, blocking collectives: 69.8 us -> none  [record(): return lax.psum(local_sum, ('hull', 'blk'))]
    pallas_call x0 -> x8, Pallas kernels: none -> 53.5 us  [call(): pl.pallas_call(kernel, out_shape=[jax.ShapeDtypeStruct(s, F32) for s in o...]
    dot_general x20 -> x0, matrix products: 27.7 us -> none  [the longest x18 25.5 us: pair_sum(): jnp.einsum('...kw,wh->...kh', blocks, pairing, precision=lax.Precision.HI...]
    slice x41 -> x1, local copies, waits for them, and re-layouts: 13.6 us -> 0.02 us  [on_device(): side_below = ring(side[0:WIDE], 'hull', -1)]
    mul x7 -> x0, other arithmetic: 12.7 us -> none  [the longest x2 7.64 us: on_device(): adjoint = smooth(adjoint, source, 0, fine_ops, diagonal) * cell_mask]
    another operation x15 -> x0, local copies, waits for them, and re-layouts: 11.3 us -> none  [the longest x10 9.15 us: coarsen_couple(): jnp.stack([face_sum - west_even - east_odd, east_even, west_odd, north, s...]
  transfers between devices with their start and end apart: 66 -> 24, of which waited for: 23 -> 13; matrix products, arithmetic and copies ran while one was open for 22% -> 1% of each run, Pallas kernels for 0% -> 14%
where the time goes in v1:
time: 138 us; the launch traced here: 137 us
  Pallas kernels  53.5 us (39%)
  starting transfers between devices  34.8 us (25%)
  waiting for transfers between devices  25.7 us (19%)
  local copies, waits for them, and re-layouts  20.7 us (15%)
  other arithmetic  1.9 us (1%)
    pallas_call x8, Pallas kernels, call(): pl.pallas_call(kernel, out_shape=[jax.ShapeDtypeStruct(s, F32) for s in o...  53.5 us
    ppermute x14, starting transfers between devices, ring(): lax.ppermute(x, axis, [(i, (i + step) % count) for i in range(count)])  21.7 us
    unnamed x18, local copies, waits for them, and re-layouts  20.6 us
    ppermute x14, waiting for transfers between devices, ring(): lax.ppermute(x, axis, [(i, (i + step) % count) for i in range(count)])  14.4 us
    ppermute x10, starting transfers between devices, xor(): return lax.ppermute(x, axis, [(i, i ^ bits) for i in range(count)])  13.1 us
    ppermute x10, waiting for transfers between devices, xor(): return lax.ppermute(x, axis, [(i, i ^ bits) for i in range(count)])  11.4 us
  transfers between devices with their start and end apart: 24, of which 13 were waited for; matrix products, arithmetic and copies ran while one was open for 1% of the time, Pallas kernels for 14%

profile of v1, /device:TPU:0, one launch (start us, length us, event | category | flops | bytes accessed | tf_op | source)
XLA Modules:
  0.0 137.4 jit_solution(13511116399077878223)
XLA Ops:
  0.6 1.9 %copy-done.5 = f32[7,7,8,2048]{3,2,1,0:T(8,128)S(1)} copy-done((f32[7,7,8,2048]{3,2,1,0:T(8,128)S(1)}, f32[7,7,8,2048]{3,2,1,0:T(8,128)}, u32[]{:S(2)}) %copy-start.5) | copy-done | bytes 3211288
  2.5 1.5 %copy-done.6 = f32[4,7,8,2048]{3,2,1,0:T(8,128)S(1)} copy-done((f32[4,7,8,2048]{3,2,1,0:T(8,128)S(1)}, f32[4,7,8,2048]{3,2,1,0:T(8,128)}, u32[]{:S(2)}) %copy-start.6) | copy-done | bytes 1835032
  4.0 1.0 copy-done.7
  5.1 0.8 copy-done.8
  5.9 4.6 %split_kernel.1 = (f32[12,12,8,2176]{3,2,1,0:T(8,128)S(1)}, f32[12,8,2176]{2,1,0:T(8,128)S(1)}, f32[2,12,8,2048]{3,2,1,0:T(8,128)}, f32[2,12,8,2048]{3,2,1,0:T(8...) custom-call(f32[7,56,2048]{2,1,0:T(8,128)S(1)} %bitcast.12, f32[4,56,2048]{2,1,0:T(8,128)S(1)} %bitcast.13, ...), custom_call_target="tpu_custom_call" | custom-call | tf_op jit(solution)/shard_map/split_kernel/pallas_call | solution.py:436
  10.5 3.8 %copy-done = f32[12,12,8,2176]{3,2,1,0:T(8,128)} copy-done((f32[12,12,8,2176]{3,2,1,0:T(8,128)}, f32[12,12,8,2176]{3,2,1,0:T(8,128)S(1)}, u32[]{:S(2)}) %copy-start) | copy-done | bytes 10027032
  14.4 0.0 collective-permute-start
  14.4 3.0 %collective-permute-start.1 = (f32[2,12,8,2048]{3,2,1,0:T(8,128)}, f32[2,12,8,2048]{3,2,1,0:T(8,128)}, u32[]{:S(2)}, u32[]{:S(2)}) collective-permute-start(f32[2,12,8,2048]{3,2,1,0:T(8,128)} %get-tuple-element.38), channel_id=1, source_target_pairs={{0,112},{16,0},{32,16},{48,32},{64,48},{80,64},{96,80},{112,96},{1... | collective-permute-start | bytes 4718600 | tf_op jit(solution)/shard_map/ppermute | solution.py:451
  17.3 6.3 %collective-permute-start.2 = (f32[8,12,8,128]{3,2,1,0:T(8,128)S(1)}, f32[8,12,8,128]{3,2,1,0:T(8,128)}, u32[]{:S(2)}, u32[]{:S(2)}) collective-permute-start(f32[8,12,8,128]{3,2,1,0:T(8,128)S(1)} %get-tuple-element.39), channel_id=1, source_target_pairs={{0,15},{1,0},{2,1},{3,2},{4,3},{5,4},{6,5},{7,6},{8,7},{9,8},{10,9... | collective-permute-start | bytes 1179656 | tf_op jit(solution)/shard_map/ppermute | solution.py:451
  23.6 0.0 collective-permute-start.3
  23.6 3.8 %copy-done.1 = f32[12,12,8,2176]{3,2,1,0:T(8,128)S(1)} copy-done((f32[12,12,8,2176]{3,2,1,0:T(8,128)S(1)}, f32[12,12,8,2176]{3,2,1,0:T(8,128)}, u32[]{:S(2)}) %copy-start.1) | copy-done | bytes 10027032
  27.5 12.6 %own_levels_kernel.1 = (f32[12,12,8,2176]{3,2,1,0:T(8,128)S(1)}, f32[12,12,8,2176]{3,2,1,0:T(8,128)S(1)}) custom-call(f32[12,12,8,2176]{3,2,1,0:T(8,128)S(1)} %copy-done.1), custom_call_target="tpu_custom_call" | custom-call | bytes 10000000 | tf_op jit(solution)/shard_map/own_levels_kernel/pallas_call | solution.py:436
  40.1 0.0 collective-permute-done.3
  40.1 1.2 broadcast_select_fusion.side
  41.3 0.0 collective-permute-start.5
  41.3 0.5 collective-permute-start.4
  41.8 0.1 add_convert_fusion.flags
  41.9 1.6 %collective-permute-done.5.side_below = f32[2,12,8,128]{3,2,1,0:T(8,128)S(1)} collective-permute-done((f32[2,12,8,128]{3,2,1,0:T(8,128)S(1)}, f32[2,12,8,128]{3,2,1,0:T(8,128)S(1)}, u32[]{:S(2)}, u32[]{:S(2)}) %collective-permute-start.5) | collective-permute-done | bytes 98336 | tf_op jit(solution)/shard_map/ppermute | solution.py:451
  43.5 3.1 %collective-permute-done.4.side_above = f32[2,12,8,128]{3,2,1,0:T(8,128)S(1)} collective-permute-done((f32[2,12,8,128]{3,2,1,0:T(8,128)S(1)}, f32[2,12,8,128]{3,2,1,0:T(8,128)S(1)}, u32[]{:S(2)}, u32[]{:S(2)}) %collective-permute-start.4) | collective-permute-done | bytes 98336 | tf_op jit(solution)/shard_map/ppermute | solution.py:451
  46.6 0.0 collective-permute-done.rows_above
  46.6 0.0 collective-permute-done.1.rows_below
  46.6 7.2 %first_kernel.1 = (f32[12,12,8,2176]{3,2,1,0:T(8,128)S(1)}, f32[12,8,2176]{2,1,0:T(8,128)S(1)}, f32[8,8,2176]{2,1,0:T(8,128)S(1)}, f32[8,8,2176]{2,1,0:T(8,128)S...) custom-call(f32[4]{0:T(128)S(1)} %add_convert_fusion.flags, ...), custom_call_target="tpu_custom_call", output_to_operand_aliasing={{0}: (1, {}), {1}: (2, {})} | custom-call | tf_op jit(solution)/shard_map/first_kernel/pallas_call | solution.py:436
  53.8 0.0 collective-permute-start.6
  53.8 2.9 %collective-permute-start.7 = (f32[2,8,2176]{2,1,0:T(8,128)S(1)}, f32[2,8,2176]{2,1,0:T(8,128)S(1)}, u32[]{:S(2)}, u32[]{:S(2)}) collective-permute-start(f32[2,8,2176]{2,1,0:T(8,128)S(1)} %get-tuple-element.49), channel_id=1, source_target_pairs={{0,112},{16,0},{32,16},{48,32},{64,48},{80,64},{96,80},{112,96},{1... | collective-permute-start | bytes 417800 | tf_op jit(solution)/shard_map/ppermute | solution.py:451
  56.8 7.2 %halo_levels_kernel.1 = (f32[12,12,8,2176]{3,2,1,0:T(8,128)S(1)}, f32[12,12,8,2176]{3,2,1,0:T(8,128)S(1)}) custom-call(f32[4]{0:T(128)S(1)} %add_convert_fusion.flags, f32[12,12,8,2176]{3,2,1,0:T(8,128)S(1)} %get-tuple-element.41.c0, f32[12,12,8,2176]{3,2,1,0:T(8,128)S(1)} %get-tuple-element.43.c1_in, ...), custom_call_target="tpu_custom_call", output_to_operand_aliasing={{0}: (2, {}), {1}: (3, {})} | custom-call | bytes 10000000 | tf_op jit(solution)/shard_map/halo_levels_kernel/pallas_call | solution.py:436
  64.0 3.8 %copy-done.3 = f32[12,12,8,2176]{3,2,1,0:T(8,128)} copy-done((f32[12,12,8,2176]{3,2,1,0:T(8,128)}, f32[12,12,8,2176]{3,2,1,0:T(8,128)S(1)}, u32[]{:S(2)}) %copy-start.3) | copy-done | bytes 10027032
  67.9 0.0 collective-permute-done.6.t1_above
  67.9 0.0 collective-permute-done.7.t1_below
  67.9 3.8 %copy-done.4 = f32[12,12,8,2176]{3,2,1,0:T(8,128)S(1)} copy-done((f32[12,12,8,2176]{3,2,1,0:T(8,128)S(1)}, f32[12,12,8,2176]{3,2,1,0:T(8,128)}, u32[]{:S(2)}) %copy-start.4) | copy-done | bytes 10027032
  71.7 5.1 %second_kernel.1 = (f32[12,8,2176]{2,1,0:T(8,128)S(1)}, f32[8,8,2176]{2,1,0:T(8,128)S(1)}, f32[8,8,2176]{2,1,0:T(8,128)S(1)}, f32[3,8,2176]{2,1,0:T(8,128)S(1)},...) custom-call(f32[12,12,8,2176]{3,2,1,0:T(8,128)S(1)} %copy-done.4, f32[12,12,8,2176]{3,2,1,0:T(8,128)S(1)} %get-tuple-element.46.c2, ...), custom_call_target="tpu_custom_call" | custom-call | tf_op jit(solution)/shard_map/second_kernel/pallas_call | solution.py:436
  76.8 0.0 collective-permute-start.8
  76.9 2.9 %collective-permute-start.9 = (f32[3,8,2176]{2,1,0:T(8,128)S(1)}, f32[3,8,2176]{2,1,0:T(8,128)S(1)}, u32[]{:S(2)}, u32[]{:S(2)}) collective-permute-start(f32[3,8,2176]{2,1,0:T(8,128)S(1)} %get-tuple-element.53), channel_id=1, source_target_pairs={{0,112},{16,0},{32,16},{48,32},{64,48},{80,64},{96,80},{112,96},{1... | collective-permute-start | bytes 626696 | tf_op jit(solution)/shard_map/ppermute | solution.py:451
  79.8 3.5 %collective-permute-done.8.above = f32[3,8,2176]{2,1,0:T(8,128)S(1)} collective-permute-done((f32[3,8,2176]{2,1,0:T(8,128)S(1)}, f32[3,8,2176]{2,1,0:T(8,128)S(1)}, u32[]{:S(2)}, u32[]{:S(2)}) %collective-permute-start.8) | collective-permute-done | bytes 208928 | tf_op jit(solution)/shard_map/ppermute | solution.py:451
  83.3 6.1 %third_kernel.1 = (f32[8,8,2176]{2,1,0:T(8,128)S(1)}, f32[2,8,2176]{2,1,0:T(8,128)S(1)}, f32[2,8,2176]{2,1,0:T(8,128)S(1)}) custom-call(f32[12,12,8,2176]{3,2,1,0:T(8,128)S(1)} %get-tuple-element.46.c2, f32[8,8,2176]{2,1,0:T(8,128)S(1)} %get-tuple-element.51.t2_own, f32[3,8,2176]{2,1,0:T(8,128)S(1)} %collective-permute-done.8.above, ...), custom_call_target="tpu_custom_call" | custom-call | tf_op jit(solution)/shard_map/third_kernel/pallas_call | solution.py:436
  89.4 0.0 collective-permute-start.10
  89.4 3.0 %collective-permute-start.11 = (f32[2,8,2176]{2,1,0:T(8,128)S(1)}, f32[2,8,2176]{2,1,0:T(8,128)S(1)}, u32[]{:S(2)}, u32[]{:S(2)}) collective-permute-start(f32[2,8,2176]{2,1,0:T(8,128)S(1)} %get-tuple-element.57), channel_id=1, source_target_pairs={{0,112},{16,0},{32,16},{48,32},{64,48},{80,64},{96,80},{112,96},{1... | collective-permute-start | bytes 417800 | tf_op jit(solution)/shard_map/ppermute | solution.py:451
  92.4 2.7 %collective-permute-done.10.above = f32[2,8,2176]{2,1,0:T(8,128)S(1)} collective-permute-done((f32[2,8,2176]{2,1,0:T(8,128)S(1)}, f32[2,8,2176]{2,1,0:T(8,128)S(1)}, u32[]{:S(2)}, u32[]{:S(2)}) %collective-permute-start.10) | collective-permute-done | bytes 139296 | tf_op jit(solution)/shard_map/ppermute | solution.py:451
  95.1 3.8 %fourth_kernel.1 = (f32[8,8,2176]{2,1,0:T(8,128)S(1)}, f32[3,8,2176]{2,1,0:T(8,128)S(1)}, f32[3,8,2176]{2,1,0:T(8,128)S(1)}) custom-call(f32[12,12,8,2176]{3,2,1,0:T(8,128)S(1)} %copy-done.4, f32[12,12,8,2176]{3,2,1,0:T(8,128)S(1)} %get-tuple-element.41.c0, f32[12,8,2176]{2,1,0:T(8,128)S(1)} %get-tuple-element.50.t1, ...), custom_call_target="tpu_custom_call" | custom-call | tf_op jit(solution)/shard_map/fourth_kernel/pallas_call | solution.py:436
  98.9 0.0 collective-permute-start.12
  98.9 3.0 %collective-permute-start.13 = (f32[3,8,2176]{2,1,0:T(8,128)S(1)}, f32[3,8,2176]{2,1,0:T(8,128)S(1)}, u32[]{:S(2)}, u32[]{:S(2)}) collective-permute-start(f32[3,8,2176]{2,1,0:T(8,128)S(1)} %get-tuple-element.61), channel_id=1, source_target_pairs={{0,112},{16,0},{32,16},{48,32},{64,48},{80,64},{96,80},{112,96},{1... | collective-permute-start | bytes 626696 | tf_op jit(solution)/shard_map/ppermute | solution.py:451
  101.9 3.5 %collective-permute-done.12.above = f32[3,8,2176]{2,1,0:T(8,128)S(1)} collective-permute-done((f32[3,8,2176]{2,1,0:T(8,128)S(1)}, f32[3,8,2176]{2,1,0:T(8,128)S(1)}, u32[]{:S(2)}, u32[]{:S(2)}) %collective-permute-start.12) | collective-permute-done | bytes 208928 | tf_op jit(solution)/shard_map/ppermute | solution.py:451
  105.3 0.0 collective-permute-done.13.below
  105.3 7.0 %fifth_kernel.1 = (f32[56,2048]{1,0:T(8,128)}, f32[56,2048]{1,0:T(8,128)}, f32[8,128]{1,0:T(8,128)S(1)}) custom-call(f32[12,12,8,2176]{3,2,1,0:T(8,128)S(1)} %get-tuple-element.41.c0, f32[12,8,2176]{2,1,0:T(8,128)S(1)} %get-tuple-element.42.t0, f32[8,8,2176]{2,1,0:T(8,128)S(1)} %get-tuple-element.59.v, f32[3,8,2176]{2,1,0:T(8,128)S(1)} %collective-permute-done.12.above, ...), custom_call_target="tpu_custom_call" | custom-call | tf_op jit(solution)/shard_map/fifth_kernel/pallas_call | solution.py:436
  112.3 0.0 collective-permute-start.14
  112.3 1.2 collective-permute-done.14
  113.5 1.6 %collective-permute-start.16 = (f32[3,8,128]{2,1,0:T(8,128)S(1)}, f32[3,8,128]{2,1,0:T(8,128)S(1)}, u32[]{:S(2)}, u32[]{:S(2)}) collective-permute-start(f32[3,8,128]{2,1,0:T(8,128)S(1)} %fusion.1), channel_id=1, source_target_pairs={{0,64},{16,80},{32,96},{48,112},{64,0},{80,16},{96,32},{112,48},{1... | collective-permute-start | bytes 36872 | tf_op jit(solution)/shard_map/ppermute | solution.py:456
  115.1 1.5 %collective-permute-start.17 = (f32[3,8,128]{2,1,0:T(8,128)S(1)}, f32[3,8,128]{2,1,0:T(8,128)S(1)}, u32[]{:S(2)}, u32[]{:S(2)}) collective-permute-start(f32[3,8,128]{2,1,0:T(8,128)S(1)} %fusion.1), channel_id=1, source_target_pairs={{0,96},{16,112},{32,64},{48,80},{64,32},{80,48},{96,0},{112,16},{1... | collective-permute-start | bytes 36872 | tf_op jit(solution)/shard_map/ppermute | solution.py:456
  116.6 0.8 collective-permute-start.15
  117.4 1.3 collective-permute-done.16
  118.7 1.3 collective-permute-done.17
  120.0 0.3 collective-permute-done.15
  120.3 2.0 %collective-permute-start.20 = (f32[3,8,128]{2,1,0:T(8,128)S(1)}, f32[3,8,128]{2,1,0:T(8,128)S(1)}, u32[]{:S(2)}, u32[]{:S(2)}) collective-permute-start(f32[3,8,128]{2,1,0:T(8,128)S(1)} %add_add_fusion.1), channel_id=1, source_target_pairs={{0,3},{1,2},{2,1},{3,0},{4,7},{5,6},{6,5},{7,4},{8,11},{9,10},{10,... | collective-permute-start | bytes 36872 | tf_op jit(solution)/shard_map/ppermute | solution.py:456
  122.3 0.0 collective-permute-start.19
  122.3 2.2 %collective-permute-start.18 = (f32[3,8,128]{2,1,0:T(8,128)S(1)}, f32[3,8,128]{2,1,0:T(8,128)S(1)}, u32[]{:S(2)}, u32[]{:S(2)}) collective-permute-start(f32[3,8,128]{2,1,0:T(8,128)S(1)} %add_add_fusion.1), channel_id=1, source_target_pairs={{0,1},{1,0},{2,3},{3,2},{4,5},{5,4},{6,7},{7,6},{8,9},{9,8},{10,11... | collective-permute-start | bytes 36872 | tf_op jit(solution)/shard_map/ppermute | solution.py:456
  124.4 0.9 collective-permute-done.20
  125.3 2.2 %collective-permute-done.19 = f32[3,8,128]{2,1,0:T(8,128)S(1)} collective-permute-done((f32[3,8,128]{2,1,0:T(8,128)S(1)}, f32[3,8,128]{2,1,0:T(8,128)S(1)}, u32[]{:S(2)}, u32[]{:S(2)}) %collective-permute-start.19) | collective-permute-done | bytes 12320 | tf_op jit(solution)/shard_map/ppermute | solution.py:456
  127.5 0.0 collective-permute-done.18
  127.5 4.0 %collective-permute-start.23 = (f32[3,8,128]{2,1,0:T(8,128)S(1)}, f32[3,8,128]{2,1,0:T(8,128)S(1)}, u32[]{:S(2)}, u32[]{:S(2)}) collective-permute-start(f32[3,8,128]{2,1,0:T(8,128)S(1)} %add_add_fusion), channel_id=1, source_target_pairs={{0,12},{1,13},{2,14},{3,15},{4,8},{5,9},{6,10},{7,11},{8,4},{9,5},... | collective-permute-start | bytes 36872 | tf_op jit(solution)/shard_map/ppermute | solution.py:456
  131.5 0.0 collective-permute-start.22
  131.6 0.9 collective-permute-start.21
  132.5 0.7 collective-permute-done.23
  133.2 3.5 %collective-permute-done.22 = f32[3,8,128]{2,1,0:T(8,128)S(1)} collective-permute-done((f32[3,8,128]{2,1,0:T(8,128)S(1)}, f32[3,8,128]{2,1,0:T(8,128)S(1)}, u32[]{:S(2)}, u32[]{:S(2)}) %collective-permute-start.22) | collective-permute-done | bytes 12320 | tf_op jit(solution)/shard_map/ppermute | solution.py:456
  136.8 0.1 fusion
  136.9 0.5 multiply_sqrt_fusion
  (20 shorter events, 0.1 us)
Async XLA Ops:
  0.6 1.9 %copy-start.5 = (f32[7,7,8,2048]{3,2,1,0:T(8,128)S(1)}, f32[7,7,8,2048]{3,2,1,0:T(8,128)}, u32[]{:S(2)}) copy-start(f32[7,7,8,2048]{3,2,1,0:T(8,128)} %param.5) | copy-start | bytes 9633796
  2.5 1.5 %copy-start.6 = (f32[4,7,8,2048]{3,2,1,0:T(8,128)S(1)}, f32[4,7,8,2048]{3,2,1,0:T(8,128)}, u32[]{:S(2)}) copy-start(f32[4,7,8,2048]{3,2,1,0:T(8,128)} %param.6) | copy-start | bytes 5505028
  4.0 1.0 copy-start.7
  5.1 0.8 copy-start.8
  10.5 3.8 %copy-start = (f32[12,12,8,2176]{3,2,1,0:T(8,128)}, f32[12,12,8,2176]{3,2,1,0:T(8,128)S(1)}, u32[]{:S(2)}) copy-start(f32[12,12,8,2176]{3,2,1,0:T(8,128)S(1)} %get-tuple-element.35.c0_in.c0) | copy-start | bytes 30081028
  14.4 32.2 %collective-permute-start = (f32[2,12,8,2048]{3,2,1,0:T(8,128)}, f32[2,12,8,2048]{3,2,1,0:T(8,128)S(1)}, u32[]{:S(2)}, u32[]{:S(2)}) collective-permute-start(f32[2,12,8,2048]{3,2,1,0:T(8,128)} %get-tuple-element.37), channel_id=1, source_target_pairs={{0,16},{16,32},{32,48},{48,64},{64,80},{80,96},{96,112},{112,0},{1... | collective-permute-start | bytes 4718600 | tf_op jit(solution)/shard_map/ppermute | solution.py:451
  14.4 32.2 %collective-permute-start.1 = (f32[2,12,8,2048]{3,2,1,0:T(8,128)}, f32[2,12,8,2048]{3,2,1,0:T(8,128)}, u32[]{:S(2)}, u32[]{:S(2)}) collective-permute-start(f32[2,12,8,2048]{3,2,1,0:T(8,128)} %get-tuple-element.38), channel_id=1, source_target_pairs={{0,112},{16,0},{32,16},{48,32},{64,48},{80,64},{96,80},{112,96},{1... | collective-permute-start | bytes 4718600 | tf_op jit(solution)/shard_map/ppermute | solution.py:451
  17.3 22.7 %collective-permute-start.2 = (f32[8,12,8,128]{3,2,1,0:T(8,128)S(1)}, f32[8,12,8,128]{3,2,1,0:T(8,128)}, u32[]{:S(2)}, u32[]{:S(2)}) collective-permute-start(f32[8,12,8,128]{3,2,1,0:T(8,128)S(1)} %get-tuple-element.39), channel_id=1, source_target_pairs={{0,15},{1,0},{2,1},{3,2},{4,3},{5,4},{6,5},{7,6},{8,7},{9,8},{10,9... | collective-permute-start | bytes 1179656 | tf_op jit(solution)/shard_map/ppermute | solution.py:451
  23.6 16.4 %collective-permute-start.3 = (f32[8,12,8,128]{3,2,1,0:T(8,128)S(1)}, f32[8,12,8,128]{3,2,1,0:T(8,128)}, u32[]{:S(2)}, u32[]{:S(2)}) collective-permute-start(f32[8,12,8,128]{3,2,1,0:T(8,128)S(1)} %get-tuple-element.40), channel_id=1, source_target_pairs={{0,1},{1,2},{2,3},{3,4},{4,5},{5,6},{6,7},{7,8},{8,9},{9,10},{10,1... | collective-permute-start | bytes 1179656 | tf_op jit(solution)/shard_map/ppermute | solution.py:451
  23.6 3.8 %copy-start.1 = (f32[12,12,8,2176]{3,2,1,0:T(8,128)S(1)}, f32[12,12,8,2176]{3,2,1,0:T(8,128)}, u32[]{:S(2)}) copy-start(f32[12,12,8,2176]{3,2,1,0:T(8,128)} %copy-done) | copy-start | bytes 30081028
  27.5 19.1 %copy-start.2 = (f32[12,12,8,2176]{3,2,1,0:T(8,128)S(1)}, f32[12,12,8,2176]{3,2,1,0:T(8,128)}, u32[]{:S(2)}) copy-start(f32[12,12,8,2176]{3,2,1,0:T(8,128)} %copy-done) | copy-start | bytes 30081028
  41.3 2.2 %collective-permute-start.5 = (f32[2,12,8,128]{3,2,1,0:T(8,128)S(1)}, f32[2,12,8,128]{3,2,1,0:T(8,128)S(1)}, u32[]{:S(2)}, u32[]{:S(2)}) collective-permute-start(f32[2,12,8,128]{3,2,1,0:T(8,128)S(1)} %get-tuple-element.67), channel_id=1, source_target_pairs={{0,112},{16,0},{32,16},{48,32},{64,48},{80,64},{96,80},{112,96},{1... | collective-permute-start | bytes 294920 | tf_op jit(solution)/shard_map/ppermute | solution.py:451
  41.3 5.3 %collective-permute-start.4 = (f32[2,12,8,128]{3,2,1,0:T(8,128)S(1)}, f32[2,12,8,128]{3,2,1,0:T(8,128)S(1)}, u32[]{:S(2)}, u32[]{:S(2)}) collective-permute-start(f32[2,12,8,128]{3,2,1,0:T(8,128)S(1)} %get-tuple-element.68), channel_id=1, source_target_pairs={{0,16},{16,32},{32,48},{48,64},{64,80},{80,96},{96,112},{112,0},{1... | collective-permute-start | bytes 294920 | tf_op jit(solution)/shard_map/ppermute | solution.py:451
  53.8 14.1 %collective-permute-start.6 = (f32[2,8,2176]{2,1,0:T(8,128)S(1)}, f32[2,8,2176]{2,1,0:T(8,128)S(1)}, u32[]{:S(2)}, u32[]{:S(2)}) collective-permute-start(f32[2,8,2176]{2,1,0:T(8,128)S(1)} %get-tuple-element.48), channel_id=1, source_target_pairs={{0,16},{16,32},{32,48},{48,64},{64,80},{80,96},{96,112},{112,0},{1... | collective-permute-start | bytes 417800 | tf_op jit(solution)/shard_map/ppermute | solution.py:451
  53.8 14.0 %collective-permute-start.7 = (f32[2,8,2176]{2,1,0:T(8,128)S(1)}, f32[2,8,2176]{2,1,0:T(8,128)S(1)}, u32[]{:S(2)}, u32[]{:S(2)}) collective-permute-start(f32[2,8,2176]{2,1,0:T(8,128)S(1)} %get-tuple-element.49), channel_id=1, source_target_pairs={{0,112},{16,0},{32,16},{48,32},{64,48},{80,64},{96,80},{112,96},{1... | collective-permute-start | bytes 417800 | tf_op jit(solution)/shard_map/ppermute | solution.py:451
  64.0 3.8 %copy-start.3 = (f32[12,12,8,2176]{3,2,1,0:T(8,128)}, f32[12,12,8,2176]{3,2,1,0:T(8,128)S(1)}, u32[]{:S(2)}) copy-start(f32[12,12,8,2176]{3,2,1,0:T(8,128)S(1)} %get-tuple-element.45.c1) | copy-start | bytes 30081028
  67.9 3.9 %copy-start.4 = (f32[12,12,8,2176]{3,2,1,0:T(8,128)S(1)}, f32[12,12,8,2176]{3,2,1,0:T(8,128)}, u32[]{:S(2)}) copy-start(f32[12,12,8,2176]{3,2,1,0:T(8,128)} %copy-done.3) | copy-start | bytes 30081028
  76.8 6.4 %collective-permute-start.8 = (f32[3,8,2176]{2,1,0:T(8,128)S(1)}, f32[3,8,2176]{2,1,0:T(8,128)S(1)}, u32[]{:S(2)}, u32[]{:S(2)}) collective-permute-start(f32[3,8,2176]{2,1,0:T(8,128)S(1)} %get-tuple-element.52), channel_id=1, source_target_pairs={{0,16},{16,32},{32,48},{48,64},{64,80},{80,96},{96,112},{112,0},{1... | collective-permute-start | bytes 626696 | tf_op jit(solution)/shard_map/ppermute | solution.py:451
  76.9 6.4 %collective-permute-start.9 = (f32[3,8,2176]{2,1,0:T(8,128)S(1)}, f32[3,8,2176]{2,1,0:T(8,128)S(1)}, u32[]{:S(2)}, u32[]{:S(2)}) collective-permute-start(f32[3,8,2176]{2,1,0:T(8,128)S(1)} %get-tuple-element.53), channel_id=1, source_target_pairs={{0,112},{16,0},{32,16},{48,32},{64,48},{80,64},{96,80},{112,96},{1... | collective-permute-start | bytes 626696 | tf_op jit(solution)/shard_map/ppermute | solution.py:451
  89.4 5.7 %collective-permute-start.10 = (f32[2,8,2176]{2,1,0:T(8,128)S(1)}, f32[2,8,2176]{2,1,0:T(8,128)S(1)}, u32[]{:S(2)}, u32[]{:S(2)}) collective-permute-start(f32[2,8,2176]{2,1,0:T(8,128)S(1)} %get-tuple-element.56), channel_id=1, source_target_pairs={{0,16},{16,32},{32,48},{48,64},{64,80},{80,96},{96,112},{112,0},{1... | collective-permute-start | bytes 417800 | tf_op jit(solution)/shard_map/ppermute | solution.py:451
  89.4 5.7 %collective-permute-start.11 = (f32[2,8,2176]{2,1,0:T(8,128)S(1)}, f32[2,8,2176]{2,1,0:T(8,128)S(1)}, u32[]{:S(2)}, u32[]{:S(2)}) collective-permute-start(f32[2,8,2176]{2,1,0:T(8,128)S(1)} %get-tuple-element.57), channel_id=1, source_target_pairs={{0,112},{16,0},{32,16},{48,32},{64,48},{80,64},{96,80},{112,96},{1... | collective-permute-start | bytes 417800 | tf_op jit(solution)/shard_map/ppermute | solution.py:451
  98.9 6.5 %collective-permute-start.12 = (f32[3,8,2176]{2,1,0:T(8,128)S(1)}, f32[3,8,2176]{2,1,0:T(8,128)S(1)}, u32[]{:S(2)}, u32[]{:S(2)}) collective-permute-start(f32[3,8,2176]{2,1,0:T(8,128)S(1)} %get-tuple-element.60), channel_id=1, source_target_pairs={{0,16},{16,32},{32,48},{48,64},{64,80},{80,96},{96,112},{112,0},{1... | collective-permute-start | bytes 626696 | tf_op jit(solution)/shard_map/ppermute | solution.py:451
  98.9 6.4 %collective-permute-start.13 = (f32[3,8,2176]{2,1,0:T(8,128)S(1)}, f32[3,8,2176]{2,1,0:T(8,128)S(1)}, u32[]{:S(2)}, u32[]{:S(2)}) collective-permute-start(f32[3,8,2176]{2,1,0:T(8,128)S(1)} %get-tuple-element.61), channel_id=1, source_target_pairs={{0,112},{16,0},{32,16},{48,32},{64,48},{80,64},{96,80},{112,96},{1... | collective-permute-start | bytes 626696 | tf_op jit(solution)/shard_map/ppermute | solution.py:451
  112.3 1.2 collective-permute-start.14
  113.5 5.2 %collective-permute-start.16 = (f32[3,8,128]{2,1,0:T(8,128)S(1)}, f32[3,8,128]{2,1,0:T(8,128)S(1)}, u32[]{:S(2)}, u32[]{:S(2)}) collective-permute-start(f32[3,8,128]{2,1,0:T(8,128)S(1)} %fusion.1), channel_id=1, source_target_pairs={{0,64},{16,80},{32,96},{48,112},{64,0},{80,16},{96,32},{112,48},{1... | collective-permute-start | bytes 36872 | tf_op jit(solution)/shard_map/ppermute | solution.py:456
  115.1 4.9 %collective-permute-start.17 = (f32[3,8,128]{2,1,0:T(8,128)S(1)}, f32[3,8,128]{2,1,0:T(8,128)S(1)}, u32[]{:S(2)}, u32[]{:S(2)}) collective-permute-start(f32[3,8,128]{2,1,0:T(8,128)S(1)} %fusion.1), channel_id=1, source_target_pairs={{0,96},{16,112},{32,64},{48,80},{64,32},{80,48},{96,0},{112,16},{1... | collective-permute-start | bytes 36872 | tf_op jit(solution)/shard_map/ppermute | solution.py:456
  116.6 3.7 %collective-permute-start.15 = (f32[3,8,128]{2,1,0:T(8,128)S(1)}, f32[3,8,128]{2,1,0:T(8,128)S(1)}, u32[]{:S(2)}, u32[]{:S(2)}) collective-permute-start(f32[3,8,128]{2,1,0:T(8,128)S(1)} %fusion.1), channel_id=1, source_target_pairs={{0,32},{16,48},{32,0},{48,16},{64,96},{80,112},{96,64},{112,80},{1... | collective-permute-start | bytes 36872 | tf_op jit(solution)/shard_map/ppermute | solution.py:456
  120.3 5.0 %collective-permute-start.20 = (f32[3,8,128]{2,1,0:T(8,128)S(1)}, f32[3,8,128]{2,1,0:T(8,128)S(1)}, u32[]{:S(2)}, u32[]{:S(2)}) collective-permute-start(f32[3,8,128]{2,1,0:T(8,128)S(1)} %add_add_fusion.1), channel_id=1, source_target_pairs={{0,3},{1,2},{2,1},{3,0},{4,7},{5,6},{6,5},{7,4},{8,11},{9,10},{10,... | collective-permute-start | bytes 36872 | tf_op jit(solution)/shard_map/ppermute | solution.py:456
  122.3 5.2 %collective-permute-start.19 = (f32[3,8,128]{2,1,0:T(8,128)S(1)}, f32[3,8,128]{2,1,0:T(8,128)S(1)}, u32[]{:S(2)}, u32[]{:S(2)}) collective-permute-start(f32[3,8,128]{2,1,0:T(8,128)S(1)} %add_add_fusion.1), channel_id=1, source_target_pairs={{0,2},{1,3},{2,0},{3,1},{4,6},{5,7},{6,4},{7,5},{8,10},{9,11},{10,... | collective-permute-start | bytes 36872 | tf_op jit(solution)/shard_map/ppermute | solution.py:456
  122.3 5.2 %collective-permute-start.18 = (f32[3,8,128]{2,1,0:T(8,128)S(1)}, f32[3,8,128]{2,1,0:T(8,128)S(1)}, u32[]{:S(2)}, u32[]{:S(2)}) collective-permute-start(f32[3,8,128]{2,1,0:T(8,128)S(1)} %add_add_fusion.1), channel_id=1, source_target_pairs={{0,1},{1,0},{2,3},{3,2},{4,5},{5,4},{6,7},{7,6},{8,9},{9,8},{10,11... | collective-permute-start | bytes 36872 | tf_op jit(solution)/shard_map/ppermute | solution.py:456
  127.5 5.7 %collective-permute-start.23 = (f32[3,8,128]{2,1,0:T(8,128)S(1)}, f32[3,8,128]{2,1,0:T(8,128)S(1)}, u32[]{:S(2)}, u32[]{:S(2)}) collective-permute-start(f32[3,8,128]{2,1,0:T(8,128)S(1)} %add_add_fusion), channel_id=1, source_target_pairs={{0,12},{1,13},{2,14},{3,15},{4,8},{5,9},{6,10},{7,11},{8,4},{9,5},... | collective-permute-start | bytes 36872 | tf_op jit(solution)/shard_map/ppermute | solution.py:456
  131.5 5.2 %collective-permute-start.22 = (f32[3,8,128]{2,1,0:T(8,128)S(1)}, f32[3,8,128]{2,1,0:T(8,128)S(1)}, u32[]{:S(2)}, u32[]{:S(2)}) collective-permute-start(f32[3,8,128]{2,1,0:T(8,128)S(1)} %add_add_fusion), channel_id=1, source_target_pairs={{0,8},{1,9},{2,10},{3,11},{4,12},{5,13},{6,14},{7,15},{8,0},{9,1},... | collective-permute-start | bytes 36872 | tf_op jit(solution)/shard_map/ppermute | solution.py:456
  131.6 5.2 %collective-permute-start.21 = (f32[3,8,128]{2,1,0:T(8,128)S(1)}, f32[3,8,128]{2,1,0:T(8,128)S(1)}, u32[]{:S(2)}, u32[]{:S(2)}) collective-permute-start(f32[3,8,128]{2,1,0:T(8,128)S(1)} %add_add_fusion), channel_id=1, source_target_pairs={{0,4},{1,5},{2,6},{3,7},{4,0},{5,1},{6,2},{7,3},{8,12},{9,13},{10,... | collective-permute-start | bytes 36872 | tf_op jit(solution)/shard_map/ppermute | solution.py:456

commit v2 on v0

v2 whole, which is shorter than its diff:
```python
import jax
import jax.numpy as jnp
from jax import lax
from jax.experimental import pallas as pl
from jax.experimental.pallas import tpu as pltpu
from jax.sharding import PartitionSpec as P

FIELDS = 7
ROWS = 8
WIDE = 2
EXT = ROWS + 2 * WIDE
T = 128
PHASES = 4
BLOCK = PHASES * T
SIDE = 8
SIDE_COLS = SIDE * PHASES
DAMP = 0.7
PLANES = 12
SWEEP_W = 11
SOURCE = 12
FINE = 13
F32 = jnp.float32
BF16 = jnp.bfloat16
LIMIT = 8 * 2**20
GRID = FIELDS * ROWS
RAW = PLANES * GRID
GROUPS = T // SIDE_COLS
PACK = RAW // GROUPS
PER_GROUP = PLANES // GROUPS


def iota(shape, dim):
    return lax.broadcasted_iota(jnp.int32, shape, dim)


def tile(j):
    return pl.ds(pl.multiple_of(j * T, T), T)


def each(count, body):
    def step(j, carry):
        body(j)
        return carry

    lax.fori_loop(0, count, step, 0)


class FineRows:
    def __init__(self, main, near, far=None):
        self.main, self.near, self.far = main, near, far
        self.shape = main.shape

    def __getitem__(self, at):
        r, *rest = at
        if r in (0, EXT - 1):
            return self.far[(r // (EXT - 1), *rest)]
        if r in (1, EXT - 2):
            return self.near[(r // (EXT - 2), *rest)]
        return self.main[(r - WIDE, *rest)]


class WithFar:
    def __init__(self, main, far):
        self.main, self.far = main, far
        self.shape = main.shape

    def __getitem__(self, at):
        r, *rest = at
        if r in (0, EXT - 1):
            return self.far[(r // (EXT - 1), *rest)]
        return self.main[(r, *rest)]


class SourceOf:
    def __init__(self, c):
        self.c = c

    def __getitem__(self, at):
        r, *rest = at
        return self.c[(r, SOURCE, *rest)]


def own_order():
    rows, cols = iota((BLOCK, BLOCK), 0), iota((BLOCK, BLOCK), 1)
    return jnp.where(rows == (cols % T) * PHASES + cols // T, 1.0, 0.0).astype(BF16)


def natural_order():
    rows, cols = iota((BLOCK, BLOCK), 0), iota((BLOCK, BLOCK), 1)
    return jnp.where(cols == (rows % T) * PHASES + rows // T, 1.0, 0.0).astype(BF16)


def side_order():
    rows, cols = iota((2 * T, BLOCK), 0), iota((2 * T, BLOCK), 1)
    lane, phase = cols % T, cols // T
    at = rows % SIDE_COLS
    after = (lane < SIDE) & (rows < T) & (at == lane * PHASES + phase)
    before = (lane >= T - SIDE) & (rows >= T) & (at == (lane - T + SIDE) * PHASES + phase)
    return jnp.where(after | before, 1.0, 0.0).astype(BF16)


def group_of(x, g):
    return jnp.where(iota(x.shape, 1) % T // SIDE_COLS == g, x, 0.0)


def reorder(x, order):
    high = x.astype(BF16)
    low = (x - high.astype(F32)).astype(BF16)
    return jnp.dot(high, order, preferred_element_type=F32) + jnp.dot(low, order, preferred_element_type=F32)


def diagonal(planes):
    sub = iota(planes[0].shape, 0)
    out = planes[FIELDS - 1]
    for f in range(FIELDS - 1):
        out = jnp.where(sub == f, planes[f], out)
    return out


def with_face_sum(planes, faces):
    total = faces[0] + faces[1] + faces[2] + faces[3]
    sub = iota(total.shape, 0)
    return [jnp.where(sub == f, x + total, x) for f, x in enumerate(planes)]


def weight_of(planes, mask):
    return jnp.where(mask > 0.0, DAMP / diagonal(planes), 0.0)


def fetch(jac, face, src, act, raw, flags, sems, columns):
    blocks = src.shape[-1] // columns

    def copies(b):
        cols = pl.ds(b * columns, columns)
        moves = [(jac.at[f, :, cols], raw.at[pl.ds(f * GRID, GRID), cols]) for f in range(FIELDS)]
        moves += [(face.at[k, :, cols], raw.at[pl.ds((FIELDS + k) * GRID, GRID), cols]) for k in range(4)]
        moves += [(src.at[:, cols], raw.at[pl.ds((PLANES - 1) * GRID, GRID), cols])]
        moves += [(act.at[:, cols], flags.at[:, cols])]
        return [pltpu.make_async_copy(a, d, sems.at[b, i]) for i, (a, d) in enumerate(moves)]

    todo = [copies(b) for b in range(blocks)]
    for group in todo:
        for copy in group:
            copy.start()

    def waiter(group):
        def wait():
            for copy in group:
                copy.wait()

        return wait

    return [waiter(group) for group in todo]


def send_kernel(jac, face, src, act, top, bottom, left, right, raw, flags, buf, sems):
    columns = src.shape[-1]
    waits = fetch(jac, face, src, act, raw, flags, sems, BLOCK)
    per = BLOCK // T

    def rows_of(b):
        def body(i):
            sl = tile(b * per + i)
            for k in range(PLANES):
                buf[k * GRID : k * GRID + GRID] = raw[k * GRID : k * GRID + GRID, sl]

            def pick(k, r):
                return buf[pl.ds(k * GRID + r, FIELDS, stride=ROWS), :]

            for out, near, far, face_k in ((top, 0, 1, 3), (bottom, ROWS - 1, ROWS - 2, 2)):
                for k in range(PLANES):
                    out[k, 0:FIELDS, sl] = pick(k, near)
                out[PLANES - 1, FIELDS : FIELDS + 1, sl] = flags[near : near + 1, sl].astype(F32)
                planes = [pick(k, far) for k in range(PLANES)]
                mask = flags[far : far + 1, sl].astype(F32)
                weight = weight_of(with_face_sum(planes[:FIELDS], planes[FIELDS : FIELDS + 4]), mask)
                out[PLANES, 0:FIELDS, sl] = planes[FIELDS + face_k] * weight * planes[PLANES - 1]
                for k in range(PLANES):
                    out[FINE + k, 0:FIELDS, sl] = planes[k]
                out[FINE + PLANES - 1, FIELDS : FIELDS + 1, sl] = mask

        each(per, body)

    for b, wait in enumerate(waits):
        wait()
        rows_of(b)
    lane = iota((PACK, T), 1) // SIDE_COLS
    for out, at, move in ((left, 0, 0), (right, columns - T, SIDE_COLS)):
        packed = None
        for g in range(GROUPS):
            part = raw[g * PACK : g * PACK + PACK, at : at + T]
            shift = (g * SIDE_COLS + move) % T
            part = pltpu.roll(part, shift, 1) if shift else part
            packed = part if packed is None else jnp.where(lane == g, part, packed)
        out[0:PACK] = packed
        mask = flags[:, at : at + T].astype(F32)
        out[PACK : PACK + ROWS] = pltpu.roll(mask, move, 1) if move else mask


def place(buf, masks, out, sl, domain):
    for r in range(ROWS):
        for p in range(PHASES):
            def pick(k):
                return buf[p, pl.ds(k * GRID + r, FIELDS, stride=ROWS), :]

            faces = [pick(FIELDS + k) for k in range(4)]
            planes = with_face_sum([pick(f) for f in range(FIELDS)], faces)
            mask = masks[p, r : r + 1, :]
            if domain is not None:
                mask = jnp.where(domain > 0.0, mask, 0.0)
            for k, x in enumerate(planes + faces + [weight_of(planes, mask), pick(PLANES - 1)]):
                out[r, k, p, 0:FIELDS, sl] = x


def side_domain(ends):
    lane = iota((1, T), 1)
    return jnp.where(lane < SIDE, ends[3], jnp.where(lane >= T - SIDE, ends[2], 0.0))


def corner_kernel(from_right, from_left, order_side, top, bottom):
    for side, packed in enumerate((from_right, from_left)):
        for out, rows in ((top, (0, 1)), (bottom, (ROWS - 1, ROWS - 2))):
            for i, r in enumerate(rows):
                for k in range(PER_GROUP):
                    out[i, side, k * 8 : k * 8 + FIELDS] = packed[pl.ds(k * GRID + r, FIELDS, stride=ROWS), :]
                out[i, side, FIELDS : FIELDS + 1] = packed[PACK + r : PACK + r + 1]


def corner_planes(corners, order):
    parts = [jnp.concatenate([c[i, 0], c[i, 1]], axis=1) for c in corners for i in range(2)]
    both = jnp.concatenate(parts, axis=0)
    size = PER_GROUP * 8
    packs = [reorder(group_of(both, g), order) for g in range(GROUPS)]
    result = []
    for n in range(len(parts)):
        def plane(k, p):
            first = n * size + k % PER_GROUP * 8
            return packs[k // PER_GROUP][first : first + 8, p * T : p * T + T]

        planes = [[plane(k, p) for p in range(PHASES)] for k in range(PLANES)]
        masks = [planes[0][p][FIELDS : FIELDS + 1] for p in range(PHASES)]
        result.append((planes, masks))
    return result


def side_kernel(ends, from_right, from_left, own, order, main, buf, masks, sems):
    inner = own.shape[-1]
    copies = [pltpu.make_async_copy(own.at[r], main.at[r, :, :, :, pl.ds(0, inner)], sems.at[r]) for r in range(ROWS)]
    for copy in copies:
        copy.start()
    both = jnp.concatenate([from_right[...], from_left[...]], axis=1)
    for g in range(GROUPS):
        x = reorder(group_of(both, g), order[...])
        for p in range(PHASES):
            buf[p, g * PACK : g * PACK + PACK] = x[0:PACK, p * T : p * T + T]
            if g == 0:
                masks[p] = x[PACK : PACK + ROWS, p * T : p * T + T]
    place(buf, masks, main, slice(inner, inner + T), side_domain(ends))
    for copy in copies:
        copy.wait()


def own_kernel(jac, face, src, act, own, order, order_side, raw, flags, buf, masks, stage, sems, out_sems):
    waits = fetch(jac, face, src, act, raw, flags, sems, BLOCK)
    order[...] = own_order()
    order_side[...] = side_order()
    outs = []
    for b, wait in enumerate(waits):
        wait()
        cols = slice(b * BLOCK, b * BLOCK + BLOCK)
        x = reorder(raw[:, cols], order[...])
        m = jnp.dot(flags[:, cols].astype(F32).astype(BF16), order[...], preferred_element_type=F32)
        for p in range(PHASES):
            buf[b % 2, p] = x[:, p * T : p * T + T]
            masks[b % 2, p] = m[:, p * T : p * T + T]
        if b >= 2:
            outs[b - 2].wait()
        place(buf.at[b % 2], masks.at[b % 2], stage.at[b % 2], slice(0, T), None)
        outs.append(pltpu.make_async_copy(stage.at[b % 2], own.at[:, :, :, :, pl.ds(b * T, T)], out_sems.at[b]))
        outs[b].start()
    for copy in outs[-2:]:
        copy.wait()


def row_flag(ends, r):
    if r < WIDE:
        return ends[0]
    if r >= WIDE + ROWS:
        return ends[1]
    return None


def merge(fine):
    count = len(fine[0]) // 2
    sub = iota(fine[0][0].shape, 0)
    f0, f1, f2, f3 = fine[FIELDS : FIELDS + 4]
    inner = [f1[2 * p + 1] + f0[2 * p] for p in range(count)]
    coarse = []
    for f in range(FIELDS):
        both = [fine[f][2 * p] + fine[f][2 * p + 1] for p in range(count)]
        coarse.append([jnp.where(sub == f, both[p] - inner[p], both[p]) for p in range(count)])
    coarse.append([f0[2 * p + 1] for p in range(count)])
    coarse.append([f1[2 * p] for p in range(count)])
    coarse.append([f2[2 * p] + f2[2 * p + 1] for p in range(count)])
    coarse.append([f3[2 * p] + f3[2 * p + 1] for p in range(count)])
    return coarse


def build_levels(read, outs, sl, domain):
    fine = [[read(k, p) for p in range(PHASES)] for k in range(PLANES - 1)]
    for write in outs:
        fine = merge(fine)
        for p in range(len(fine[0])):
            weight = DAMP / diagonal([fine[f][p] for f in range(FIELDS)])
            if domain is not None:
                weight = jnp.where(domain > 0.0, weight, 0.0)
            if write is not None:
                for k, planes in enumerate(fine):
                    write(k, p, planes[p])
                write(SWEEP_W, p, weight)


def levels_kernel(ends, main, near, c1, c2):
    tiles = main.shape[-1] // T
    sides = side_domain(ends)

    def build(source, row, r, sl, domain):
        def put(out):
            def write(k, p, x):
                out[r, k, p, :, sl] = x

            return write

        build_levels(lambda k, p: source[row, k, p, :, sl], [put(c1), put(c2)], sl, domain)

    def body(r):
        each(tiles - 1, lambda j: build(main, r, r + WIDE, tile(j), None))

    each(ROWS, body)
    sl = slice((tiles - 1) * T, tiles * T)
    each(ROWS, lambda r: build(main, r, r + WIDE, sl, sides))
    for i, r in enumerate((1, EXT - 2)):
        each(tiles - 1, lambda j: build(near, i, r, tile(j), row_flag(ends, r)))
        build(near, i, r, sl, sides * row_flag(ends, r))


def far_kernel(ends, rows_above, rows_below, corner_above, corner_below, order, order_side, far, order_out):
    order_out[...] = natural_order()
    wide = far.shape[-1]

    def put(i, p, planes, mask, sl):
        faces = planes[FIELDS : FIELDS + 4]
        jac = with_face_sum(planes[:FIELDS], faces)
        for k, x in enumerate(jac + faces + [weight_of(jac, mask), planes[PLANES - 1]]):
            far[i, k, p, :, sl] = x

    def fill(j):
        cols = pl.ds(pl.multiple_of(j * BLOCK, BLOCK), BLOCK)
        for i, rows in enumerate((rows_above, rows_below)):
            x = reorder(rows[FINE : FINE + PLANES, :, cols].reshape(PLANES * 8, BLOCK), order[...])
            for p in range(PHASES):
                planes = [x[k * 8 : k * 8 + 8, p * T : p * T + T] for k in range(PLANES)]
                put(i, p, planes, planes[PLANES - 1][FIELDS : FIELDS + 1] * ends[i], tile(j))

    each(wide // T - 1, fill)
    corners = corner_planes((corner_above, corner_below), order_side[...])
    for i in range(2):
        domain = side_domain(ends) * ends[i]
        planes, masks = corners[2 * i + 1]
        for p in range(PHASES):
            put(i, p, [x[p] for x in planes], jnp.where(domain > 0.0, masks[p], 0.0), slice(wide - T, wide))


def apply_at(c, r, v, j, above=None, below=None):
    tiles = c.shape[-1] // T
    count = c.shape[2]
    sl = tile(j)
    before = tile(lax.rem(j + tiles - 1, tiles))
    after = tile(lax.rem(j + 1, tiles))
    lane = iota((8, T), 1)
    here = [v[r, p, :, sl] for p in range(count)]
    k = FIELDS
    east = [c[r, k, p, :, sl] * here[p] for p in range(count)]
    west = [c[r, k + 1, p, :, sl] * here[p] for p in range(count)]
    end = count - 1
    wrap = jnp.where(lane == T - 1, c[r, k, end, :, before] * v[r, end, :, before], east[end])
    from_left = [pltpu.roll(wrap, 1, 1)] + east[:end]
    wrap = jnp.where(lane == 0, c[r, k + 1, 0, :, after] * v[r, 0, :, after], west[0])
    from_right = west[1:] + [pltpu.roll(wrap, T - 1, 1)]
    outs = []
    for p in range(count):
        out = c[r, 0, p, :, sl] * v[r, p, 0:1, sl]
        for f in range(1, FIELDS):
            out = out + c[r, f, p, :, sl] * v[r, p, f : f + 1, sl]
        up = c[r - 1, k + 2, p, :, sl] * v[r - 1, p, :, sl] if above is None else above[p, :, sl]
        down = c[r + 1, k + 3, p, :, sl] * v[r + 1, p, :, sl] if below is None else below[p, :, sl]
        outs.append(out - (from_left[p] + from_right[p]) - (up + down))
    return outs


def smooth(c, t, old, new, first, last, above=None, below=None):
    def body(j):
        sl = tile(j)
        for r in range(first, last):
            up = above if r == first else None
            down = below if r == last - 1 else None
            for p, out in enumerate(apply_at(c, r, old, j, up, down)):
                diff = t[r, p, :, sl] - out
                new[r, p, :, sl] = old[r, p, :, sl] + diff * c[r, SWEEP_W, p, :, sl]

    each(c.shape[-1] // T, body)


def gather_rows(out, own, above, below, j, wide, weight=None):
    sl = tile(j)
    for r in range(WIDE - wide, WIDE + ROWS + wide):
        for p in range(out.shape[1]):
            if r < WIDE:
                val = above[WIDE - 1 - r, p, :, sl]
            elif r < WIDE + ROWS:
                val = own[r - WIDE, p, :, sl]
            else:
                val = below[r - WIDE - ROWS, p, :, sl]
            if weight is not None and not WIDE <= r < WIDE + ROWS:
                val = jnp.where(weight[r, SWEEP_W, p, :, sl] != 0.0, val, 0.0)
            out[r, p, :, sl] = val


def send_rows(top, bottom, row, p, sl, val, wide, product):
    if row < wide:
        top[row, p, :, sl] = val
    if row >= ROWS - wide:
        bottom[ROWS - 1 - row, p, :, sl] = val
    if row == wide:
        top[wide, p, :, sl] = product(FIELDS + 3)
    if row == ROWS - 1 - wide:
        bottom[wide, p, :, sl] = product(FIELDS + 2)


def first_kernel(ends, main, rows_above, rows_below, corner_above, corner_below, order, order_side, near, v2, t1, t1_top, t1_bottom, sums, va, vb, prods):
    tiles = main.shape[-1] // T
    c0 = FineRows(main, near)
    t0 = SourceOf(c0)
    last = slice((tiles - 1) * T, tiles * T)

    def put(i, p, planes, mask, sl):
        faces = planes[FIELDS : FIELDS + 4]
        source = planes[PLANES - 1]
        jac = with_face_sum(planes[:FIELDS], faces)
        weight = weight_of(jac, mask)
        for k, x in enumerate(jac + faces + [weight, source]):
            near[i, k, p, :, sl] = x
        va[1 if i == 0 else EXT - 2, p, :, sl] = weight * source

    def fill(j):
        sl = tile(j)
        cols = pl.ds(pl.multiple_of(j * BLOCK, BLOCK), BLOCK)
        for i, rows in enumerate((rows_above, rows_below)):
            x = reorder(rows[0:FINE, :, cols].reshape(FINE * 8, BLOCK), order[...])
            for p in range(PHASES):
                planes = [x[k * 8 : k * 8 + 8, p * T : p * T + T] for k in range(FINE)]
                put(i, p, planes, planes[PLANES - 1][FIELDS : FIELDS + 1] * ends[i], sl)
                prods[i, p, :, sl] = planes[PLANES]

    each(tiles - 1, fill)
    sides = side_domain(ends)
    corners = corner_planes((corner_above, corner_below), order_side[...])
    for i in range(2):
        domain = sides * ends[i]
        planes, masks = corners[2 * i]
        far, far_masks = corners[2 * i + 1]
        for p in range(PHASES):
            put(i, p, [x[p] for x in planes], jnp.where(domain > 0.0, masks[p], 0.0), last)
            here = [x[p] for x in far]
            jac = with_face_sum(here[:FIELDS], here[FIELDS : FIELDS + 4])
            weight = weight_of(jac, jnp.where(domain > 0.0, far_masks[p], 0.0))
            prods[i, p, :, last] = here[FIELDS + 2 + i] * weight * here[PLANES - 1]

    def own(j):
        sl = tile(j)
        for r in range(WIDE, WIDE + ROWS):
            for p in range(PHASES):
                va[r, p, :, sl] = c0[r, SWEEP_W, p, :, sl] * t0[r, p, :, sl]

    each(tiles, own)

    smooth(c0, t0, va, vb, 1, EXT - 1, prods.at[0], prods.at[1])
    sums[...] = jnp.zeros_like(sums)

    def rest(j):
        sl = tile(j)
        total = jnp.zeros((8, T), F32)
        for r in range(WIDE, WIDE + ROWS):
            res = []
            for p, out in enumerate(apply_at(c0, r, vb, j)):
                diff = t0[r, p, :, sl] - out
                res.append(jnp.where(c0[r, SWEEP_W, p, :, sl] != 0.0, diff, 0.0))
                total = total + res[p] * res[p]
                v2[r - WIDE, p, :, sl] = vb[r, p, :, sl]
            row = r - WIDE
            if row in (1, ROWS - 2):
                coarse = merge([[c0[r, k, p, :, sl] for p in range(PHASES)] for k in range(PLANES - 1)])
            for p in range(PHASES // 2):
                val = res[2 * p] + res[2 * p + 1]
                t1[row, p, :, sl] = val

                def product(k):
                    diag = diagonal([coarse[f][p] for f in range(FIELDS)])
                    return coarse[k][p] * jnp.where(diag > 0.0, DAMP / diag, 0.0) * val

                send_rows(t1_top, t1_bottom, row, p, sl, val, 1, product)
        sums[...] += jnp.where(j < tiles - 1, total, 0.0)

    each(tiles, rest)


def second_kernel(c1, c2, t1_own, above, below, t1, e1, t2, top, bottom, sums, va, vb):
    tiles = c1.shape[-1] // T

    def fill(j):
        sl = tile(j)
        gather_rows(t1, t1_own, above, below, j, 1)
        for r in range(1, EXT - 1):
            for p in range(2):
                va[r, p, :, sl] = c1[r, SWEEP_W, p, :, sl] * t1[r, p, :, sl]

    each(tiles, fill)
    smooth(c1, t1, va, vb, 1, EXT - 1, above.at[1], below.at[1])
    sums[...] = jnp.zeros_like(sums)

    def rest(j):
        sl = tile(j)
        total = jnp.zeros((8, T), F32)
        for r in range(WIDE, WIDE + ROWS):
            res = [t1[r, p, :, sl] - out for p, out in enumerate(apply_at(c1, r, vb, j))]
            total = total + res[0] * res[0] + res[1] * res[1]
            for p in range(2):
                e1[r - WIDE, p, :, sl] = vb[r, p, :, sl]
            val = res[0] + res[1]
            t2[r - WIDE, 0, :, sl] = val

            def product(k):
                return c2[r, k, 0, :, sl] * c2[r, SWEEP_W, 0, :, sl] * val

            send_rows(top, bottom, r - WIDE, 0, sl, val, WIDE, product)
        sums[...] += jnp.where(j < tiles - 1, total, 0.0)

    each(tiles, rest)


def third_kernel(ends, main, c1, far0, t2_own, above, below, e1_in, e1, top, bottom, t2, va, vb, far):
    tiles = main.shape[-1] // T
    sides = side_domain(ends)

    def build(i, sl, domain):
        def write(k, p, x):
            far[i, k, p, :, sl] = x

        build_levels(lambda k, p: far0[i, k, p, :, sl], [None, write], sl, domain)

    for i in range(2):
        each(tiles - 1, lambda j: build(i, tile(j), ends[i]))
        build(i, slice((tiles - 1) * T, tiles * T), sides * ends[i])
    c2 = WithFar(main, far)

    def fill(j):
        sl = tile(j)
        gather_rows(t2, t2_own, above, below, j, WIDE)
        for r in range(EXT):
            va[r, 0, :, sl] = c2[r, SWEEP_W, 0, :, sl] * t2[r, 0, :, sl]

    each(tiles, fill)
    smooth(c2, t2, va, vb, 0, EXT, above.at[WIDE], below.at[WIDE])
    smooth(c2, t2, vb, va, 1, EXT - 1)
    smooth(c2, t2, va, vb, WIDE, WIDE + ROWS)

    def last(j):
        sl = tile(j)
        for r in range(WIDE, WIDE + ROWS):
            for p in range(2):
                val = e1_in[r - WIDE, p, :, sl] + vb[r, 0, :, sl]
                e1[r - WIDE, p, :, sl] = val
                send_rows(top, bottom, r - WIDE, p, sl, val, 1, lambda k: c1[r, k, p, :, sl] * val)

    each(tiles, last)


def fourth_kernel(c1, main, t1, e1, above, below, v2, v, top, bottom, va, vb):
    tiles = c1.shape[-1] // T
    each(tiles, lambda j: gather_rows(va, e1, above, below, j, 1, c1))
    smooth(c1, t1, va, vb, 1, EXT - 1, above.at[1], below.at[1])
    smooth(c1, t1, vb, va, WIDE, WIDE + ROWS)

    def last(j):
        sl = tile(j)
        for r in range(ROWS):
            for p in range(PHASES):
                add = jnp.where(main[r, SWEEP_W, p, :, sl] != 0.0, va[r + WIDE, p // 2, :, sl], 0.0)
                val = v2[r, p, :, sl] + add
                v[r, p, :, sl] = val
                send_rows(top, bottom, r, p, sl, val, WIDE, lambda k: main[r, k, p, :, sl] * val)

    each(tiles, last)


def fifth_kernel(main, near, far, v, above, below, order, adjoint, residual, sums, va, vb, buf):
    tiles = main.shape[-1] // T
    c0 = FineRows(main, near, far)
    t0 = SourceOf(c0)
    each(tiles, lambda j: gather_rows(va, v, above, below, j, WIDE, c0))
    smooth(c0, t0, va, vb, 0, EXT, above.at[WIDE], below.at[WIDE])
    smooth(c0, t0, vb, va, 1, EXT - 1)
    sums[...] = jnp.zeros_like(sums)

    def rest(j):
        sl = tile(j)
        total = jnp.zeros((8, T), F32)
        for r in range(WIDE, WIDE + ROWS):
            for p, out in enumerate(apply_at(c0, r, va, j)):
                diff = t0[r, p, :, sl] - out
                res = jnp.where(c0[r, SWEEP_W, p, :, sl] != 0.0, diff, 0.0)
                total = total + res * res
                buf[p, pl.ds(r - WIDE, FIELDS, stride=ROWS), :] = va[r, p, 0:FIELDS, sl]
                buf[p, pl.ds(GRID + r - WIDE, FIELDS, stride=ROWS), :] = res[0:FIELDS]
        sums[...] += total
        x = jnp.concatenate([buf[p] for p in range(PHASES)], axis=1)
        y = reorder(x, order[...])
        cols = pl.ds(pl.multiple_of(j * BLOCK, BLOCK), BLOCK)
        adjoint[:, cols] = y[0:GRID]
        residual[:, cols] = y[GRID : 2 * GRID]

    each(tiles - 1, rest)


def call(kernel, outs, args, scratch=(), spaces=None, size=0, limit=LIMIT, out_spaces=None):
    spaces = spaces or {}
    return pl.pallas_call(
        kernel,
        out_shape=[jax.ShapeDtypeStruct(s, F32) if isinstance(s, tuple) else s for s in outs],
        in_specs=[pl.BlockSpec(memory_space=spaces.get(i, pltpu.VMEM)) for i in range(len(args))],
        out_specs=[pl.BlockSpec(memory_space=(out_spaces or {}).get(i, pltpu.VMEM)) for i in range(len(outs))],
        scratch_shapes=[pltpu.VMEM(s, F32) if isinstance(s, tuple) else s for s in scratch],
        compiler_params=pltpu.CompilerParams(vmem_limit_bytes=limit),
        cost_estimate=pl.CostEstimate(flops=0, bytes_accessed=size, transcendentals=0),
        name=kernel.__name__,
    )(*args)


def ring(x, axis, step):
    count = lax.axis_size(axis)
    return lax.ppermute(x, axis, [(i, (i + step) % count) for i in range(count)])


def total_over_devices(x):
    axes = ("hull", "blk")
    count = lax.axis_size(axes)
    sent = jnp.broadcast_to(jnp.pad(x, (0, T - x.size))[None], (count, T))
    return jnp.sum(lax.all_to_all(sent, axes, 0, 0, tiled=True), axis=0)[: x.size]


def on_device(source, jacobian, face_coef, active):
    columns = source.shape[2]
    quads = columns // PHASES
    wide = quads + T
    blocks = columns // BLOCK
    hull, blk = lax.axis_index("hull"), lax.axis_index("blk")
    ends = jnp.stack([hull > 0, hull < lax.axis_size("hull") - 1, blk > 0, blk < lax.axis_size("blk") - 1]).astype(F32)

    def cells(rows, phases):
        return (rows, phases, 8, wide)

    def coefs(rows, planes, phases):
        return (rows, planes, phases, 8, wide)

    flag = {0: pltpu.SMEM}
    inputs = [
        pltpu.with_memory_space_constraint(x, pltpu.HBM)
        for x in (
            jacobian.reshape(FIELDS, GRID, columns),
            face_coef.reshape(4, GRID, columns),
            source.reshape(GRID, columns),
            active,
        )
    ]
    in_hbm = {i: pltpu.HBM for i in range(len(inputs))}
    staged = [(RAW, columns), pltpu.VMEM((ROWS, columns), jnp.int32)]
    copies = pltpu.SemaphoreType.DMA((blocks, PLANES + 1))
    order = jax.ShapeDtypeStruct((BLOCK, BLOCK), BF16)
    order_side = jax.ShapeDtypeStruct((2 * T, BLOCK), BF16)
    sum_tile = (8, T)

    top, bottom, left, right = call(
        send_kernel,
        [(FINE + PLANES, 8, columns)] * 2 + [(PACK + ROWS, T)] * 2,
        inputs,
        [*staged, (RAW, T), copies],
        in_hbm,
        limit=12 * 2**20,
    )
    from_right = ring(left, "blk", -1)
    from_left = ring(right, "blk", 1)
    rows_below = ring(top, "hull", -1)
    rows_above = ring(bottom, "hull", 1)
    inner, own, side = call(
        own_kernel,
        [pltpu.HBM((ROWS, FINE, PHASES, 8, quads), F32), order, order_side],
        inputs,
        [
            *staged,
            (2, PHASES, RAW, T),
            (2, PHASES, ROWS, T),
            (2, ROWS, FINE, PHASES, 8, T),
            copies,
            pltpu.SemaphoreType.DMA((blocks,)),
        ],
        in_hbm,
        size=25 * 10**6,
        limit=16 * 2**20,
        out_spaces={0: pltpu.HBM},
    )
    inner = pltpu.with_memory_space_constraint(inner, pltpu.HBM)
    corner = (2, 2, PER_GROUP * 8, T)
    top, bottom = call(corner_kernel, [corner, corner], [from_right, from_left, side], spaces={2: pl.ANY})
    corner_below = ring(top, "hull", -1)
    corner_above = ring(bottom, "hull", 1)
    (main,) = call(
        side_kernel,
        [coefs(ROWS, FINE, 4)],
        [ends, from_right, from_left, inner, side],
        [(PHASES, RAW, T), (PHASES, ROWS, T), pltpu.SemaphoreType.DMA((ROWS,))],
        {0: pltpu.SMEM, 3: pltpu.HBM},
        size=9 * 10**6,
    )
    near, v2, t1, top, bottom, sum0 = call(
        first_kernel,
        [coefs(2, FINE, 4), cells(ROWS, 4), cells(ROWS, 2), cells(2, 2), cells(2, 2), sum_tile],
        [ends, main, rows_above, rows_below, corner_above, corner_below, own, side],
        [cells(EXT, 4), cells(EXT, 4), cells(2, 4)],
        flag,
    )
    below = ring(top, "hull", -1)
    above = ring(bottom, "hull", 1)
    far, natural = call(
        far_kernel,
        [coefs(2, FINE, 4), order],
        [ends, rows_above, rows_below, corner_above, corner_below, own, side],
        (),
        flag,
        size=8 * 10**6,
    )
    c1, c2 = call(levels_kernel, [coefs(EXT, PLANES, 2), coefs(EXT, PLANES, 1)], [ends, main, near], (), flag, size=10**7)
    t1, e1, t2, top, bottom, sum1 = call(
        second_kernel,
        [cells(EXT, 2), cells(ROWS, 2), cells(ROWS, 1), cells(3, 1), cells(3, 1), sum_tile],
        [c1, c2, t1, above, below],
        [cells(EXT, 2)] * 2,
    )
    below = ring(top, "hull", -1)
    above = ring(bottom, "hull", 1)
    e1, top, bottom = call(
        third_kernel,
        [cells(ROWS, 2), cells(2, 2), cells(2, 2)],
        [ends, c2, c1, far, t2, above, below, e1],
        [cells(EXT, 1)] * 3 + [coefs(2, PLANES, 1)],
        flag,
    )
    below = ring(top, "hull", -1)
    above = ring(bottom, "hull", 1)
    v, top, bottom = call(
        fourth_kernel, [cells(ROWS, 4), cells(3, 4), cells(3, 4)], [c1, main, t1, e1, above, below, v2], [cells(EXT, 2)] * 2
    )
    below = ring(top, "hull", -1)
    above = ring(bottom, "hull", 1)
    adjoint, residual, sum2 = call(
        fifth_kernel,
        [(GRID, columns), (GRID, columns), sum_tile],
        [main, near, far, v, above, below, natural],
        [cells(EXT, 4)] * 2 + [(PHASES, 2 * GRID, T)],
    )
    squares = jnp.stack([sum0, 2.0 * sum1, sum2])
    squares = total_over_devices(jnp.sum(squares[:, :FIELDS], axis=(1, 2)))
    count = source.size * lax.axis_size("hull") * lax.axis_size("blk")
    level_rms = jnp.sqrt(squares / float(count))
    return adjoint.reshape(source.shape), residual.reshape(source.shape), level_rms


def solution(mesh):
    return jax.shard_map(
        on_device,
        mesh=mesh,
        in_specs=(
            P(None, "hull", "blk"),
            P(None, None, "hull", "blk"),
            P(None, None, "hull", "blk"),
            P("hull", "blk"),
        ),
        out_specs=(P(None, "hull", "blk"), P(None, "hull", "blk"), P()),
        check_vma=False,
    )
```

time: 504 us -> 92.6 us (0.18); the launches traced: 495 us -> 92 us
  starting transfers between devices: 169 us -> 24.1 us
  waiting for transfers between devices: 103 us -> 6.21 us
  local copies, waits for them, and re-layouts: 72.3 us -> 0.86 us
  blocking collectives: 69.8 us -> 19 us
  other arithmetic: 51.1 us -> 0.74 us
  Pallas kernels: 0 us -> 40.2 us
  matrix products: 27.7 us -> 0 us
    ppermute x66 -> x14, starting transfers between devices: 169 us -> 24.1 us  [ring(): lax.ppermute(x, axis, [(i, (i + step) % count) for i in range(count)])]
    ppermute x66 -> x14, waiting for transfers between devices: 103 us -> 6.21 us  [ring(): lax.ppermute(x, axis, [(i, (i + step) % count) for i in range(count)])]
    psum x1 -> x0, blocking collectives: 69.8 us -> none  [record(): return lax.psum(local_sum, ('hull', 'blk'))]
    pallas_call x0 -> x11, Pallas kernels: none -> 40.2 us  [call(): pl.pallas_call(kernel, out_shape=[jax.ShapeDtypeStruct(s, F32) if isinsta...]
    dot_general x20 -> x0, matrix products: 27.7 us -> none  [the longest x18 25.5 us: pair_sum(): jnp.einsum('...kw,wh->...kh', blocks, pairing, precision=lax.Precision.HI...]
    unnamed x104 -> x4, local copies, waits for them, and re-layouts: 21.1 us -> 0.81 us
    all_to_all x0 -> x1, blocking collectives: none -> 19 us  [total_over_devices(): lax.all_to_all(sent, axes, 0, 0, tiled=True)]
    slice x41 -> x0, local copies, waits for them, and re-layouts: 13.6 us -> none  [the longest x13 5.32 us: with_halo(): lax.slice_in_dim(cells, cells.shape[dim] - width, cells.shape[dim], axis=...]
  transfers between devices with their start and end apart: 66 -> 14, of which waited for: 23 -> 3; matrix products, arithmetic and copies ran while one was open for 22% -> 0% of each run, Pallas kernels for 0% -> 20%
where the time goes in v2:
time: 92.6 us; the launch traced here: 92 us
  Pallas kernels  40.2 us (43%)
  starting transfers between devices  24.1 us (26%)
  blocking collectives  19 us (21%)
  waiting for transfers between devices  6.21 us (7%)
    pallas_call x11, Pallas kernels, call(): pl.pallas_call(kernel, out_shape=[jax.ShapeDtypeStruct(s, F32) if isinsta...  40.2 us
    ppermute x14, starting transfers between devices, ring(): lax.ppermute(x, axis, [(i, (i + step) % count) for i in range(count)])  24.1 us
    all_to_all x1, blocking collectives, total_over_devices(): lax.all_to_all(sent, axes, 0, 0, tiled=True)  19 us
    ppermute x14, waiting for transfers between devices, ring(): lax.ppermute(x, axis, [(i, (i + step) % count) for i in range(count)])  6.21 us
  transfers between devices with their start and end apart: 14, of which 3 were waited for; matrix products, arithmetic and copies ran while one was open for 0% of the time, Pallas kernels for 20%

profile of v2, /device:TPU:0, one launch (start us, length us, event | category | flops | bytes accessed | tf_op | source)
XLA Modules:
  0.0 92.0 jit_solution(7130937130747194735)
XLA Ops:
  0.6 5.4 %send_kernel.1 = (f32[25,8,2048]{2,1,0:T(8,128)}, f32[25,8,2048]{2,1,0:T(8,128)}, f32[176,128]{1,0:T(8,128)}, f32[176,128]{1,0:T(8,128)}) custom-call(f32[7,56,2048]{2,1,0:T(8,128)} %bitcast.16, f32[4,56,2048]{2,1,0:T(8,128)} %bitcast.18, f32[56,2048]{1,0:T(8,128)} %bitcast.20, s32[8,2048]{1,0:T(8,128)} %act.3), custom_call_target="tpu_custom_call" | custom-call | tf_op jit(solution)/shard_map/send_kernel/pallas_call | solution.py:637
  6.1 0.0 collective-permute-start.2
  6.1 2.9 %collective-permute-start.3 = (f32[25,8,2048]{2,1,0:T(8,128)}, f32[25,8,2048]{2,1,0:T(8,128)S(1)}, u32[]{:S(2)}, u32[]{:S(2)}) collective-permute-start(f32[25,8,2048]{2,1,0:T(8,128)} %get-tuple-element.42), channel_id=1, source_target_pairs={{0,112},{16,0},{32,16},{48,32},{64,48},{80,64},{96,80},{112,96},{1... | collective-permute-start | bytes 4915208 | tf_op jit(solution)/shard_map/ppermute | solution.py:651
  9.0 6.3 %collective-permute-start = (f32[176,128]{1,0:T(8,128)}, f32[176,128]{1,0:T(8,128)}, u32[]{:S(2)}, u32[]{:S(2)}) collective-permute-start(f32[176,128]{1,0:T(8,128)} %get-tuple-element.37), channel_id=1, source_target_pairs={{0,15},{1,0},{2,1},{3,2},{4,3},{5,4},{6,5},{7,6},{8,7},{9,8},{10,9... | collective-permute-start | bytes 270344 | tf_op jit(solution)/shard_map/ppermute | solution.py:651
  15.3 0.0 collective-permute-start.1
  15.3 8.4 %own_kernel.1 = (f32[8,13,4,8,512]{4,3,2,1,0:T(8,128)}, bf16[512,512]{1,0:T(8,128)(2,1)S(1)}, bf16[256,512]{1,0:T(8,128)(2,1)S(1)}) custom-call(f32[7,56,2048]{2,1,0:T(8,128)} %bitcast.17, f32[4,56,2048]{2,1,0:T(8,128)} %bitcast.19, f32[56,2048]{1,0:T(8,128)} %bitcast.21, s32[8,2048]{1,0:T(8,128)} %act.3), custom_call_target="tpu_custom_call" | custom-call | bytes 25000000 | tf_op jit(solution)/shard_map/own_kernel/pallas_call | solution.py:637
  23.8 0.0 copy-start
  23.8 0.8 copy-done
  24.6 0.0 collective-permute-done.from_right
  24.6 0.0 collective-permute-done.1.from_left
  24.6 1.0 %corner_kernel.1 = (f32[2,2,24,128]{3,2,1,0:T(8,128)S(1)}, f32[2,2,24,128]{3,2,1,0:T(8,128)S(1)}) custom-call(f32[176,128]{1,0:T(8,128)} %collective-permute-done.from_right, f32[176,128]{1,0:T(8,128)} %collective-permute-done.1.from_left, bf16[256,512]{1,0:T(8,128)(2,1)S(1)} %get-tuple-element.40.order.order_side), custom_call_target="tpu_custom_call" | custom-call | tf_op jit(solution)/shard_map/corner_kernel/pallas_call | solution.py:637
  25.5 0.0 collective-permute-start.4
  25.6 2.9 %collective-permute-start.5 = (f32[2,2,24,128]{3,2,1,0:T(8,128)S(1)}, f32[2,2,24,128]{3,2,1,0:T(8,128)S(1)}, u32[]{:S(2)}, u32[]{:S(2)}) collective-permute-start(f32[2,2,24,128]{3,2,1,0:T(8,128)S(1)} %get-tuple-element.44), channel_id=1, source_target_pairs={{0,112},{16,0},{32,16},{48,32},{64,48},{80,64},{96,80},{112,96},{1... | collective-permute-start | bytes 147464 | tf_op jit(solution)/shard_map/ppermute | solution.py:651
  28.5 0.1 add_convert_fusion.ends
  28.6 0.0 copy-start.1
  28.6 4.1 %side_kernel.1.main = f32[8,13,4,8,640]{4,3,2,1,0:T(8,128)S(1)} custom-call(f32[4]{0:T(128)S(1)} %add_convert_fusion.ends, f32[176,128]{1,0:T(8,128)} %collective-permute-done.from_right, f32[176,128]{1,0:T(8,128)} %collective-permute-done.1.from_left, f32[8,13,4,8,512]{4,3,2,1,0:T(8,128)} %get-tuple-element.39.own, ...), custom_call_target="tpu_custom_call" | custom-call | bytes 9000000 | tf_op jit(solution)/shard_map/side_kernel/pallas_call | solution.py:637
  32.7 0.0 collective-permute-done.4.corner_above
  32.7 0.0 collective-permute-done.5.corner_below
  32.7 0.0 collective-permute-done.2.rows_above
  32.7 0.0 collective-permute-done.3.rows_below
  32.7 0.0 copy-done.1
  32.8 5.2 %first_kernel.1 = (f32[2,13,4,8,640]{4,3,2,1,0:T(8,128)S(1)}, f32[8,4,8,640]{3,2,1,0:T(8,128)S(1)}, f32[8,2,8,640]{3,2,1,0:T(8,128)S(1)}, f32[2,2,8,640]{3,2,1,0...) custom-call(f32[4]{0:T(128)S(1)} %add_convert_fusion.ends, f32[8,13,4,8,640]{4,3,2,1,0:T(8,128)S(1)} %side_kernel.1.main, ...), custom_call_target="tpu_custom_call" | custom-call | tf_op jit(solution)/shard_map/first_kernel/pallas_call | solution.py:637
  38.0 0.0 collective-permute-start.6
  38.0 2.9 %collective-permute-start.7 = (f32[2,2,8,640]{3,2,1,0:T(8,128)S(1)}, f32[2,2,8,640]{3,2,1,0:T(8,128)S(1)}, u32[]{:S(2)}, u32[]{:S(2)}) collective-permute-start(f32[2,2,8,640]{3,2,1,0:T(8,128)S(1)} %get-tuple-element.52), channel_id=1, source_target_pairs={{0,112},{16,0},{32,16},{48,32},{64,48},{80,64},{96,80},{112,96},{1... | collective-permute-start | bytes 245768 | tf_op jit(solution)/shard_map/ppermute | solution.py:651
  40.9 1.9 %levels_kernel.1 = (f32[12,12,2,8,640]{4,3,2,1,0:T(8,128)S(1)}, f32[12,12,1,8,640]{4,3,2,1,0:T(8,128)S(1)}) custom-call(f32[4]{0:T(128)S(1)} %add_convert_fusion.ends, f32[8,13,4,8,640]{4,3,2,1,0:T(8,128)S(1)} %side_kernel.1.main, f32[2,13,4,8,640]{4,3,2,1,0:T(8,128)S(1)} %get-tuple-element.46.near), custom_call_target="tpu_custom_call" | custom-call | bytes 10000000 | tf_op jit(solution)/shard_map/levels_kernel/pallas_call | solution.py:637
  42.9 0.2 collective-permute-done.6.above
  43.1 0.0 collective-permute-done.7.below
  43.1 1.4 %second_kernel.1 = (f32[12,2,8,640]{3,2,1,0:T(8,128)S(1)}, f32[8,2,8,640]{3,2,1,0:T(8,128)S(1)}, f32[8,1,8,640]{3,2,1,0:T(8,128)S(1)}, f32[3,1,8,640]{3,2,1,0:T(...) custom-call(f32[12,12,2,8,640]{4,3,2,1,0:T(8,128)S(1)} %get-tuple-element.48.c1, ...), custom_call_target="tpu_custom_call" | custom-call | tf_op jit(solution)/shard_map/second_kernel/pallas_call | solution.py:637
  44.5 0.0 collective-permute-start.8
  44.5 3.0 %collective-permute-start.9 = (f32[3,1,8,640]{3,2,1,0:T(8,128)S(1)}, f32[3,1,8,640]{3,2,1,0:T(8,128)S(1)}, u32[]{:S(2)}, u32[]{:S(2)}) collective-permute-start(f32[3,1,8,640]{3,2,1,0:T(8,128)S(1)} %get-tuple-element.56), channel_id=1, source_target_pairs={{0,112},{16,0},{32,16},{48,32},{64,48},{80,64},{96,80},{112,96},{1... | collective-permute-start | bytes 184328 | tf_op jit(solution)/shard_map/ppermute | solution.py:651
  47.5 3.1 %far_kernel.1 = (f32[2,13,4,8,640]{4,3,2,1,0:T(8,128)S(1)}, bf16[512,512]{1,0:T(8,128)(2,1)S(1)}) custom-call(f32[4]{0:T(128)S(1)} %add_convert_fusion.ends, f32[25,8,2048]{2,1,0:T(8,128)S(1)} %collective-permute-done.2.rows_above, f32[25,8,2048]{2,1,0:T(8,128)S(1)} %collective-permute-done.3.rows_below, ...), custom_call_target="tpu_custom_call" | custom-call | bytes 8000000 | tf_op jit(solution)/shard_map/far_kernel/pallas_call | solution.py:637
  50.6 0.0 collective-permute-done.8.above
  50.6 0.0 collective-permute-done.9.below
  50.6 2.6 %third_kernel.1 = (f32[8,2,8,640]{3,2,1,0:T(8,128)S(1)}, f32[2,2,8,640]{3,2,1,0:T(8,128)S(1)}, f32[2,2,8,640]{3,2,1,0:T(8,128)S(1)}) custom-call(f32[4]{0:T(128)S(1)} %add_convert_fusion.ends, f32[12,12,1,8,640]{4,3,2,1,0:T(8,128)S(1)} %get-tuple-element.49.c2.main, f32[12,12,2,8,640]{4,3,2,1,0:T(8,128)S(1)} %get-tuple-element.48.c1, ...), custom_call_target="tpu_custom_call" | custom-call | tf_op jit(solution)/shard_map/third_kernel/pallas_call | solution.py:637
  53.3 0.0 collective-permute-start.10
  53.3 2.9 %collective-permute-start.11 = (f32[2,2,8,640]{3,2,1,0:T(8,128)S(1)}, f32[2,2,8,640]{3,2,1,0:T(8,128)S(1)}, u32[]{:S(2)}, u32[]{:S(2)}) collective-permute-start(f32[2,2,8,640]{3,2,1,0:T(8,128)S(1)} %get-tuple-element.60), channel_id=1, source_target_pairs={{0,112},{16,0},{32,16},{48,32},{64,48},{80,64},{96,80},{112,96},{1... | collective-permute-start | bytes 245768 | tf_op jit(solution)/shard_map/ppermute | solution.py:651
  56.2 2.1 %collective-permute-done.10.above = f32[2,2,8,640]{3,2,1,0:T(8,128)S(1)} collective-permute-done((f32[2,2,8,640]{3,2,1,0:T(8,128)S(1)}, f32[2,2,8,640]{3,2,1,0:T(8,128)S(1)}, u32[]{:S(2)}, u32[]{:S(2)}) %collective-permute-start.10) | collective-permute-done | bytes 81952 | tf_op jit(solution)/shard_map/ppermute | solution.py:651
  58.3 0.0 collective-permute-done.11.below
  58.3 1.5 %fourth_kernel.1 = (f32[8,4,8,640]{3,2,1,0:T(8,128)S(1)}, f32[3,4,8,640]{3,2,1,0:T(8,128)S(1)}, f32[3,4,8,640]{3,2,1,0:T(8,128)S(1)}) custom-call(f32[12,12,2,8,640]{4,3,2,1,0:T(8,128)S(1)} %get-tuple-element.48.c1, f32[8,13,4,8,640]{4,3,2,1,0:T(8,128)S(1)} %side_kernel.1.main, f32[12,2,8,640]{3,2,1,0:T(8,128)S(1)} %get-tuple-element.53.t1, ...), custom_call_target="tpu_custom_call" | custom-call | tf_op jit(solution)/shard_map/fourth_kernel/pallas_call | solution.py:637
  59.8 0.0 collective-permute-start.12
  59.9 3.0 %collective-permute-start.13 = (f32[3,4,8,640]{3,2,1,0:T(8,128)S(1)}, f32[3,4,8,640]{3,2,1,0:T(8,128)S(1)}, u32[]{:S(2)}, u32[]{:S(2)}) collective-permute-start(f32[3,4,8,640]{3,2,1,0:T(8,128)S(1)} %get-tuple-element.64), channel_id=1, source_target_pairs={{0,112},{16,0},{32,16},{48,32},{64,48},{80,64},{96,80},{112,96},{1... | collective-permute-start | bytes 737288 | tf_op jit(solution)/shard_map/ppermute | solution.py:651
  62.8 3.9 %collective-permute-done.12.above = f32[3,4,8,640]{3,2,1,0:T(8,128)S(1)} collective-permute-done((f32[3,4,8,640]{3,2,1,0:T(8,128)S(1)}, f32[3,4,8,640]{3,2,1,0:T(8,128)S(1)}, u32[]{:S(2)}, u32[]{:S(2)}) %collective-permute-start.12) | collective-permute-done | bytes 245792 | tf_op jit(solution)/shard_map/ppermute | solution.py:651
  66.7 0.0 collective-permute-done.13.below
  66.7 5.6 %fifth_kernel.1 = (f32[56,2048]{1,0:T(8,128)}, f32[56,2048]{1,0:T(8,128)}, f32[8,128]{1,0:T(8,128)S(1)}) custom-call(f32[8,13,4,8,640]{4,3,2,1,0:T(8,128)S(1)} %side_kernel.1.main, f32[2,13,4,8,640]{4,3,2,1,0:T(8,128)S(1)} %get-tuple-element.46.near, f32[2,13,4,8,640]{4,3,2,1,0:T(8,128)S(1)} %get-tuple-element.47.far0.far, ...), custom_call_target="tpu_custom_call" | custom-call | tf_op jit(solution)/shard_map/fifth_kernel/pallas_call | solution.py:637
  72.3 0.1 fusion
  72.4 19.0 %all_to_all.6 = f32[128,1,128]{2,1,0:T(1,128)S(1)} all-to-all(f32[128,1,128]{2,1,0:T(1,128)S(1)} %broadcast_in_dim.2), channel_id=1, replica_groups=mesh['hull'=8,'blk'=16] {'hull','blk'}, dimensions={0} | all-to-all | bytes 131072 | tf_op jit(solution)/shard_map/all_to_all | solution.py:658
  91.4 0.5 multiply_sqrt_fusion
  (4 shorter events, 0.1 us)
Async XLA Ops:
  6.1 26.7 %collective-permute-start.2 = (f32[25,8,2048]{2,1,0:T(8,128)}, f32[25,8,2048]{2,1,0:T(8,128)S(1)}, u32[]{:S(2)}, u32[]{:S(2)}) collective-permute-start(f32[25,8,2048]{2,1,0:T(8,128)} %get-tuple-element.41), channel_id=1, source_target_pairs={{0,16},{16,32},{32,48},{48,64},{64,80},{80,96},{96,112},{112,0},{1... | collective-permute-start | bytes 4915208 | tf_op jit(solution)/shard_map/ppermute | solution.py:651
  6.1 26.7 %collective-permute-start.3 = (f32[25,8,2048]{2,1,0:T(8,128)}, f32[25,8,2048]{2,1,0:T(8,128)S(1)}, u32[]{:S(2)}, u32[]{:S(2)}) collective-permute-start(f32[25,8,2048]{2,1,0:T(8,128)} %get-tuple-element.42), channel_id=1, source_target_pairs={{0,112},{16,0},{32,16},{48,32},{64,48},{80,64},{96,80},{112,96},{1... | collective-permute-start | bytes 4915208 | tf_op jit(solution)/shard_map/ppermute | solution.py:651
  9.0 15.5 %collective-permute-start = (f32[176,128]{1,0:T(8,128)}, f32[176,128]{1,0:T(8,128)}, u32[]{:S(2)}, u32[]{:S(2)}) collective-permute-start(f32[176,128]{1,0:T(8,128)} %get-tuple-element.37), channel_id=1, source_target_pairs={{0,15},{1,0},{2,1},{3,2},{4,3},{5,4},{6,5},{7,6},{8,7},{9,8},{10,9... | collective-permute-start | bytes 270344 | tf_op jit(solution)/shard_map/ppermute | solution.py:651
  15.3 9.2 %collective-permute-start.1 = (f32[176,128]{1,0:T(8,128)}, f32[176,128]{1,0:T(8,128)}, u32[]{:S(2)}, u32[]{:S(2)}) collective-permute-start(f32[176,128]{1,0:T(8,128)} %get-tuple-element.38), channel_id=1, source_target_pairs={{0,1},{1,2},{2,3},{3,4},{4,5},{5,6},{6,7},{7,8},{8,9},{9,10},{10,1... | collective-permute-start | bytes 270344 | tf_op jit(solution)/shard_map/ppermute | solution.py:651
  23.8 0.8 copy-start
  25.5 7.2 %collective-permute-start.4 = (f32[2,2,24,128]{3,2,1,0:T(8,128)S(1)}, f32[2,2,24,128]{3,2,1,0:T(8,128)S(1)}, u32[]{:S(2)}, u32[]{:S(2)}) collective-permute-start(f32[2,2,24,128]{3,2,1,0:T(8,128)S(1)} %get-tuple-element.43), channel_id=1, source_target_pairs={{0,16},{16,32},{32,48},{48,64},{64,80},{80,96},{96,112},{112,0},{1... | collective-permute-start | bytes 147464 | tf_op jit(solution)/shard_map/ppermute | solution.py:651
  25.6 7.2 %collective-permute-start.5 = (f32[2,2,24,128]{3,2,1,0:T(8,128)S(1)}, f32[2,2,24,128]{3,2,1,0:T(8,128)S(1)}, u32[]{:S(2)}, u32[]{:S(2)}) collective-permute-start(f32[2,2,24,128]{3,2,1,0:T(8,128)S(1)} %get-tuple-element.44), channel_id=1, source_target_pairs={{0,112},{16,0},{32,16},{48,32},{64,48},{80,64},{96,80},{112,96},{1... | collective-permute-start | bytes 147464 | tf_op jit(solution)/shard_map/ppermute | solution.py:651
  28.6 4.2 %copy-start.1 = (bf16[512,512]{1,0:T(8,128)(2,1)S(1)}, bf16[512,512]{1,0:T(8,128)(2,1)}, u32[]{:S(2)}) copy-start(bf16[512,512]{1,0:T(8,128)(2,1)} %copy-done) | copy-start | bytes 1572868
  38.0 5.1 %collective-permute-start.6 = (f32[2,2,8,640]{3,2,1,0:T(8,128)S(1)}, f32[2,2,8,640]{3,2,1,0:T(8,128)S(1)}, u32[]{:S(2)}, u32[]{:S(2)}) collective-permute-start(f32[2,2,8,640]{3,2,1,0:T(8,128)S(1)} %get-tuple-element.51), channel_id=1, source_target_pairs={{0,16},{16,32},{32,48},{48,64},{64,80},{80,96},{96,112},{112,0},{1... | collective-permute-start | bytes 245768 | tf_op jit(solution)/shard_map/ppermute | solution.py:651
  38.0 5.1 %collective-permute-start.7 = (f32[2,2,8,640]{3,2,1,0:T(8,128)S(1)}, f32[2,2,8,640]{3,2,1,0:T(8,128)S(1)}, u32[]{:S(2)}, u32[]{:S(2)}) collective-permute-start(f32[2,2,8,640]{3,2,1,0:T(8,128)S(1)} %get-tuple-element.52), channel_id=1, source_target_pairs={{0,112},{16,0},{32,16},{48,32},{64,48},{80,64},{96,80},{112,96},{1... | collective-permute-start | bytes 245768 | tf_op jit(solution)/shard_map/ppermute | solution.py:651
  44.5 6.1 %collective-permute-start.8 = (f32[3,1,8,640]{3,2,1,0:T(8,128)S(1)}, f32[3,1,8,640]{3,2,1,0:T(8,128)S(1)}, u32[]{:S(2)}, u32[]{:S(2)}) collective-permute-start(f32[3,1,8,640]{3,2,1,0:T(8,128)S(1)} %get-tuple-element.55), channel_id=1, source_target_pairs={{0,16},{16,32},{32,48},{48,64},{64,80},{80,96},{96,112},{112,0},{1... | collective-permute-start | bytes 184328 | tf_op jit(solution)/shard_map/ppermute | solution.py:651
  44.5 6.1 %collective-permute-start.9 = (f32[3,1,8,640]{3,2,1,0:T(8,128)S(1)}, f32[3,1,8,640]{3,2,1,0:T(8,128)S(1)}, u32[]{:S(2)}, u32[]{:S(2)}) collective-permute-start(f32[3,1,8,640]{3,2,1,0:T(8,128)S(1)} %get-tuple-element.56), channel_id=1, source_target_pairs={{0,112},{16,0},{32,16},{48,32},{64,48},{80,64},{96,80},{112,96},{1... | collective-permute-start | bytes 184328 | tf_op jit(solution)/shard_map/ppermute | solution.py:651
  53.3 5.1 %collective-permute-start.10 = (f32[2,2,8,640]{3,2,1,0:T(8,128)S(1)}, f32[2,2,8,640]{3,2,1,0:T(8,128)S(1)}, u32[]{:S(2)}, u32[]{:S(2)}) collective-permute-start(f32[2,2,8,640]{3,2,1,0:T(8,128)S(1)} %get-tuple-element.59), channel_id=1, source_target_pairs={{0,16},{16,32},{32,48},{48,64},{64,80},{80,96},{96,112},{112,0},{1... | collective-permute-start | bytes 245768 | tf_op jit(solution)/shard_map/ppermute | solution.py:651
  53.3 5.1 %collective-permute-start.11 = (f32[2,2,8,640]{3,2,1,0:T(8,128)S(1)}, f32[2,2,8,640]{3,2,1,0:T(8,128)S(1)}, u32[]{:S(2)}, u32[]{:S(2)}) collective-permute-start(f32[2,2,8,640]{3,2,1,0:T(8,128)S(1)} %get-tuple-element.60), channel_id=1, source_target_pairs={{0,112},{16,0},{32,16},{48,32},{64,48},{80,64},{96,80},{112,96},{1... | collective-permute-start | bytes 245768 | tf_op jit(solution)/shard_map/ppermute | solution.py:651
  59.8 6.8 %collective-permute-start.12 = (f32[3,4,8,640]{3,2,1,0:T(8,128)S(1)}, f32[3,4,8,640]{3,2,1,0:T(8,128)S(1)}, u32[]{:S(2)}, u32[]{:S(2)}) collective-permute-start(f32[3,4,8,640]{3,2,1,0:T(8,128)S(1)} %get-tuple-element.63), channel_id=1, source_target_pairs={{0,16},{16,32},{32,48},{48,64},{64,80},{80,96},{96,112},{112,0},{1... | collective-permute-start | bytes 737288 | tf_op jit(solution)/shard_map/ppermute | solution.py:651
  59.9 6.8 %collective-permute-start.13 = (f32[3,4,8,640]{3,2,1,0:T(8,128)S(1)}, f32[3,4,8,640]{3,2,1,0:T(8,128)S(1)}, u32[]{:S(2)}, u32[]{:S(2)}) collective-permute-start(f32[3,4,8,640]{3,2,1,0:T(8,128)S(1)} %get-tuple-element.64), channel_id=1, source_target_pairs={{0,112},{16,0},{32,16},{48,32},{64,48},{80,64},{96,80},{112,96},{1... | collective-permute-start | bytes 737288 | tf_op jit(solution)/shard_map/ppermute | solution.py:651

commit v3 on v2

--- a/solution.py
+++ b/solution.py
@@ -19,9 +19,10 @@
 SWEEP_W = 11
 SOURCE = 12
 FINE = 13
+SENT = 22
 F32 = jnp.float32
 BF16 = jnp.bfloat16
-LIMIT = 8 * 2**20
+LIMIT = 12 * 2**20
 GRID = FIELDS * ROWS
 RAW = PLANES * GRID
 GROUPS = T // SIDE_COLS
@@ -123,6 +124,14 @@
     return [jnp.where(sub == f, x + total, x) for f, x in enumerate(planes)]
 
 
+def last_sublanes(planes):
+    sub = iota(planes[0].shape, 0)
+    out = planes[FIELDS - 1][FIELDS:8]
+    for f in range(FIELDS - 1):
+        out = jnp.where(sub == f, planes[f][FIELDS:8], out)
+    return out
+
+
 def weight_of(planes, mask):
     return jnp.where(mask > 0.0, DAMP / diagonal(planes), 0.0)
 
@@ -153,10 +162,11 @@
     return [waiter(group) for group in todo]
 
 
-def send_kernel(jac, face, src, act, top, bottom, left, right, raw, flags, buf, sems):
+def send_kernel(jac, face, src, act, top, bottom, left, right, raw, flags, buf, stage, sems, out_sems):
     columns = src.shape[-1]
     waits = fetch(jac, face, src, act, raw, flags, sems, BLOCK)
     per = BLOCK // T
+    jobs = ((0, 0, 1, 3), (1, ROWS - 1, ROWS - 2, 2))
 
     def rows_of(b):
         def body(i):
@@ -164,26 +174,35 @@
             for k in range(PLANES):
                 buf[k * GRID : k * GRID + GRID] = raw[k * GRID : k * GRID + GRID, sl]
 
-            def pick(k, r):
-                return buf[pl.ds(k * GRID + r, FIELDS, stride=ROWS), :]
-
-            for out, near, far, face_k in ((top, 0, 1, 3), (bottom, ROWS - 1, ROWS - 2, 2)):
-                for k in range(PLANES):
-                    out[k, 0:FIELDS, sl] = pick(k, near)
-                out[PLANES - 1, FIELDS : FIELDS + 1, sl] = flags[near : near + 1, sl].astype(F32)
-                planes = [pick(k, far) for k in range(PLANES)]
-                mask = flags[far : far + 1, sl].astype(F32)
-                weight = weight_of(with_face_sum(planes[:FIELDS], planes[FIELDS : FIELDS + 4]), mask)
-                out[PLANES, 0:FIELDS, sl] = planes[FIELDS + face_k] * weight * planes[PLANES - 1]
-                for k in range(PLANES):
-                    out[FINE + k, 0:FIELDS, sl] = planes[k]
-                out[FINE + PLANES - 1, FIELDS : FIELDS + 1, sl] = mask
+            def row(r):
+                planes = [buf[pl.ds(k * GRID + r, FIELDS, stride=ROWS), :] for k in range(PLANES)]
+                faces = planes[FIELDS : FIELDS + 4]
+                return with_face_sum(planes[:FIELDS], faces), faces, planes[PLANES - 1], flags[r : r + 1, sl].astype(F32)
+
+            for out, near, far, face_k in jobs:
+                planes, faces, source, mask = row(near)
+                for k, x in enumerate(planes + faces + [source]):
+                    stage[out, k, 0:FIELDS, sl] = x
+                stage[out, PLANES - 1, FIELDS:8, sl] = mask
+                planes, faces, source, mask = row(far)
+                product = faces[face_k] * weight_of(planes, mask) * source
+                for k, x in enumerate(planes + [faces[0], faces[1], faces[face_k]]):
+                    stage[out, PLANES + k, 0:FIELDS, sl] = x
+                for g in range(FIELDS):
+                    stage[out, g, FIELDS:8, sl] = product[g : g + 1]
+                    stage[out, PLANES + g, FIELDS:8, sl] = source[g : g + 1]
+                stage[out, PLANES + FIELDS, FIELDS:8, sl] = mask
 
         each(per, body)
 
+    copies = []
     for b, wait in enumerate(waits):
         wait()
         rows_of(b)
+        cols = pl.ds(b * BLOCK, BLOCK)
+        for i, out in enumerate((top, bottom)):
+            copies.append(pltpu.make_async_copy(stage.at[i, :, :, cols], out.at[:, :, cols], out_sems.at[b, i]))
+            copies[-1].start()
     lane = iota((PACK, T), 1) // SIDE_COLS
     for out, at, move in ((left, 0, 0), (right, columns - T, SIDE_COLS)):
         packed = None
@@ -195,6 +214,8 @@
         out[0:PACK] = packed
         mask = flags[:, at : at + T].astype(F32)
         out[PACK : PACK + ROWS] = pltpu.roll(mask, move, 1) if move else mask
+    for copy in copies:
+        copy.wait()
 
 
 def place(buf, masks, out, sl, domain):
@@ -217,7 +238,7 @@
     return jnp.where(lane < SIDE, ends[3], jnp.where(lane >= T - SIDE, ends[2], 0.0))
 
 
-def corner_kernel(from_right, from_left, order_side, top, bottom):
+def corner_kernel(from_right, from_left, token, top, bottom):
     for side, packed in enumerate((from_right, from_left)):
         for out, rows in ((top, (0, 1)), (bottom, (ROWS - 1, ROWS - 2))):
             for i, r in enumerate(rows):
@@ -230,7 +251,8 @@
     parts = [jnp.concatenate([c[i, 0], c[i, 1]], axis=1) for c in corners for i in range(2)]
     both = jnp.concatenate(parts, axis=0)
     size = PER_GROUP * 8
-    packs = [reorder(group_of(both, g), order) for g in range(GROUPS)]
+    every = reorder(jnp.concatenate([group_of(both, g) for g in range(GROUPS)], axis=0), order)
+    packs = [every[g * both.shape[0] : (g + 1) * both.shape[0]] for g in range(GROUPS)]
     result = []
     for n in range(len(parts)):
         def plane(k, p):
@@ -243,14 +265,17 @@
     return result
 
 
-def side_kernel(ends, from_right, from_left, own, order, main, buf, masks, sems):
+def side_kernel(ends, from_right, from_left, own, main, order_own, order, buf, masks, sems):
     inner = own.shape[-1]
     copies = [pltpu.make_async_copy(own.at[r], main.at[r, :, :, :, pl.ds(0, inner)], sems.at[r]) for r in range(ROWS)]
     for copy in copies:
         copy.start()
+    order[...] = side_order()
+    order_own[...] = own_order()
     both = jnp.concatenate([from_right[...], from_left[...]], axis=1)
+    every = reorder(jnp.concatenate([group_of(both, g) for g in range(GROUPS)], axis=0), order[...])
     for g in range(GROUPS):
-        x = reorder(group_of(both, g), order[...])
+        x = every[g * (PACK + ROWS) : (g + 1) * (PACK + ROWS)]
         for p in range(PHASES):
             buf[p, g * PACK : g * PACK + PACK] = x[0:PACK, p * T : p * T + T]
             if g == 0:
@@ -260,16 +285,15 @@
         copy.wait()
 
 
-def own_kernel(jac, face, src, act, own, order, order_side, raw, flags, buf, masks, stage, sems, out_sems):
-    waits = fetch(jac, face, src, act, raw, flags, sems, BLOCK)
+def own_kernel(jac, face, src, act, own, token, order, buf, masks, stage, out_sems):
     order[...] = own_order()
-    order_side[...] = side_order()
+    token[...] = jnp.zeros_like(token)
     outs = []
-    for b, wait in enumerate(waits):
-        wait()
+    for b in range(src.shape[-1] // BLOCK):
         cols = slice(b * BLOCK, b * BLOCK + BLOCK)
-        x = reorder(raw[:, cols], order[...])
-        m = jnp.dot(flags[:, cols].astype(F32).astype(BF16), order[...], preferred_element_type=F32)
+        parts = [jac[f, :, cols] for f in range(FIELDS)] + [face[k, :, cols] for k in range(4)] + [src[:, cols]]
+        x = reorder(jnp.concatenate(parts, axis=0), order[...])
+        m = jnp.dot(act[:, cols].astype(F32).astype(BF16), order[...], preferred_element_type=F32)
         for p in range(PHASES):
             buf[b % 2, p] = x[:, p * T : p * T + T]
             masks[b % 2, p] = m[:, p * T : p * T + T]
@@ -344,31 +368,62 @@
         build(near, i, r, sl, sides * row_flag(ends, r))
 
 
-def far_kernel(ends, rows_above, rows_below, corner_above, corner_below, order, order_side, far, order_out):
-    order_out[...] = natural_order()
-    wide = far.shape[-1]
-
-    def put(i, p, planes, mask, sl):
-        faces = planes[FIELDS : FIELDS + 4]
-        jac = with_face_sum(planes[:FIELDS], faces)
-        for k, x in enumerate(jac + faces + [weight_of(jac, mask), planes[PLANES - 1]]):
-            far[i, k, p, :, sl] = x
-
+def far_planes(ends, rows, corners, wide, put):
     def fill(j):
-        cols = pl.ds(pl.multiple_of(j * BLOCK, BLOCK), BLOCK)
-        for i, rows in enumerate((rows_above, rows_below)):
-            x = reorder(rows[FINE : FINE + PLANES, :, cols].reshape(PLANES * 8, BLOCK), order[...])
+        for i in range(2):
+            cells = []
             for p in range(PHASES):
-                planes = [x[k * 8 : k * 8 + 8, p * T : p * T + T] for k in range(PLANES)]
-                put(i, p, planes, planes[PLANES - 1][FIELDS : FIELDS + 1] * ends[i], tile(j))
+                planes = [rows[i, j, k * 8 : k * 8 + 8, p * T : p * T + T] for k in range(SENT - PLANES)]
+                mask = planes[FIELDS][FIELDS:8] * ends[i]
+                cells.append((planes[:FIELDS], planes[FIELDS:], planes, mask))
+            put(i, cells, tile(j), ends[i])
 
     each(wide // T - 1, fill)
-    corners = corner_planes((corner_above, corner_below), order_side[...])
     for i in range(2):
         domain = side_domain(ends) * ends[i]
         planes, masks = corners[2 * i + 1]
+        cells = []
         for p in range(PHASES):
-            put(i, p, [x[p] for x in planes], jnp.where(domain > 0.0, masks[p], 0.0), slice(wide - T, wide))
+            raw = [x[p] for x in planes]
+            faces = raw[FIELDS : FIELDS + 4]
+            mask = jnp.where(domain > 0.0, masks[p], 0.0)
+            cells.append((with_face_sum(raw[:FIELDS], faces), [faces[0], faces[1], faces[2 + i]], raw[PLANES - 1], mask))
+        put(i, cells, slice(wide - T, wide), domain)
+
+
+def far_kernel(ends, rows_above, rows_below, corner_above, corner_below, order, order_side, far, order_out, rows):
+    order_out[...] = natural_order()
+    reorder_rows(rows_above, rows_below, slice(PLANES, SENT), order[...], rows)
+
+    def put(i, cells, sl, domain):
+        for p, (planes, faces, source, mask) in enumerate(cells):
+            for k, x in enumerate(planes + faces[:2]):
+                far[i, k, p, :, sl] = x
+            far[i, FIELDS + 2 + i, p, :, sl] = faces[2]
+            far[i, SWEEP_W, p, :, sl] = weight_of(planes, mask)
+            far[i, SOURCE, p, :, sl] = last_sublanes(source) if isinstance(source, list) else source
+
+    corners = corner_planes((corner_above, corner_below), order_side[...])
+    far_planes(ends, rows, corners, far.shape[-1], put)
+
+
+def far_coarse_kernel(ends, rows_above, rows_below, corner_above, corner_below, order, order_side, far, rows):
+    reorder_rows(rows_above, rows_below, slice(PLANES, SENT), order[...], rows)
+
+    def put(i, cells, sl, domain):
+        def read(k, p):
+            planes, faces, _, _ = cells[p]
+            return planes[k] if k < FIELDS else faces[min(k - FIELDS, 2)]
+
+        def write(k, p, x):
+            if k in (FIELDS + 2, FIELDS + 3) and k != FIELDS + 2 + i:
+                return
+            far[i, k, p, :, sl] = x
+
+        build_levels(read, [None, write], sl, domain)
+
+    corners = corner_planes((corner_above, corner_below), order_side[...])
+    far_planes(ends, rows, corners, far.shape[-1], put)
 
 
 def apply_at(c, r, v, j, above=None, below=None):
@@ -437,31 +492,37 @@
         bottom[wide, p, :, sl] = product(FIELDS + 2)
 
 
-def first_kernel(ends, main, rows_above, rows_below, corner_above, corner_below, order, order_side, near, v2, t1, t1_top, t1_bottom, sums, va, vb, prods):
+def reorder_rows(rows_above, rows_below, planes, order, out):
+    blocks = rows_above.shape[-1] // BLOCK
+    size = (planes.stop - planes.start) * 8
+    parts = [rows[planes, :, b * BLOCK : b * BLOCK + BLOCK].reshape(size, BLOCK) for rows in (rows_above, rows_below) for b in range(blocks)]
+    x = reorder(jnp.concatenate(parts, axis=0), order)
+    for n in range(len(parts)):
+        out[n // blocks, n % blocks] = x[n * size : n * size + size]
+
+
+def first_kernel(ends, main, rows_above, rows_below, corner_above, corner_below, order, order_side, near, v2, t1, t1_top, t1_bottom, sums, va, vb, prods, rows):
     tiles = main.shape[-1] // T
     c0 = FineRows(main, near)
     t0 = SourceOf(c0)
     last = slice((tiles - 1) * T, tiles * T)
 
     def put(i, p, planes, mask, sl):
-        faces = planes[FIELDS : FIELDS + 4]
         source = planes[PLANES - 1]
-        jac = with_face_sum(planes[:FIELDS], faces)
-        weight = weight_of(jac, mask)
-        for k, x in enumerate(jac + faces + [weight, source]):
+        weight = weight_of(planes[:FIELDS], mask)
+        for k, x in enumerate(planes[: PLANES - 1] + [weight, source]):
             near[i, k, p, :, sl] = x
         va[1 if i == 0 else EXT - 2, p, :, sl] = weight * source
 
     def fill(j):
         sl = tile(j)
-        cols = pl.ds(pl.multiple_of(j * BLOCK, BLOCK), BLOCK)
-        for i, rows in enumerate((rows_above, rows_below)):
-            x = reorder(rows[0:FINE, :, cols].reshape(FINE * 8, BLOCK), order[...])
+        for i in range(2):
             for p in range(PHASES):
-                planes = [x[k * 8 : k * 8 + 8, p * T : p * T + T] for k in range(FINE)]
-                put(i, p, planes, planes[PLANES - 1][FIELDS : FIELDS + 1] * ends[i], sl)
-                prods[i, p, :, sl] = planes[PLANES]
-
+                planes = [rows[i, j, k * 8 : k * 8 + 8, p * T : p * T + T] for k in range(PLANES)]
+                put(i, p, planes, planes[PLANES - 1][FIELDS:8] * ends[i], sl)
+                prods[i, p, :, sl] = last_sublanes(planes)
+
+    reorder_rows(rows_above, rows_below, slice(0, PLANES), order[...], rows)
     each(tiles - 1, fill)
     sides = side_domain(ends)
     corners = corner_planes((corner_above, corner_below), order_side[...])
@@ -470,7 +531,9 @@
         planes, masks = corners[2 * i]
         far, far_masks = corners[2 * i + 1]
         for p in range(PHASES):
-            put(i, p, [x[p] for x in planes], jnp.where(domain > 0.0, masks[p], 0.0), last)
+            raw = [x[p] for x in planes]
+            raw[:FIELDS] = with_face_sum(raw[:FIELDS], raw[FIELDS : FIELDS + 4])
+            put(i, p, raw, jnp.where(domain > 0.0, masks[p], 0.0), last)
             here = [x[p] for x in far]
             jac = with_face_sum(here[:FIELDS], here[FIELDS : FIELDS + 4])
             weight = weight_of(jac, jnp.where(domain > 0.0, far_masks[p], 0.0))
@@ -548,19 +611,8 @@
     each(tiles, rest)
 
 
-def third_kernel(ends, main, c1, far0, t2_own, above, below, e1_in, e1, top, bottom, t2, va, vb, far):
+def third_kernel(main, c1, far, t2_own, above, below, e1_in, e1, top, bottom, t2, va, vb):
     tiles = main.shape[-1] // T
-    sides = side_domain(ends)
-
-    def build(i, sl, domain):
-        def write(k, p, x):
-            far[i, k, p, :, sl] = x
-
-        build_levels(lambda k, p: far0[i, k, p, :, sl], [None, write], sl, domain)
-
-    for i in range(2):
-        each(tiles - 1, lambda j: build(i, tile(j), ends[i]))
-        build(i, slice((tiles - 1) * T, tiles * T), sides * ends[i])
     c2 = WithFar(main, far)
 
     def fill(j):
@@ -620,16 +672,17 @@
                 diff = t0[r, p, :, sl] - out
                 res = jnp.where(c0[r, SWEEP_W, p, :, sl] != 0.0, diff, 0.0)
                 total = total + res * res
-                buf[p, pl.ds(r - WIDE, FIELDS, stride=ROWS), :] = va[r, p, 0:FIELDS, sl]
-                buf[p, pl.ds(GRID + r - WIDE, FIELDS, stride=ROWS), :] = res[0:FIELDS]
+                buf[j, p, pl.ds(r - WIDE, FIELDS, stride=ROWS), :] = va[r, p, 0:FIELDS, sl]
+                buf[j, p, pl.ds(GRID + r - WIDE, FIELDS, stride=ROWS), :] = res[0:FIELDS]
         sums[...] += total
-        x = jnp.concatenate([buf[p] for p in range(PHASES)], axis=1)
-        y = reorder(x, order[...])
-        cols = pl.ds(pl.multiple_of(j * BLOCK, BLOCK), BLOCK)
-        adjoint[:, cols] = y[0:GRID]
-        residual[:, cols] = y[GRID : 2 * GRID]
 
     each(tiles - 1, rest)
+    x = jnp.concatenate([jnp.concatenate([buf[j, p] for p in range(PHASES)], axis=1) for j in range(tiles - 1)], axis=0)
+    y = reorder(x, order[...])
+    for j in range(tiles - 1):
+        cols = slice(j * BLOCK, j * BLOCK + BLOCK)
+        adjoint[:, cols] = y[2 * j * GRID : (2 * j + 1) * GRID]
+        residual[:, cols] = y[(2 * j + 1) * GRID : (2 * j + 2) * GRID]
 
 
 def call(kernel, outs, args, scratch=(), spaces=None, size=0, limit=LIMIT, out_spaces=None):
@@ -674,13 +727,10 @@
 
     flag = {0: pltpu.SMEM}
     inputs = [
-        pltpu.with_memory_space_constraint(x, pltpu.HBM)
-        for x in (
-            jacobian.reshape(FIELDS, GRID, columns),
-            face_coef.reshape(4, GRID, columns),
-            source.reshape(GRID, columns),
-            active,
-        )
+        jacobian.reshape(FIELDS, GRID, columns),
+        face_coef.reshape(4, GRID, columns),
+        source.reshape(GRID, columns),
+        active,
     ]
     in_hbm = {i: pltpu.HBM for i in range(len(inputs))}
     staged = [(RAW, columns), pltpu.VMEM((ROWS, columns), jnp.int32)]
@@ -689,44 +739,44 @@
     order_side = jax.ShapeDtypeStruct((2 * T, BLOCK), BF16)
     sum_tile = (8, T)
 
+    rows = pltpu.HBM((SENT, 8, columns), F32)
     top, bottom, left, right = call(
         send_kernel,
-        [(FINE + PLANES, 8, columns)] * 2 + [(PACK + ROWS, T)] * 2,
-        inputs,
-        [*staged, (RAW, T), copies],
+        [rows, rows] + [(PACK + ROWS, T)] * 2,
+        [pltpu.with_memory_space_constraint(x, pltpu.HBM) for x in inputs],
+        [*staged, (RAW, T), (2, SENT, 8, columns), copies, pltpu.SemaphoreType.DMA((blocks, 2))],
         in_hbm,
         limit=12 * 2**20,
+        out_spaces={0: pltpu.HBM, 1: pltpu.HBM},
     )
     from_right = ring(left, "blk", -1)
     from_left = ring(right, "blk", 1)
     rows_below = ring(top, "hull", -1)
     rows_above = ring(bottom, "hull", 1)
-    inner, own, side = call(
+    inner, token = call(
         own_kernel,
-        [pltpu.HBM((ROWS, FINE, PHASES, 8, quads), F32), order, order_side],
+        [pltpu.HBM((ROWS, FINE, PHASES, 8, quads), F32), sum_tile],
         inputs,
         [
-            *staged,
+            pltpu.VMEM((BLOCK, BLOCK), BF16),
             (2, PHASES, RAW, T),
             (2, PHASES, ROWS, T),
             (2, ROWS, FINE, PHASES, 8, T),
-            copies,
             pltpu.SemaphoreType.DMA((blocks,)),
         ],
-        in_hbm,
         size=25 * 10**6,
         limit=16 * 2**20,
         out_spaces={0: pltpu.HBM},
     )
     inner = pltpu.with_memory_space_constraint(inner, pltpu.HBM)
     corner = (2, 2, PER_GROUP * 8, T)
-    top, bottom = call(corner_kernel, [corner, corner], [from_right, from_left, side], spaces={2: pl.ANY})
+    top, bottom = call(corner_kernel, [corner, corner], [from_right, from_left, token], spaces={2: pl.ANY})
     corner_below = ring(top, "hull", -1)
     corner_above = ring(bottom, "hull", 1)
-    (main,) = call(
+    main, own, side = call(
         side_kernel,
-        [coefs(ROWS, FINE, 4)],
-        [ends, from_right, from_left, inner, side],
+        [coefs(ROWS, FINE, 4), order, order_side],
+        [ends, from_right, from_left, inner],
         [(PHASES, RAW, T), (PHASES, ROWS, T), pltpu.SemaphoreType.DMA((ROWS,))],
         {0: pltpu.SMEM, 3: pltpu.HBM},
         size=9 * 10**6,
@@ -735,16 +785,24 @@
         first_kernel,
         [coefs(2, FINE, 4), cells(ROWS, 4), cells(ROWS, 2), cells(2, 2), cells(2, 2), sum_tile],
         [ends, main, rows_above, rows_below, corner_above, corner_below, own, side],
-        [cells(EXT, 4), cells(EXT, 4), cells(2, 4)],
+        [cells(EXT, 4), cells(EXT, 4), cells(2, 4), (2, blocks, PLANES * 8, BLOCK)],
         flag,
     )
     below = ring(top, "hull", -1)
     above = ring(bottom, "hull", 1)
+    (far2,) = call(
+        far_coarse_kernel,
+        [coefs(2, PLANES, 1)],
+        [ends, rows_above, rows_below, corner_above, corner_below, own, side],
+        [(2, blocks, (SENT - PLANES) * 8, BLOCK)],
+        flag,
+        size=7 * 10**6,
+    )
     far, natural = call(
         far_kernel,
         [coefs(2, FINE, 4), order],
         [ends, rows_above, rows_below, corner_above, corner_below, own, side],
-        (),
+        [(2, blocks, (SENT - PLANES) * 8, BLOCK)],
         flag,
         size=8 * 10**6,
     )
@@ -760,9 +818,8 @@
     e1, top, bottom = call(
         third_kernel,
         [cells(ROWS, 2), cells(2, 2), cells(2, 2)],
-        [ends, c2, c1, far, t2, above, below, e1],
-        [cells(EXT, 1)] * 3 + [coefs(2, PLANES, 1)],
-        flag,
+        [c2, c1, far2, t2, above, below, e1],
+        [cells(EXT, 1)] * 3,
     )
     below = ring(top, "hull", -1)
     above = ring(bottom, "hull", 1)
@@ -775,7 +832,7 @@
         fifth_kernel,
         [(GRID, columns), (GRID, columns), sum_tile],
         [main, near, far, v, above, below, natural],
-        [cells(EXT, 4)] * 2 + [(PHASES, 2 * GRID, T)],
+        [cells(EXT, 4)] * 2 + [(blocks, PHASES, 2 * GRID, T)],
     )
     squares = jnp.stack([sum0, 2.0 * sum1, sum2])
     squares = total_over_devices(jnp.sum(squares[:, :FIELDS], axis=(1, 2)))

time: 92.6 us -> 84.8 us (0.916)
  Pallas kernels: 40.2 us -> 35.4 us
  blocking collectives: 19 us -> 17.8 us
    pallas_call x11 -> x12, Pallas kernels: 40.2 us -> 35.4 us  [call(): pl.pallas_call(kernel, out_shape=[jax.ShapeDtypeStruct(s, F32) if isinsta...]
    all_to_all x1, blocking collectives: 19 us -> 17.8 us  [total_over_devices(): lax.all_to_all(sent, axes, 0, 0, tiled=True)]
  transfers between devices with their start and end apart: 14 -> 14, of which waited for: 3 -> 5; matrix products, arithmetic and copies ran while one was open for 0% -> 0% of each run, Pallas kernels for 20% -> 19%
where the time goes in v3:
time: 84.8 us; the launch traced here: 84.3 us
  Pallas kernels  35.4 us (42%)
  starting transfers between devices  24.2 us (29%)
  blocking collectives  17.8 us (21%)
  waiting for transfers between devices  5.29 us (6%)
  between operations  0.87 us (1%)
    pallas_call x12, Pallas kernels, call(): pl.pallas_call(kernel, out_shape=[jax.ShapeDtypeStruct(s, F32) if isinsta...  35.4 us
    ppermute x14, starting transfers between devices, ring(): lax.ppermute(x, axis, [(i, (i + step) % count) for i in range(count)])  24.2 us
    all_to_all x1, blocking collectives, total_over_devices(): lax.all_to_all(sent, axes, 0, 0, tiled=True)  17.8 us
    ppermute x14, waiting for transfers between devices, ring(): lax.ppermute(x, axis, [(i, (i + step) % count) for i in range(count)])  5.29 us
  transfers between devices with their start and end apart: 14, of which 5 were waited for; matrix products, arithmetic and copies ran while one was open for 0% of the time, Pallas kernels for 19%

profile of v3, /device:TPU:0, one launch (start us, length us, event | category | flops | bytes accessed | tf_op | source)
XLA Modules:
  0.0 84.3 jit_solution(9911451682607115898)
XLA Ops:
  0.6 0.0 copy-start
  0.6 0.0 copy-start.1
  0.7 0.0 copy-start.2
  0.7 0.0 copy-start.3
  0.7 5.1 %send_kernel.1 = (f32[22,8,2048]{2,1,0:T(8,128)}, f32[22,8,2048]{2,1,0:T(8,128)}, f32[176,128]{1,0:T(8,128)S(1)}, f32[176,128]{1,0:T(8,128)S(1)}) custom-call(f32[7,56,2048]{2,1,0:T(8,128)} %bitcast.14, f32[4,56,2048]{2,1,0:T(8,128)} %bitcast.16, f32[56,2048]{1,0:T(8,128)} %bitcast.18, s32[8,2048]{1,0:T(8,128)} %act.3), custom_call_target="tpu_custom_call" | custom-call | tf_op jit(solution)/shard_map/send_kernel/pallas_call | solution.py:690
  5.8 0.0 collective-permute-start.2
  5.8 2.9 %collective-permute-start.3 = (f32[22,8,2048]{2,1,0:T(8,128)}, f32[22,8,2048]{2,1,0:T(8,128)S(1)}, u32[]{:S(2)}, u32[]{:S(2)}) collective-permute-start(f32[22,8,2048]{2,1,0:T(8,128)} %get-tuple-element.44), channel_id=1, source_target_pairs={{0,112},{16,0},{32,16},{48,32},{64,48},{80,64},{96,80},{112,96},{1... | collective-permute-start | bytes 4325384 | tf_op jit(solution)/shard_map/ppermute | solution.py:704
  8.7 6.3 %collective-permute-start = (f32[176,128]{1,0:T(8,128)S(1)}, f32[176,128]{1,0:T(8,128)S(1)}, u32[]{:S(2)}, u32[]{:S(2)}) collective-permute-start(f32[176,128]{1,0:T(8,128)S(1)} %get-tuple-element.39), channel_id=1, source_target_pairs={{0,15},{1,0},{2,1},{3,2},{4,3},{5,4},{6,5},{7,6},{8,7},{9,8},{10,9... | collective-permute-start | bytes 270344 | tf_op jit(solution)/shard_map/ppermute | solution.py:704
  15.1 0.0 collective-permute-start.1
  15.1 0.0 copy-done
  15.1 0.0 copy-done.1
  15.1 0.0 copy-done.2
  15.1 0.0 copy-done.3
  15.1 6.6 %own_kernel.1 = (f32[8,13,4,8,512]{4,3,2,1,0:T(8,128)}, f32[8,128]{1,0:T(8,128)S(1)}) custom-call(f32[7,56,2048]{2,1,0:T(8,128)S(1)} %bitcast.15, f32[4,56,2048]{2,1,0:T(8,128)S(1)} %bitcast.17, f32[56,2048]{1,0:T(8,128)S(1)} %bitcast.19, s32[8,2048]{1,0:T(8,128)S(1)} %copy-done.3), custom_call_target="tpu_custom_call" | custom-call | bytes 25000000 | tf_op jit(solution)/shard_map/own_kernel/pallas_call | solution.py:690
  21.7 0.0 collective-permute-done.from_right
  21.7 1.2 %collective-permute-done.1.from_left = f32[176,128]{1,0:T(8,128)S(1)} collective-permute-done((f32[176,128]{1,0:T(8,128)S(1)}, f32[176,128]{1,0:T(8,128)S(1)}, u32[]{:S(2)}, u32[]{:S(2)}) %collective-permute-start.1) | collective-permute-done | bytes 90144 | tf_op jit(solution)/shard_map/ppermute | solution.py:704
  22.9 0.0 collective-permute-start.4
  23.0 2.9 %collective-permute-start.5 = (f32[2,2,24,128]{3,2,1,0:T(8,128)S(1)}, f32[2,2,24,128]{3,2,1,0:T(8,128)S(1)}, u32[]{:S(2)}, u32[]{:S(2)}) collective-permute-start(f32[2,2,24,128]{3,2,1,0:T(8,128)S(1)} %get-tuple-element.47), channel_id=1, source_target_pairs={{0,112},{16,0},{32,16},{48,32},{64,48},{80,64},{96,80},{112,96},{1... | collective-permute-start | bytes 147464 | tf_op jit(solution)/shard_map/ppermute | solution.py:704
  25.9 0.1 add_convert_fusion.ends
  26.0 3.7 %side_kernel.1 = (f32[8,13,4,8,640]{4,3,2,1,0:T(8,128)S(1)}, bf16[512,512]{1,0:T(8,128)(2,1)S(1)}, bf16[256,512]{1,0:T(8,128)(2,1)S(1)}) custom-call(f32[4]{0:T(128)S(1)} %add_convert_fusion.ends, f32[176,128]{1,0:T(8,128)S(1)} %collective-permute-done.from_right, f32[176,128]{1,0:T(8,128)S(1)} %collective-permute-done.1.from_left, ...), custom_call_target="tpu_custom_call" | custom-call | bytes 9000000 | tf_op jit(solution)/shard_map/side_kernel/pallas_call | solution.py:690
  29.7 0.0 collective-permute-done.4.corner_above
  29.7 0.0 collective-permute-done.5.corner_below
  29.7 0.0 collective-permute-done.2.rows_above
  29.7 0.0 collective-permute-done.3.rows_below
  29.7 4.4 %first_kernel.1 = (f32[2,13,4,8,640]{4,3,2,1,0:T(8,128)S(1)}, f32[8,4,8,640]{3,2,1,0:T(8,128)S(1)}, f32[8,2,8,640]{3,2,1,0:T(8,128)S(1)}, f32[2,2,8,640]{3,2,1,0...) custom-call(f32[4]{0:T(128)S(1)} %add_convert_fusion.ends, ...), custom_call_target="tpu_custom_call" | custom-call | tf_op jit(solution)/shard_map/first_kernel/pallas_call | solution.py:690
  34.2 0.0 collective-permute-start.6
  34.2 2.9 %collective-permute-start.7 = (f32[2,2,8,640]{3,2,1,0:T(8,128)S(1)}, f32[2,2,8,640]{3,2,1,0:T(8,128)S(1)}, u32[]{:S(2)}, u32[]{:S(2)}) collective-permute-start(f32[2,2,8,640]{3,2,1,0:T(8,128)S(1)} %get-tuple-element.56), channel_id=1, source_target_pairs={{0,112},{16,0},{32,16},{48,32},{64,48},{80,64},{96,80},{112,96},{1... | collective-permute-start | bytes 245768 | tf_op jit(solution)/shard_map/ppermute | solution.py:704
  37.1 1.9 %levels_kernel.1 = (f32[12,12,2,8,640]{4,3,2,1,0:T(8,128)S(1)}, f32[12,12,1,8,640]{4,3,2,1,0:T(8,128)S(1)}) custom-call(f32[4]{0:T(128)S(1)} %add_convert_fusion.ends, f32[8,13,4,8,640]{4,3,2,1,0:T(8,128)S(1)} %get-tuple-element.42.main, f32[2,13,4,8,640]{4,3,2,1,0:T(8,128)S(1)} %get-tuple-element.50.near), custom_call_target="tpu_custom_call" | custom-call | bytes 10000000 | tf_op jit(solution)/shard_map/levels_kernel/pallas_call | solution.py:690
  39.0 0.2 collective-permute-done.6.above
  39.2 0.0 collective-permute-done.7.below
  39.3 1.4 %second_kernel.1 = (f32[12,2,8,640]{3,2,1,0:T(8,128)S(1)}, f32[8,2,8,640]{3,2,1,0:T(8,128)S(1)}, f32[8,1,8,640]{3,2,1,0:T(8,128)S(1)}, f32[3,1,8,640]{3,2,1,0:T(...) custom-call(f32[12,12,2,8,640]{4,3,2,1,0:T(8,128)S(1)} %get-tuple-element.52.c1, ...), custom_call_target="tpu_custom_call" | custom-call | tf_op jit(solution)/shard_map/second_kernel/pallas_call | solution.py:690
  40.6 0.0 collective-permute-start.8
  40.7 3.0 %collective-permute-start.9 = (f32[3,1,8,640]{3,2,1,0:T(8,128)S(1)}, f32[3,1,8,640]{3,2,1,0:T(8,128)S(1)}, u32[]{:S(2)}, u32[]{:S(2)}) collective-permute-start(f32[3,1,8,640]{3,2,1,0:T(8,128)S(1)} %get-tuple-element.60), channel_id=1, source_target_pairs={{0,112},{16,0},{32,16},{48,32},{64,48},{80,64},{96,80},{112,96},{1... | collective-permute-start | bytes 184328 | tf_op jit(solution)/shard_map/ppermute | solution.py:704
  43.6 1.8 %far_coarse_kernel.1.far = f32[2,12,1,8,640]{4,3,2,1,0:T(8,128)S(1)} custom-call(f32[4]{0:T(128)S(1)} %add_convert_fusion.ends, f32[22,8,2048]{2,1,0:T(8,128)S(1)} %collective-permute-done.2.rows_above, f32[22,8,2048]{2,1,0:T(8,128)S(1)} %collective-permute-done.3.rows_below, f32[2,2,24,128]{3,2,1,0:T(8,128)S(1)} %collective-permute-done.4.corner_above, ...), custom_call_target="tpu_custom_call" | custom-call | bytes 7000000 | tf_op jit(solution)/shard_map/far_coarse_kernel/pallas_call | solution.py:690
  45.5 0.1 collective-permute-done.8.above
  45.5 0.0 collective-permute-done.9.below
  45.5 1.8 %third_kernel.1 = (f32[8,2,8,640]{3,2,1,0:T(8,128)S(1)}, f32[2,2,8,640]{3,2,1,0:T(8,128)S(1)}, f32[2,2,8,640]{3,2,1,0:T(8,128)S(1)}) custom-call(f32[12,12,1,8,640]{4,3,2,1,0:T(8,128)S(1)} %get-tuple-element.53.c2.main, f32[12,12,2,8,640]{4,3,2,1,0:T(8,128)S(1)} %get-tuple-element.52.c1, f32[2,12,1,8,640]{4,3,2,1,0:T(8,128)S(1)} %far_coarse_kernel.1.far, ...), custom_call_target="tpu_custom_call" | custom-call | tf_op jit(solution)/shard_map/third_kernel/pallas_call | solution.py:690
  47.4 0.0 collective-permute-start.10
  47.4 3.0 %collective-permute-start.11 = (f32[2,2,8,640]{3,2,1,0:T(8,128)S(1)}, f32[2,2,8,640]{3,2,1,0:T(8,128)S(1)}, u32[]{:S(2)}, u32[]{:S(2)}) collective-permute-start(f32[2,2,8,640]{3,2,1,0:T(8,128)S(1)} %get-tuple-element.64), channel_id=1, source_target_pairs={{0,112},{16,0},{32,16},{48,32},{64,48},{80,64},{96,80},{112,96},{1... | collective-permute-start | bytes 245768 | tf_op jit(solution)/shard_map/ppermute | solution.py:704
  50.4 2.1 %collective-permute-done.10.above = f32[2,2,8,640]{3,2,1,0:T(8,128)S(1)} collective-permute-done((f32[2,2,8,640]{3,2,1,0:T(8,128)S(1)}, f32[2,2,8,640]{3,2,1,0:T(8,128)S(1)}, u32[]{:S(2)}, u32[]{:S(2)}) %collective-permute-start.10) | collective-permute-done | bytes 81952 | tf_op jit(solution)/shard_map/ppermute | solution.py:704
  52.5 0.0 collective-permute-done.11.below
  52.5 1.5 %fourth_kernel.1 = (f32[8,4,8,640]{3,2,1,0:T(8,128)S(1)}, f32[3,4,8,640]{3,2,1,0:T(8,128)S(1)}, f32[3,4,8,640]{3,2,1,0:T(8,128)S(1)}) custom-call(f32[12,12,2,8,640]{4,3,2,1,0:T(8,128)S(1)} %get-tuple-element.52.c1, f32[8,13,4,8,640]{4,3,2,1,0:T(8,128)S(1)} %get-tuple-element.42.main, f32[12,2,8,640]{3,2,1,0:T(8,128)S(1)} %get-tuple-element.57.t1, ...), custom_call_target="tpu_custom_call" | custom-call | tf_op jit(solution)/shard_map/fourth_kernel/pallas_call | solution.py:690
  54.0 0.0 collective-permute-start.12
  54.0 3.0 %collective-permute-start.13 = (f32[3,4,8,640]{3,2,1,0:T(8,128)S(1)}, f32[3,4,8,640]{3,2,1,0:T(8,128)S(1)}, u32[]{:S(2)}, u32[]{:S(2)}) collective-permute-start(f32[3,4,8,640]{3,2,1,0:T(8,128)S(1)} %get-tuple-element.68), channel_id=1, source_target_pairs={{0,112},{16,0},{32,16},{48,32},{64,48},{80,64},{96,80},{112,96},{1... | collective-permute-start | bytes 737288 | tf_op jit(solution)/shard_map/ppermute | solution.py:704
  57.0 2.1 %far_kernel.1 = (f32[2,13,4,8,640]{4,3,2,1,0:T(8,128)S(1)}, bf16[512,512]{1,0:T(8,128)(2,1)S(1)}) custom-call(f32[4]{0:T(128)S(1)} %add_convert_fusion.ends, f32[22,8,2048]{2,1,0:T(8,128)S(1)} %collective-permute-done.2.rows_above, f32[22,8,2048]{2,1,0:T(8,128)S(1)} %collective-permute-done.3.rows_below, ...), custom_call_target="tpu_custom_call" | custom-call | bytes 8000000 | tf_op jit(solution)/shard_map/far_kernel/pallas_call | solution.py:690
  59.1 1.7 %collective-permute-done.12.above = f32[3,4,8,640]{3,2,1,0:T(8,128)S(1)} collective-permute-done((f32[3,4,8,640]{3,2,1,0:T(8,128)S(1)}, f32[3,4,8,640]{3,2,1,0:T(8,128)S(1)}, u32[]{:S(2)}, u32[]{:S(2)}) %collective-permute-start.12) | collective-permute-done | bytes 245792 | tf_op jit(solution)/shard_map/ppermute | solution.py:704
  60.8 0.0 collective-permute-done.13.below
  60.8 5.0 %fifth_kernel.1 = (f32[56,2048]{1,0:T(8,128)}, f32[56,2048]{1,0:T(8,128)}, f32[8,128]{1,0:T(8,128)S(1)}) custom-call(f32[8,13,4,8,640]{4,3,2,1,0:T(8,128)S(1)} %get-tuple-element.42.main, f32[2,13,4,8,640]{4,3,2,1,0:T(8,128)S(1)} %get-tuple-element.50.near, f32[2,13,4,8,640]{4,3,2,1,0:T(8,128)S(1)} %get-tuple-element.51.far, ...), custom_call_target="tpu_custom_call" | custom-call | tf_op jit(solution)/shard_map/fifth_kernel/pallas_call | solution.py:690
  65.8 0.1 fusion
  66.0 17.8 %all_to_all.6 = f32[128,1,128]{2,1,0:T(1,128)S(1)} all-to-all(f32[128,1,128]{2,1,0:T(1,128)S(1)} %broadcast_in_dim.2), channel_id=1, replica_groups=mesh['hull'=8,'blk'=16] {'hull','blk'}, dimensions={0} | all-to-all | bytes 131072 | tf_op jit(solution)/shard_map/all_to_all | solution.py:711
  83.8 0.5 multiply_sqrt_fusion
  (5 shorter events, 0.1 us)
Async XLA Ops:
  0.6 14.4 %copy-start = (f32[7,7,8,2048]{3,2,1,0:T(8,128)S(1)}, f32[7,7,8,2048]{3,2,1,0:T(8,128)}, u32[]{:S(2)}) copy-start(f32[7,7,8,2048]{3,2,1,0:T(8,128)} %param.5) | copy-start | bytes 9633796
  0.6 14.4 %copy-start.1 = (f32[4,7,8,2048]{3,2,1,0:T(8,128)S(1)}, f32[4,7,8,2048]{3,2,1,0:T(8,128)}, u32[]{:S(2)}) copy-start(f32[4,7,8,2048]{3,2,1,0:T(8,128)} %param.6) | copy-start | bytes 5505028
  0.7 14.4 %copy-start.2 = (f32[7,8,2048]{2,1,0:T(8,128)S(1)}, f32[7,8,2048]{2,1,0:T(8,128)}, u32[]{:S(2)}) copy-start(f32[7,8,2048]{2,1,0:T(8,128)} %param.4) | copy-start | bytes 1376260
  0.7 14.4 %copy-start.3 = (s32[8,2048]{1,0:T(8,128)S(1)}, s32[8,2048]{1,0:T(8,128)}, u32[]{:S(2)}) copy-start(s32[8,2048]{1,0:T(8,128)} %act.3) | copy-start | bytes 196612
  5.8 23.9 %collective-permute-start.2 = (f32[22,8,2048]{2,1,0:T(8,128)}, f32[22,8,2048]{2,1,0:T(8,128)S(1)}, u32[]{:S(2)}, u32[]{:S(2)}) collective-permute-start(f32[22,8,2048]{2,1,0:T(8,128)} %get-tuple-element.43), channel_id=1, source_target_pairs={{0,16},{16,32},{32,48},{48,64},{64,80},{80,96},{96,112},{112,0},{1... | collective-permute-start | bytes 4325384 | tf_op jit(solution)/shard_map/ppermute | solution.py:704
  5.8 23.9 %collective-permute-start.3 = (f32[22,8,2048]{2,1,0:T(8,128)}, f32[22,8,2048]{2,1,0:T(8,128)S(1)}, u32[]{:S(2)}, u32[]{:S(2)}) collective-permute-start(f32[22,8,2048]{2,1,0:T(8,128)} %get-tuple-element.44), channel_id=1, source_target_pairs={{0,112},{16,0},{32,16},{48,32},{64,48},{80,64},{96,80},{112,96},{1... | collective-permute-start | bytes 4325384 | tf_op jit(solution)/shard_map/ppermute | solution.py:704
  8.7 13.0 %collective-permute-start = (f32[176,128]{1,0:T(8,128)S(1)}, f32[176,128]{1,0:T(8,128)S(1)}, u32[]{:S(2)}, u32[]{:S(2)}) collective-permute-start(f32[176,128]{1,0:T(8,128)S(1)} %get-tuple-element.39), channel_id=1, source_target_pairs={{0,15},{1,0},{2,1},{3,2},{4,3},{5,4},{6,5},{7,6},{8,7},{9,8},{10,9... | collective-permute-start | bytes 270344 | tf_op jit(solution)/shard_map/ppermute | solution.py:704
  15.1 7.8 %collective-permute-start.1 = (f32[176,128]{1,0:T(8,128)S(1)}, f32[176,128]{1,0:T(8,128)S(1)}, u32[]{:S(2)}, u32[]{:S(2)}) collective-permute-start(f32[176,128]{1,0:T(8,128)S(1)} %get-tuple-element.40), channel_id=1, source_target_pairs={{0,1},{1,2},{2,3},{3,4},{4,5},{5,6},{6,7},{7,8},{8,9},{9,10},{10,1... | collective-permute-start | bytes 270344 | tf_op jit(solution)/shard_map/ppermute | solution.py:704
  22.9 6.8 %collective-permute-start.4 = (f32[2,2,24,128]{3,2,1,0:T(8,128)S(1)}, f32[2,2,24,128]{3,2,1,0:T(8,128)S(1)}, u32[]{:S(2)}, u32[]{:S(2)}) collective-permute-start(f32[2,2,24,128]{3,2,1,0:T(8,128)S(1)} %get-tuple-element.46), channel_id=1, source_target_pairs={{0,16},{16,32},{32,48},{48,64},{64,80},{80,96},{96,112},{112,0},{1... | collective-permute-start | bytes 147464 | tf_op jit(solution)/shard_map/ppermute | solution.py:704
  23.0 6.7 %collective-permute-start.5 = (f32[2,2,24,128]{3,2,1,0:T(8,128)S(1)}, f32[2,2,24,128]{3,2,1,0:T(8,128)S(1)}, u32[]{:S(2)}, u32[]{:S(2)}) collective-permute-start(f32[2,2,24,128]{3,2,1,0:T(8,128)S(1)} %get-tuple-element.47), channel_id=1, source_target_pairs={{0,112},{16,0},{32,16},{48,32},{64,48},{80,64},{96,80},{112,96},{1... | collective-permute-start | bytes 147464 | tf_op jit(solution)/shard_map/ppermute | solution.py:704
  34.2 5.1 %collective-permute-start.6 = (f32[2,2,8,640]{3,2,1,0:T(8,128)S(1)}, f32[2,2,8,640]{3,2,1,0:T(8,128)S(1)}, u32[]{:S(2)}, u32[]{:S(2)}) collective-permute-start(f32[2,2,8,640]{3,2,1,0:T(8,128)S(1)} %get-tuple-element.55), channel_id=1, source_target_pairs={{0,16},{16,32},{32,48},{48,64},{64,80},{80,96},{96,112},{112,0},{1... | collective-permute-start | bytes 245768 | tf_op jit(solution)/shard_map/ppermute | solution.py:704
  34.2 5.1 %collective-permute-start.7 = (f32[2,2,8,640]{3,2,1,0:T(8,128)S(1)}, f32[2,2,8,640]{3,2,1,0:T(8,128)S(1)}, u32[]{:S(2)}, u32[]{:S(2)}) collective-permute-start(f32[2,2,8,640]{3,2,1,0:T(8,128)S(1)} %get-tuple-element.56), channel_id=1, source_target_pairs={{0,112},{16,0},{32,16},{48,32},{64,48},{80,64},{96,80},{112,96},{1... | collective-permute-start | bytes 245768 | tf_op jit(solution)/shard_map/ppermute | solution.py:704
  40.6 4.9 %collective-permute-start.8 = (f32[3,1,8,640]{3,2,1,0:T(8,128)S(1)}, f32[3,1,8,640]{3,2,1,0:T(8,128)S(1)}, u32[]{:S(2)}, u32[]{:S(2)}) collective-permute-start(f32[3,1,8,640]{3,2,1,0:T(8,128)S(1)} %get-tuple-element.59), channel_id=1, source_target_pairs={{0,16},{16,32},{32,48},{48,64},{64,80},{80,96},{96,112},{112,0},{1... | collective-permute-start | bytes 184328 | tf_op jit(solution)/shard_map/ppermute | solution.py:704
  40.7 4.8 %collective-permute-start.9 = (f32[3,1,8,640]{3,2,1,0:T(8,128)S(1)}, f32[3,1,8,640]{3,2,1,0:T(8,128)S(1)}, u32[]{:S(2)}, u32[]{:S(2)}) collective-permute-start(f32[3,1,8,640]{3,2,1,0:T(8,128)S(1)} %get-tuple-element.60), channel_id=1, source_target_pairs={{0,112},{16,0},{32,16},{48,32},{64,48},{80,64},{96,80},{112,96},{1... | collective-permute-start | bytes 184328 | tf_op jit(solution)/shard_map/ppermute | solution.py:704
  47.4 5.1 %collective-permute-start.10 = (f32[2,2,8,640]{3,2,1,0:T(8,128)S(1)}, f32[2,2,8,640]{3,2,1,0:T(8,128)S(1)}, u32[]{:S(2)}, u32[]{:S(2)}) collective-permute-start(f32[2,2,8,640]{3,2,1,0:T(8,128)S(1)} %get-tuple-element.63), channel_id=1, source_target_pairs={{0,16},{16,32},{32,48},{48,64},{64,80},{80,96},{96,112},{112,0},{1... | collective-permute-start | bytes 245768 | tf_op jit(solution)/shard_map/ppermute | solution.py:704
  47.4 5.1 %collective-permute-start.11 = (f32[2,2,8,640]{3,2,1,0:T(8,128)S(1)}, f32[2,2,8,640]{3,2,1,0:T(8,128)S(1)}, u32[]{:S(2)}, u32[]{:S(2)}) collective-permute-start(f32[2,2,8,640]{3,2,1,0:T(8,128)S(1)} %get-tuple-element.64), channel_id=1, source_target_pairs={{0,112},{16,0},{32,16},{48,32},{64,48},{80,64},{96,80},{112,96},{1... | collective-permute-start | bytes 245768 | tf_op jit(solution)/shard_map/ppermute | solution.py:704
  54.0 6.9 %collective-permute-start.12 = (f32[3,4,8,640]{3,2,1,0:T(8,128)S(1)}, f32[3,4,8,640]{3,2,1,0:T(8,128)S(1)}, u32[]{:S(2)}, u32[]{:S(2)}) collective-permute-start(f32[3,4,8,640]{3,2,1,0:T(8,128)S(1)} %get-tuple-element.67), channel_id=1, source_target_pairs={{0,16},{16,32},{32,48},{48,64},{64,80},{80,96},{96,112},{112,0},{1... | collective-permute-start | bytes 737288 | tf_op jit(solution)/shard_map/ppermute | solution.py:704
  54.0 6.8 %collective-permute-start.13 = (f32[3,4,8,640]{3,2,1,0:T(8,128)S(1)}, f32[3,4,8,640]{3,2,1,0:T(8,128)S(1)}, u32[]{:S(2)}, u32[]{:S(2)}) collective-permute-start(f32[3,4,8,640]{3,2,1,0:T(8,128)S(1)} %get-tuple-element.68), channel_id=1, source_target_pairs={{0,112},{16,0},{32,16},{48,32},{64,48},{80,64},{96,80},{112,96},{1... | collective-permute-start | bytes 737288 | tf_op jit(solution)/shard_map/ppermute | solution.py:704

commit v4 on v3

--- a/solution.py
+++ b/solution.py
@@ -136,48 +136,32 @@
     return jnp.where(mask > 0.0, DAMP / diagonal(planes), 0.0)
 
 
-def fetch(jac, face, src, act, raw, flags, sems, columns):
-    blocks = src.shape[-1] // columns
-
-    def copies(b):
-        cols = pl.ds(b * columns, columns)
-        moves = [(jac.at[f, :, cols], raw.at[pl.ds(f * GRID, GRID), cols]) for f in range(FIELDS)]
-        moves += [(face.at[k, :, cols], raw.at[pl.ds((FIELDS + k) * GRID, GRID), cols]) for k in range(4)]
-        moves += [(src.at[:, cols], raw.at[pl.ds((PLANES - 1) * GRID, GRID), cols])]
-        moves += [(act.at[:, cols], flags.at[:, cols])]
-        return [pltpu.make_async_copy(a, d, sems.at[b, i]) for i, (a, d) in enumerate(moves)]
-
-    todo = [copies(b) for b in range(blocks)]
-    for group in todo:
-        for copy in group:
+def send_kernel(jac, face, src, act, top, bottom, left, right, raw_jac, raw_face, raw_src, flags, stage, sems, out_sems):
+    columns = src.shape[-1]
+    per = BLOCK // T
+    blocks = columns // BLOCK
+    fetches = []
+    for j in range(columns // T):
+        cols = pl.ds(j * T, T)
+        moves = [(jac.at[:, :, cols], raw_jac.at[j]), (face.at[:, :, cols], raw_face.at[j]), (src.at[:, cols], raw_src.at[j])]
+        fetches.append([pltpu.make_async_copy(a, d, sems.at[j, i]) for i, (a, d) in enumerate(moves)])
+    fetches[0].append(pltpu.make_async_copy(act, flags, sems.at[0, 3]))
+    last = columns // T - 1
+    for j in [0, last] + list(range(1, last)):
+        for copy in fetches[j]:
             copy.start()
-
-    def waiter(group):
-        def wait():
-            for copy in group:
-                copy.wait()
-
-        return wait
-
-    return [waiter(group) for group in todo]
-
-
-def send_kernel(jac, face, src, act, top, bottom, left, right, raw, flags, buf, stage, sems, out_sems):
-    columns = src.shape[-1]
-    waits = fetch(jac, face, src, act, raw, flags, sems, BLOCK)
-    per = BLOCK // T
     jobs = ((0, 0, 1, 3), (1, ROWS - 1, ROWS - 2, 2))
 
     def rows_of(b):
         def body(i):
-            sl = tile(b * per + i)
-            for k in range(PLANES):
-                buf[k * GRID : k * GRID + GRID] = raw[k * GRID : k * GRID + GRID, sl]
+            j = b * per + i
+            sl = tile(j)
 
             def row(r):
-                planes = [buf[pl.ds(k * GRID + r, FIELDS, stride=ROWS), :] for k in range(PLANES)]
-                faces = planes[FIELDS : FIELDS + 4]
-                return with_face_sum(planes[:FIELDS], faces), faces, planes[PLANES - 1], flags[r : r + 1, sl].astype(F32)
+                pick = pl.ds(r, FIELDS, stride=ROWS)
+                planes = [raw_jac[j, f, pick, :] for f in range(FIELDS)]
+                faces = [raw_face[j, k, pick, :] for k in range(4)]
+                return with_face_sum(planes, faces), faces, raw_src[j, pick, :], flags[r : r + 1, sl].astype(F32)
 
             for out, near, far, face_k in jobs:
                 planes, faces, source, mask = row(near)
@@ -195,25 +179,39 @@
 
         each(per, body)
 
+    def raw_plane(k, j):
+        if k < FIELDS:
+            return raw_jac[j, k]
+        return raw_face[j, k - FIELDS] if k < PLANES - 1 else raw_src[j]
+
+    def pack():
+        lane = iota((PACK, T), 1) // SIDE_COLS
+        for out, at, move in ((left, 0, 0), (right, columns - T, SIDE_COLS)):
+            packed = None
+            for g in range(GROUPS):
+                planes = range(g * PER_GROUP, g * PER_GROUP + PER_GROUP)
+                part = jnp.concatenate([raw_plane(k, at // T) for k in planes], axis=0)
+                shift = (g * SIDE_COLS + move) % T
+                part = pltpu.roll(part, shift, 1) if shift else part
+                packed = part if packed is None else jnp.where(lane == g, part, packed)
+            out[0:PACK] = packed
+            mask = flags[:, at : at + T].astype(F32)
+            out[PACK : PACK + ROWS] = pltpu.roll(mask, move, 1) if move else mask
+
     copies = []
-    for b, wait in enumerate(waits):
-        wait()
+    for copy in fetches[0] + fetches[last]:
+        copy.wait()
+    pack()
+    for b in range(blocks):
+        for j in range(b * per, b * per + per):
+            if j not in (0, last):
+                for copy in fetches[j]:
+                    copy.wait()
         rows_of(b)
         cols = pl.ds(b * BLOCK, BLOCK)
         for i, out in enumerate((top, bottom)):
             copies.append(pltpu.make_async_copy(stage.at[i, :, :, cols], out.at[:, :, cols], out_sems.at[b, i]))
             copies[-1].start()
-    lane = iota((PACK, T), 1) // SIDE_COLS
-    for out, at, move in ((left, 0, 0), (right, columns - T, SIDE_COLS)):
-        packed = None
-        for g in range(GROUPS):
-            part = raw[g * PACK : g * PACK + PACK, at : at + T]
-            shift = (g * SIDE_COLS + move) % T
-            part = pltpu.roll(part, shift, 1) if shift else part
-            packed = part if packed is None else jnp.where(lane == g, part, packed)
-        out[0:PACK] = packed
-        mask = flags[:, at : at + T].astype(F32)
-        out[PACK : PACK + ROWS] = pltpu.roll(mask, move, 1) if move else mask
     for copy in copies:
         copy.wait()
 
@@ -267,7 +265,11 @@
 
 def side_kernel(ends, from_right, from_left, own, main, order_own, order, buf, masks, sems):
     inner = own.shape[-1]
-    copies = [pltpu.make_async_copy(own.at[r], main.at[r, :, :, :, pl.ds(0, inner)], sems.at[r]) for r in range(ROWS)]
+    half = ROWS // 2
+    copies = [
+        pltpu.make_async_copy(own.at[pl.ds(r, half)], main.at[pl.ds(r, half), :, :, :, pl.ds(0, inner)], sems.at[r])
+        for r in (0, half)
+    ]
     for copy in copies:
         copy.start()
     order[...] = side_order()
@@ -733,8 +735,8 @@
         active,
     ]
     in_hbm = {i: pltpu.HBM for i in range(len(inputs))}
-    staged = [(RAW, columns), pltpu.VMEM((ROWS, columns), jnp.int32)]
-    copies = pltpu.SemaphoreType.DMA((blocks, PLANES + 1))
+    tiles = columns // T
+    staged = [(tiles, FIELDS, GRID, T), (tiles, 4, GRID, T), (tiles, GRID, T), pltpu.VMEM((ROWS, columns), jnp.int32)]
     order = jax.ShapeDtypeStruct((BLOCK, BLOCK), BF16)
     order_side = jax.ShapeDtypeStruct((2 * T, BLOCK), BF16)
     sum_tile = (8, T)
@@ -744,7 +746,7 @@
         send_kernel,
         [rows, rows] + [(PACK + ROWS, T)] * 2,
         [pltpu.with_memory_space_constraint(x, pltpu.HBM) for x in inputs],
-        [*staged, (RAW, T), (2, SENT, 8, columns), copies, pltpu.SemaphoreType.DMA((blocks, 2))],
+        [*staged, (2, SENT, 8, columns), pltpu.SemaphoreType.DMA((tiles, 4)), pltpu.SemaphoreType.DMA((blocks, 2))],
         in_hbm,
         limit=12 * 2**20,
         out_spaces={0: pltpu.HBM, 1: pltpu.HBM},

time: 84.8 us -> 84.5 us (level)
  no operation moved by 1% of the time
where the time goes in v4:
time: 84.5 us; the launch traced here: 84 us
  Pallas kernels  35 us (41%)
  starting transfers between devices  24.2 us (29%)
  blocking collectives  17.8 us (21%)
  waiting for transfers between devices  5.28 us (6%)
  between operations  0.87 us (1%)
    pallas_call x12, Pallas kernels, call(): pl.pallas_call(kernel, out_shape=[jax.ShapeDtypeStruct(s, F32) if isinsta...  35 us
    ppermute x14, starting transfers between devices, ring(): lax.ppermute(x, axis, [(i, (i + step) % count) for i in range(count)])  24.2 us
    all_to_all x1, blocking collectives, total_over_devices(): lax.all_to_all(sent, axes, 0, 0, tiled=True)  17.8 us
    ppermute x14, waiting for transfers between devices, ring(): lax.ppermute(x, axis, [(i, (i + step) % count) for i in range(count)])  5.28 us
  transfers between devices with their start and end apart: 14, of which 5 were waited for; matrix products, arithmetic and copies ran while one was open for 0% of the time, Pallas kernels for 19%

profile of v4, /device:TPU:0, one launch (start us, length us, event | category | flops | bytes accessed | tf_op | source)
XLA Modules:
  0.0 84.0 jit_solution(6761979535881394843)
XLA Ops:
  0.6 0.0 copy-start
  0.6 0.0 copy-start.1
  0.7 0.0 copy-start.2
  0.7 0.0 copy-start.3
  0.7 4.8 %send_kernel.1 = (f32[22,8,2048]{2,1,0:T(8,128)}, f32[22,8,2048]{2,1,0:T(8,128)}, f32[176,128]{1,0:T(8,128)S(1)}, f32[176,128]{1,0:T(8,128)S(1)}) custom-call(f32[7,56,2048]{2,1,0:T(8,128)} %bitcast.14, f32[4,56,2048]{2,1,0:T(8,128)} %bitcast.16, f32[56,2048]{1,0:T(8,128)} %bitcast.18, s32[8,2048]{1,0:T(8,128)} %act.3), custom_call_target="tpu_custom_call" | custom-call | tf_op jit(solution)/shard_map/send_kernel/pallas_call | solution.py:692
  5.5 0.0 collective-permute-start.2
  5.5 2.9 %collective-permute-start.3 = (f32[22,8,2048]{2,1,0:T(8,128)}, f32[22,8,2048]{2,1,0:T(8,128)S(1)}, u32[]{:S(2)}, u32[]{:S(2)}) collective-permute-start(f32[22,8,2048]{2,1,0:T(8,128)} %get-tuple-element.44), channel_id=1, source_target_pairs={{0,112},{16,0},{32,16},{48,32},{64,48},{80,64},{96,80},{112,96},{1... | collective-permute-start | bytes 4325384 | tf_op jit(solution)/shard_map/ppermute | solution.py:706
  8.5 6.3 %collective-permute-start = (f32[176,128]{1,0:T(8,128)S(1)}, f32[176,128]{1,0:T(8,128)S(1)}, u32[]{:S(2)}, u32[]{:S(2)}) collective-permute-start(f32[176,128]{1,0:T(8,128)S(1)} %get-tuple-element.39), channel_id=1, source_target_pairs={{0,15},{1,0},{2,1},{3,2},{4,3},{5,4},{6,5},{7,6},{8,7},{9,8},{10,9... | collective-permute-start | bytes 270344 | tf_op jit(solution)/shard_map/ppermute | solution.py:706
  14.8 0.0 collective-permute-start.1
  14.8 0.0 copy-done
  14.8 0.0 copy-done.1
  14.8 0.0 copy-done.2
  14.8 0.0 copy-done.3
  14.8 6.6 %own_kernel.1 = (f32[8,13,4,8,512]{4,3,2,1,0:T(8,128)}, f32[8,128]{1,0:T(8,128)S(1)}) custom-call(f32[7,56,2048]{2,1,0:T(8,128)S(1)} %bitcast.15, f32[4,56,2048]{2,1,0:T(8,128)S(1)} %bitcast.17, f32[56,2048]{1,0:T(8,128)S(1)} %bitcast.19, s32[8,2048]{1,0:T(8,128)S(1)} %copy-done.3), custom_call_target="tpu_custom_call" | custom-call | bytes 25000000 | tf_op jit(solution)/shard_map/own_kernel/pallas_call | solution.py:692
  21.4 0.0 collective-permute-done.from_right
  21.5 1.2 %collective-permute-done.1.from_left = f32[176,128]{1,0:T(8,128)S(1)} collective-permute-done((f32[176,128]{1,0:T(8,128)S(1)}, f32[176,128]{1,0:T(8,128)S(1)}, u32[]{:S(2)}, u32[]{:S(2)}) %collective-permute-start.1) | collective-permute-done | bytes 90144 | tf_op jit(solution)/shard_map/ppermute | solution.py:706
  22.7 0.0 collective-permute-start.4
  22.7 2.9 %collective-permute-start.5 = (f32[2,2,24,128]{3,2,1,0:T(8,128)S(1)}, f32[2,2,24,128]{3,2,1,0:T(8,128)S(1)}, u32[]{:S(2)}, u32[]{:S(2)}) collective-permute-start(f32[2,2,24,128]{3,2,1,0:T(8,128)S(1)} %get-tuple-element.47), channel_id=1, source_target_pairs={{0,112},{16,0},{32,16},{48,32},{64,48},{80,64},{96,80},{112,96},{1... | collective-permute-start | bytes 147464 | tf_op jit(solution)/shard_map/ppermute | solution.py:706
  25.6 0.1 add_convert_fusion.ends
  25.7 3.6 %side_kernel.1 = (f32[8,13,4,8,640]{4,3,2,1,0:T(8,128)S(1)}, bf16[512,512]{1,0:T(8,128)(2,1)S(1)}, bf16[256,512]{1,0:T(8,128)(2,1)S(1)}) custom-call(f32[4]{0:T(128)S(1)} %add_convert_fusion.ends, f32[176,128]{1,0:T(8,128)S(1)} %collective-permute-done.from_right, f32[176,128]{1,0:T(8,128)S(1)} %collective-permute-done.1.from_left, ...), custom_call_target="tpu_custom_call" | custom-call | bytes 9000000 | tf_op jit(solution)/shard_map/side_kernel/pallas_call | solution.py:692
  29.3 0.0 collective-permute-done.4.corner_above
  29.4 0.0 collective-permute-done.5.corner_below
  29.4 0.0 collective-permute-done.2.rows_above
  29.4 0.0 collective-permute-done.3.rows_below
  29.4 4.4 %first_kernel.1 = (f32[2,13,4,8,640]{4,3,2,1,0:T(8,128)S(1)}, f32[8,4,8,640]{3,2,1,0:T(8,128)S(1)}, f32[8,2,8,640]{3,2,1,0:T(8,128)S(1)}, f32[2,2,8,640]{3,2,1,0...) custom-call(f32[4]{0:T(128)S(1)} %add_convert_fusion.ends, ...), custom_call_target="tpu_custom_call" | custom-call | tf_op jit(solution)/shard_map/first_kernel/pallas_call | solution.py:692
  33.8 0.0 collective-permute-start.6
  33.8 2.9 %collective-permute-start.7 = (f32[2,2,8,640]{3,2,1,0:T(8,128)S(1)}, f32[2,2,8,640]{3,2,1,0:T(8,128)S(1)}, u32[]{:S(2)}, u32[]{:S(2)}) collective-permute-start(f32[2,2,8,640]{3,2,1,0:T(8,128)S(1)} %get-tuple-element.56), channel_id=1, source_target_pairs={{0,112},{16,0},{32,16},{48,32},{64,48},{80,64},{96,80},{112,96},{1... | collective-permute-start | bytes 245768 | tf_op jit(solution)/shard_map/ppermute | solution.py:706
  36.8 1.9 %levels_kernel.1 = (f32[12,12,2,8,640]{4,3,2,1,0:T(8,128)S(1)}, f32[12,12,1,8,640]{4,3,2,1,0:T(8,128)S(1)}) custom-call(f32[4]{0:T(128)S(1)} %add_convert_fusion.ends, f32[8,13,4,8,640]{4,3,2,1,0:T(8,128)S(1)} %get-tuple-element.42.main, f32[2,13,4,8,640]{4,3,2,1,0:T(8,128)S(1)} %get-tuple-element.50.near), custom_call_target="tpu_custom_call" | custom-call | bytes 10000000 | tf_op jit(solution)/shard_map/levels_kernel/pallas_call | solution.py:692
  38.7 0.2 collective-permute-done.6.above
  38.9 0.0 collective-permute-done.7.below
  38.9 1.4 %second_kernel.1 = (f32[12,2,8,640]{3,2,1,0:T(8,128)S(1)}, f32[8,2,8,640]{3,2,1,0:T(8,128)S(1)}, f32[8,1,8,640]{3,2,1,0:T(8,128)S(1)}, f32[3,1,8,640]{3,2,1,0:T(...) custom-call(f32[12,12,2,8,640]{4,3,2,1,0:T(8,128)S(1)} %get-tuple-element.52.c1, ...), custom_call_target="tpu_custom_call" | custom-call | tf_op jit(solution)/shard_map/second_kernel/pallas_call | solution.py:692
  40.3 0.0 collective-permute-start.8
  40.3 3.0 %collective-permute-start.9 = (f32[3,1,8,640]{3,2,1,0:T(8,128)S(1)}, f32[3,1,8,640]{3,2,1,0:T(8,128)S(1)}, u32[]{:S(2)}, u32[]{:S(2)}) collective-permute-start(f32[3,1,8,640]{3,2,1,0:T(8,128)S(1)} %get-tuple-element.60), channel_id=1, source_target_pairs={{0,112},{16,0},{32,16},{48,32},{64,48},{80,64},{96,80},{112,96},{1... | collective-permute-start | bytes 184328 | tf_op jit(solution)/shard_map/ppermute | solution.py:706
  43.3 1.8 %far_coarse_kernel.1.far = f32[2,12,1,8,640]{4,3,2,1,0:T(8,128)S(1)} custom-call(f32[4]{0:T(128)S(1)} %add_convert_fusion.ends, f32[22,8,2048]{2,1,0:T(8,128)S(1)} %collective-permute-done.2.rows_above, f32[22,8,2048]{2,1,0:T(8,128)S(1)} %collective-permute-done.3.rows_below, f32[2,2,24,128]{3,2,1,0:T(8,128)S(1)} %collective-permute-done.4.corner_above, ...), custom_call_target="tpu_custom_call" | custom-call | bytes 7000000 | tf_op jit(solution)/shard_map/far_coarse_kernel/pallas_call | solution.py:692
  45.1 0.1 collective-permute-done.8.above
  45.2 0.0 collective-permute-done.9.below
  45.2 1.8 %third_kernel.1 = (f32[8,2,8,640]{3,2,1,0:T(8,128)S(1)}, f32[2,2,8,640]{3,2,1,0:T(8,128)S(1)}, f32[2,2,8,640]{3,2,1,0:T(8,128)S(1)}) custom-call(f32[12,12,1,8,640]{4,3,2,1,0:T(8,128)S(1)} %get-tuple-element.53.c2.main, f32[12,12,2,8,640]{4,3,2,1,0:T(8,128)S(1)} %get-tuple-element.52.c1, f32[2,12,1,8,640]{4,3,2,1,0:T(8,128)S(1)} %far_coarse_kernel.1.far, ...), custom_call_target="tpu_custom_call" | custom-call | tf_op jit(solution)/shard_map/third_kernel/pallas_call | solution.py:692
  47.0 0.0 collective-permute-start.10
  47.0 3.0 %collective-permute-start.11 = (f32[2,2,8,640]{3,2,1,0:T(8,128)S(1)}, f32[2,2,8,640]{3,2,1,0:T(8,128)S(1)}, u32[]{:S(2)}, u32[]{:S(2)}) collective-permute-start(f32[2,2,8,640]{3,2,1,0:T(8,128)S(1)} %get-tuple-element.64), channel_id=1, source_target_pairs={{0,112},{16,0},{32,16},{48,32},{64,48},{80,64},{96,80},{112,96},{1... | collective-permute-start | bytes 245768 | tf_op jit(solution)/shard_map/ppermute | solution.py:706
  50.0 2.1 %collective-permute-done.10.above = f32[2,2,8,640]{3,2,1,0:T(8,128)S(1)} collective-permute-done((f32[2,2,8,640]{3,2,1,0:T(8,128)S(1)}, f32[2,2,8,640]{3,2,1,0:T(8,128)S(1)}, u32[]{:S(2)}, u32[]{:S(2)}) %collective-permute-start.10) | collective-permute-done | bytes 81952 | tf_op jit(solution)/shard_map/ppermute | solution.py:706
  52.1 0.0 collective-permute-done.11.below
  52.1 1.5 %fourth_kernel.1 = (f32[8,4,8,640]{3,2,1,0:T(8,128)S(1)}, f32[3,4,8,640]{3,2,1,0:T(8,128)S(1)}, f32[3,4,8,640]{3,2,1,0:T(8,128)S(1)}) custom-call(f32[12,12,2,8,640]{4,3,2,1,0:T(8,128)S(1)} %get-tuple-element.52.c1, f32[8,13,4,8,640]{4,3,2,1,0:T(8,128)S(1)} %get-tuple-element.42.main, f32[12,2,8,640]{3,2,1,0:T(8,128)S(1)} %get-tuple-element.57.t1, ...), custom_call_target="tpu_custom_call" | custom-call | tf_op jit(solution)/shard_map/fourth_kernel/pallas_call | solution.py:692
  53.6 0.0 collective-permute-start.12
  53.6 3.0 %collective-permute-start.13 = (f32[3,4,8,640]{3,2,1,0:T(8,128)S(1)}, f32[3,4,8,640]{3,2,1,0:T(8,128)S(1)}, u32[]{:S(2)}, u32[]{:S(2)}) collective-permute-start(f32[3,4,8,640]{3,2,1,0:T(8,128)S(1)} %get-tuple-element.68), channel_id=1, source_target_pairs={{0,112},{16,0},{32,16},{48,32},{64,48},{80,64},{96,80},{112,96},{1... | collective-permute-start | bytes 737288 | tf_op jit(solution)/shard_map/ppermute | solution.py:706
  56.6 2.1 %far_kernel.1 = (f32[2,13,4,8,640]{4,3,2,1,0:T(8,128)S(1)}, bf16[512,512]{1,0:T(8,128)(2,1)S(1)}) custom-call(f32[4]{0:T(128)S(1)} %add_convert_fusion.ends, f32[22,8,2048]{2,1,0:T(8,128)S(1)} %collective-permute-done.2.rows_above, f32[22,8,2048]{2,1,0:T(8,128)S(1)} %collective-permute-done.3.rows_below, ...), custom_call_target="tpu_custom_call" | custom-call | bytes 8000000 | tf_op jit(solution)/shard_map/far_kernel/pallas_call | solution.py:692
  58.8 1.7 %collective-permute-done.12.above = f32[3,4,8,640]{3,2,1,0:T(8,128)S(1)} collective-permute-done((f32[3,4,8,640]{3,2,1,0:T(8,128)S(1)}, f32[3,4,8,640]{3,2,1,0:T(8,128)S(1)}, u32[]{:S(2)}, u32[]{:S(2)}) %collective-permute-start.12) | collective-permute-done | bytes 245792 | tf_op jit(solution)/shard_map/ppermute | solution.py:706
  60.5 0.0 collective-permute-done.13.below
  60.5 5.0 %fifth_kernel.1 = (f32[56,2048]{1,0:T(8,128)}, f32[56,2048]{1,0:T(8,128)}, f32[8,128]{1,0:T(8,128)S(1)}) custom-call(f32[8,13,4,8,640]{4,3,2,1,0:T(8,128)S(1)} %get-tuple-element.42.main, f32[2,13,4,8,640]{4,3,2,1,0:T(8,128)S(1)} %get-tuple-element.50.near, f32[2,13,4,8,640]{4,3,2,1,0:T(8,128)S(1)} %get-tuple-element.51.far, ...), custom_call_target="tpu_custom_call" | custom-call | tf_op jit(solution)/shard_map/fifth_kernel/pallas_call | solution.py:692
  65.4 0.1 fusion
  65.6 17.8 %all_to_all.6 = f32[128,1,128]{2,1,0:T(1,128)S(1)} all-to-all(f32[128,1,128]{2,1,0:T(1,128)S(1)} %broadcast_in_dim.2), channel_id=1, replica_groups=mesh['hull'=8,'blk'=16] {'hull','blk'}, dimensions={0} | all-to-all | bytes 131072 | tf_op jit(solution)/shard_map/all_to_all | solution.py:713
  83.4 0.5 multiply_sqrt_fusion
  (5 shorter events, 0.1 us)
Async XLA Ops:
  0.6 14.2 %copy-start = (f32[7,7,8,2048]{3,2,1,0:T(8,128)S(1)}, f32[7,7,8,2048]{3,2,1,0:T(8,128)}, u32[]{:S(2)}) copy-start(f32[7,7,8,2048]{3,2,1,0:T(8,128)} %param.5) | copy-start | bytes 9633796
  0.6 14.2 %copy-start.1 = (f32[4,7,8,2048]{3,2,1,0:T(8,128)S(1)}, f32[4,7,8,2048]{3,2,1,0:T(8,128)}, u32[]{:S(2)}) copy-start(f32[4,7,8,2048]{3,2,1,0:T(8,128)} %param.6) | copy-start | bytes 5505028
  0.7 14.2 %copy-start.2 = (f32[7,8,2048]{2,1,0:T(8,128)S(1)}, f32[7,8,2048]{2,1,0:T(8,128)}, u32[]{:S(2)}) copy-start(f32[7,8,2048]{2,1,0:T(8,128)} %param.4) | copy-start | bytes 1376260
  0.7 14.2 %copy-start.3 = (s32[8,2048]{1,0:T(8,128)S(1)}, s32[8,2048]{1,0:T(8,128)}, u32[]{:S(2)}) copy-start(s32[8,2048]{1,0:T(8,128)} %act.3) | copy-start | bytes 196612
  5.5 23.9 %collective-permute-start.2 = (f32[22,8,2048]{2,1,0:T(8,128)}, f32[22,8,2048]{2,1,0:T(8,128)S(1)}, u32[]{:S(2)}, u32[]{:S(2)}) collective-permute-start(f32[22,8,2048]{2,1,0:T(8,128)} %get-tuple-element.43), channel_id=1, source_target_pairs={{0,16},{16,32},{32,48},{48,64},{64,80},{80,96},{96,112},{112,0},{1... | collective-permute-start | bytes 4325384 | tf_op jit(solution)/shard_map/ppermute | solution.py:706
  5.5 23.8 %collective-permute-start.3 = (f32[22,8,2048]{2,1,0:T(8,128)}, f32[22,8,2048]{2,1,0:T(8,128)S(1)}, u32[]{:S(2)}, u32[]{:S(2)}) collective-permute-start(f32[22,8,2048]{2,1,0:T(8,128)} %get-tuple-element.44), channel_id=1, source_target_pairs={{0,112},{16,0},{32,16},{48,32},{64,48},{80,64},{96,80},{112,96},{1... | collective-permute-start | bytes 4325384 | tf_op jit(solution)/shard_map/ppermute | solution.py:706
  8.5 13.0 %collective-permute-start = (f32[176,128]{1,0:T(8,128)S(1)}, f32[176,128]{1,0:T(8,128)S(1)}, u32[]{:S(2)}, u32[]{:S(2)}) collective-permute-start(f32[176,128]{1,0:T(8,128)S(1)} %get-tuple-element.39), channel_id=1, source_target_pairs={{0,15},{1,0},{2,1},{3,2},{4,3},{5,4},{6,5},{7,6},{8,7},{9,8},{10,9... | collective-permute-start | bytes 270344 | tf_op jit(solution)/shard_map/ppermute | solution.py:706
  14.8 7.8 %collective-permute-start.1 = (f32[176,128]{1,0:T(8,128)S(1)}, f32[176,128]{1,0:T(8,128)S(1)}, u32[]{:S(2)}, u32[]{:S(2)}) collective-permute-start(f32[176,128]{1,0:T(8,128)S(1)} %get-tuple-element.40), channel_id=1, source_target_pairs={{0,1},{1,2},{2,3},{3,4},{4,5},{5,6},{6,7},{7,8},{8,9},{9,10},{10,1... | collective-permute-start | bytes 270344 | tf_op jit(solution)/shard_map/ppermute | solution.py:706
  22.7 6.7 %collective-permute-start.4 = (f32[2,2,24,128]{3,2,1,0:T(8,128)S(1)}, f32[2,2,24,128]{3,2,1,0:T(8,128)S(1)}, u32[]{:S(2)}, u32[]{:S(2)}) collective-permute-start(f32[2,2,24,128]{3,2,1,0:T(8,128)S(1)} %get-tuple-element.46), channel_id=1, source_target_pairs={{0,16},{16,32},{32,48},{48,64},{64,80},{80,96},{96,112},{112,0},{1... | collective-permute-start | bytes 147464 | tf_op jit(solution)/shard_map/ppermute | solution.py:706
  22.7 6.7 %collective-permute-start.5 = (f32[2,2,24,128]{3,2,1,0:T(8,128)S(1)}, f32[2,2,24,128]{3,2,1,0:T(8,128)S(1)}, u32[]{:S(2)}, u32[]{:S(2)}) collective-permute-start(f32[2,2,24,128]{3,2,1,0:T(8,128)S(1)} %get-tuple-element.47), channel_id=1, source_target_pairs={{0,112},{16,0},{32,16},{48,32},{64,48},{80,64},{96,80},{112,96},{1... | collective-permute-start | bytes 147464 | tf_op jit(solution)/shard_map/ppermute | solution.py:706
  33.8 5.1 %collective-permute-start.6 = (f32[2,2,8,640]{3,2,1,0:T(8,128)S(1)}, f32[2,2,8,640]{3,2,1,0:T(8,128)S(1)}, u32[]{:S(2)}, u32[]{:S(2)}) collective-permute-start(f32[2,2,8,640]{3,2,1,0:T(8,128)S(1)} %get-tuple-element.55), channel_id=1, source_target_pairs={{0,16},{16,32},{32,48},{48,64},{64,80},{80,96},{96,112},{112,0},{1... | collective-permute-start | bytes 245768 | tf_op jit(solution)/shard_map/ppermute | solution.py:706
  33.8 5.1 %collective-permute-start.7 = (f32[2,2,8,640]{3,2,1,0:T(8,128)S(1)}, f32[2,2,8,640]{3,2,1,0:T(8,128)S(1)}, u32[]{:S(2)}, u32[]{:S(2)}) collective-permute-start(f32[2,2,8,640]{3,2,1,0:T(8,128)S(1)} %get-tuple-element.56), channel_id=1, source_target_pairs={{0,112},{16,0},{32,16},{48,32},{64,48},{80,64},{96,80},{112,96},{1... | collective-permute-start | bytes 245768 | tf_op jit(solution)/shard_map/ppermute | solution.py:706
  40.3 4.9 %collective-permute-start.8 = (f32[3,1,8,640]{3,2,1,0:T(8,128)S(1)}, f32[3,1,8,640]{3,2,1,0:T(8,128)S(1)}, u32[]{:S(2)}, u32[]{:S(2)}) collective-permute-start(f32[3,1,8,640]{3,2,1,0:T(8,128)S(1)} %get-tuple-element.59), channel_id=1, source_target_pairs={{0,16},{16,32},{32,48},{48,64},{64,80},{80,96},{96,112},{112,0},{1... | collective-permute-start | bytes 184328 | tf_op jit(solution)/shard_map/ppermute | solution.py:706
  40.3 4.8 %collective-permute-start.9 = (f32[3,1,8,640]{3,2,1,0:T(8,128)S(1)}, f32[3,1,8,640]{3,2,1,0:T(8,128)S(1)}, u32[]{:S(2)}, u32[]{:S(2)}) collective-permute-start(f32[3,1,8,640]{3,2,1,0:T(8,128)S(1)} %get-tuple-element.60), channel_id=1, source_target_pairs={{0,112},{16,0},{32,16},{48,32},{64,48},{80,64},{96,80},{112,96},{1... | collective-permute-start | bytes 184328 | tf_op jit(solution)/shard_map/ppermute | solution.py:706
  47.0 5.1 %collective-permute-start.10 = (f32[2,2,8,640]{3,2,1,0:T(8,128)S(1)}, f32[2,2,8,640]{3,2,1,0:T(8,128)S(1)}, u32[]{:S(2)}, u32[]{:S(2)}) collective-permute-start(f32[2,2,8,640]{3,2,1,0:T(8,128)S(1)} %get-tuple-element.63), channel_id=1, source_target_pairs={{0,16},{16,32},{32,48},{48,64},{64,80},{80,96},{96,112},{112,0},{1... | collective-permute-start | bytes 245768 | tf_op jit(solution)/shard_map/ppermute | solution.py:706
  47.0 5.1 %collective-permute-start.11 = (f32[2,2,8,640]{3,2,1,0:T(8,128)S(1)}, f32[2,2,8,640]{3,2,1,0:T(8,128)S(1)}, u32[]{:S(2)}, u32[]{:S(2)}) collective-permute-start(f32[2,2,8,640]{3,2,1,0:T(8,128)S(1)} %get-tuple-element.64), channel_id=1, source_target_pairs={{0,112},{16,0},{32,16},{48,32},{64,48},{80,64},{96,80},{112,96},{1... | collective-permute-start | bytes 245768 | tf_op jit(solution)/shard_map/ppermute | solution.py:706
  53.6 6.9 %collective-permute-start.12 = (f32[3,4,8,640]{3,2,1,0:T(8,128)S(1)}, f32[3,4,8,640]{3,2,1,0:T(8,128)S(1)}, u32[]{:S(2)}, u32[]{:S(2)}) collective-permute-start(f32[3,4,8,640]{3,2,1,0:T(8,128)S(1)} %get-tuple-element.67), channel_id=1, source_target_pairs={{0,16},{16,32},{32,48},{48,64},{64,80},{80,96},{96,112},{112,0},{1... | collective-permute-start | bytes 737288 | tf_op jit(solution)/shard_map/ppermute | solution.py:706
  53.6 6.8 %collective-permute-start.13 = (f32[3,4,8,640]{3,2,1,0:T(8,128)S(1)}, f32[3,4,8,640]{3,2,1,0:T(8,128)S(1)}, u32[]{:S(2)}, u32[]{:S(2)}) collective-permute-start(f32[3,4,8,640]{3,2,1,0:T(8,128)S(1)} %get-tuple-element.68), channel_id=1, source_target_pairs={{0,112},{16,0},{32,16},{48,32},{64,48},{80,64},{96,80},{112,96},{1... | collective-permute-start | bytes 737288 | tf_op jit(solution)/shard_map/ppermute | solution.py:706

commit v5 on v4

--- a/solution.py
+++ b/solution.py
@@ -503,7 +503,7 @@
         out[n // blocks, n % blocks] = x[n * size : n * size + size]
 
 
-def first_kernel(ends, main, rows_above, rows_below, corner_above, corner_below, order, order_side, near, v2, t1, t1_top, t1_bottom, sums, va, vb, prods, rows):
+def first_kernel(ends, main, rows_above, rows_below, corner_above, corner_below, order, order_side, near, vb, t1, t1_top, t1_bottom, sums, va, prods, rows):
     tiles = main.shape[-1] // T
     c0 = FineRows(main, near)
     t0 = SourceOf(c0)
@@ -561,7 +561,6 @@
                 diff = t0[r, p, :, sl] - out
                 res.append(jnp.where(c0[r, SWEEP_W, p, :, sl] != 0.0, diff, 0.0))
                 total = total + res[p] * res[p]
-                v2[r - WIDE, p, :, sl] = vb[r, p, :, sl]
             row = r - WIDE
             if row in (1, ROWS - 2):
                 coarse = merge([[c0[r, k, p, :, sl] for p in range(PHASES)] for k in range(PLANES - 1)])
@@ -579,7 +578,7 @@
     each(tiles, rest)
 
 
-def second_kernel(c1, c2, t1_own, above, below, t1, e1, t2, top, bottom, sums, va, vb):
+def second_kernel(c1, c2, t1_own, above, below, t1, vb, t2, top, bottom, sums, va):
     tiles = c1.shape[-1] // T
 
     def fill(j):
@@ -599,8 +598,6 @@
         for r in range(WIDE, WIDE + ROWS):
             res = [t1[r, p, :, sl] - out for p, out in enumerate(apply_at(c1, r, vb, j))]
             total = total + res[0] * res[0] + res[1] * res[1]
-            for p in range(2):
-                e1[r - WIDE, p, :, sl] = vb[r, p, :, sl]
             val = res[0] + res[1]
             t2[r - WIDE, 0, :, sl] = val
 
@@ -632,7 +629,7 @@
         sl = tile(j)
         for r in range(WIDE, WIDE + ROWS):
             for p in range(2):
-                val = e1_in[r - WIDE, p, :, sl] + vb[r, 0, :, sl]
+                val = e1_in[r, p, :, sl] + vb[r, 0, :, sl]
                 e1[r - WIDE, p, :, sl] = val
                 send_rows(top, bottom, r - WIDE, p, sl, val, 1, lambda k: c1[r, k, p, :, sl] * val)
 
@@ -650,7 +647,7 @@
         for r in range(ROWS):
             for p in range(PHASES):
                 add = jnp.where(main[r, SWEEP_W, p, :, sl] != 0.0, va[r + WIDE, p // 2, :, sl], 0.0)
-                val = v2[r, p, :, sl] + add
+                val = v2[r + WIDE, p, :, sl] + add
                 v[r, p, :, sl] = val
                 send_rows(top, bottom, r, p, sl, val, WIDE, lambda k: main[r, k, p, :, sl] * val)
 
@@ -785,9 +782,9 @@
     )
     near, v2, t1, top, bottom, sum0 = call(
         first_kernel,
-        [coefs(2, FINE, 4), cells(ROWS, 4), cells(ROWS, 2), cells(2, 2), cells(2, 2), sum_tile],
+        [coefs(2, FINE, 4), cells(EXT, 4), cells(ROWS, 2), cells(2, 2), cells(2, 2), sum_tile],
         [ends, main, rows_above, rows_below, corner_above, corner_below, own, side],
-        [cells(EXT, 4), cells(EXT, 4), cells(2, 4), (2, blocks, PLANES * 8, BLOCK)],
+        [cells(EXT, 4), cells(2, 4), (2, blocks, PLANES * 8, BLOCK)],
         flag,
     )
     below = ring(top, "hull", -1)
@@ -811,9 +808,9 @@
     c1, c2 = call(levels_kernel, [coefs(EXT, PLANES, 2), coefs(EXT, PLANES, 1)], [ends, main, near], (), flag, size=10**7)
     t1, e1, t2, top, bottom, sum1 = call(
         second_kernel,
-        [cells(EXT, 2), cells(ROWS, 2), cells(ROWS, 1), cells(3, 1), cells(3, 1), sum_tile],
+        [cells(EXT, 2), cells(EXT, 2), cells(ROWS, 1), cells(3, 1), cells(3, 1), sum_tile],
         [c1, c2, t1, above, below],
-        [cells(EXT, 2)] * 2,
+        [cells(EXT, 2)],
     )
     below = ring(top, "hull", -1)
     above = ring(bottom, "hull", 1)

time: 84.5 us -> 84.2 us (level)
  no operation moved by 1% of the time
where the time goes in v5:
time: 84.2 us; the launch traced here: 83.7 us
  Pallas kernels  34.7 us (41%)
  starting transfers between devices  24.2 us (29%)
  blocking collectives  17.8 us (21%)
  waiting for transfers between devices  5.28 us (6%)
  between operations  0.87 us (1%)
    pallas_call x12, Pallas kernels, call(): pl.pallas_call(kernel, out_shape=[jax.ShapeDtypeStruct(s, F32) if isinsta...  34.7 us
    ppermute x14, starting transfers between devices, ring(): lax.ppermute(x, axis, [(i, (i + step) % count) for i in range(count)])  24.2 us
    all_to_all x1, blocking collectives, total_over_devices(): lax.all_to_all(sent, axes, 0, 0, tiled=True)  17.8 us
    ppermute x14, waiting for transfers between devices, ring(): lax.ppermute(x, axis, [(i, (i + step) % count) for i in range(count)])  5.28 us
  transfers between devices with their start and end apart: 14, of which 5 were waited for; matrix products, arithmetic and copies ran while one was open for 0% of the time, Pallas kernels for 19%

profile of v5, /device:TPU:0, one launch (start us, length us, event | category | flops | bytes accessed | tf_op | source)
XLA Modules:
  0.0 83.7 jit_solution(3053106303797270800)
XLA Ops:
  0.6 0.0 copy-start
  0.6 0.0 copy-start.1
  0.7 0.0 copy-start.2
  0.7 0.0 copy-start.3
  0.7 4.8 %send_kernel.1 = (f32[22,8,2048]{2,1,0:T(8,128)}, f32[22,8,2048]{2,1,0:T(8,128)}, f32[176,128]{1,0:T(8,128)S(1)}, f32[176,128]{1,0:T(8,128)S(1)}) custom-call(f32[7,56,2048]{2,1,0:T(8,128)} %bitcast.14, f32[4,56,2048]{2,1,0:T(8,128)} %bitcast.16, f32[56,2048]{1,0:T(8,128)} %bitcast.18, s32[8,2048]{1,0:T(8,128)} %act.3), custom_call_target="tpu_custom_call" | custom-call | tf_op jit(solution)/shard_map/send_kernel/pallas_call | solution.py:689
  5.5 0.0 collective-permute-start.2
  5.5 2.9 %collective-permute-start.3 = (f32[22,8,2048]{2,1,0:T(8,128)}, f32[22,8,2048]{2,1,0:T(8,128)S(1)}, u32[]{:S(2)}, u32[]{:S(2)}) collective-permute-start(f32[22,8,2048]{2,1,0:T(8,128)} %get-tuple-element.44), channel_id=1, source_target_pairs={{0,112},{16,0},{32,16},{48,32},{64,48},{80,64},{96,80},{112,96},{1... | collective-permute-start | bytes 4325384 | tf_op jit(solution)/shard_map/ppermute | solution.py:703
  8.5 6.3 %collective-permute-start = (f32[176,128]{1,0:T(8,128)S(1)}, f32[176,128]{1,0:T(8,128)S(1)}, u32[]{:S(2)}, u32[]{:S(2)}) collective-permute-start(f32[176,128]{1,0:T(8,128)S(1)} %get-tuple-element.39), channel_id=1, source_target_pairs={{0,15},{1,0},{2,1},{3,2},{4,3},{5,4},{6,5},{7,6},{8,7},{9,8},{10,9... | collective-permute-start | bytes 270344 | tf_op jit(solution)/shard_map/ppermute | solution.py:703
  14.8 0.0 collective-permute-start.1
  14.8 0.0 copy-done
  14.8 0.0 copy-done.1
  14.8 0.0 copy-done.2
  14.8 0.0 copy-done.3
  14.8 6.6 %own_kernel.1 = (f32[8,13,4,8,512]{4,3,2,1,0:T(8,128)}, f32[8,128]{1,0:T(8,128)S(1)}) custom-call(f32[7,56,2048]{2,1,0:T(8,128)S(1)} %bitcast.15, f32[4,56,2048]{2,1,0:T(8,128)S(1)} %bitcast.17, f32[56,2048]{1,0:T(8,128)S(1)} %bitcast.19, s32[8,2048]{1,0:T(8,128)S(1)} %copy-done.3), custom_call_target="tpu_custom_call" | custom-call | bytes 25000000 | tf_op jit(solution)/shard_map/own_kernel/pallas_call | solution.py:689
  21.4 0.0 collective-permute-done.from_right
  21.5 1.2 %collective-permute-done.1.from_left = f32[176,128]{1,0:T(8,128)S(1)} collective-permute-done((f32[176,128]{1,0:T(8,128)S(1)}, f32[176,128]{1,0:T(8,128)S(1)}, u32[]{:S(2)}, u32[]{:S(2)}) %collective-permute-start.1) | collective-permute-done | bytes 90144 | tf_op jit(solution)/shard_map/ppermute | solution.py:703
  22.7 0.0 collective-permute-start.4
  22.7 2.9 %collective-permute-start.5 = (f32[2,2,24,128]{3,2,1,0:T(8,128)S(1)}, f32[2,2,24,128]{3,2,1,0:T(8,128)S(1)}, u32[]{:S(2)}, u32[]{:S(2)}) collective-permute-start(f32[2,2,24,128]{3,2,1,0:T(8,128)S(1)} %get-tuple-element.47), channel_id=1, source_target_pairs={{0,112},{16,0},{32,16},{48,32},{64,48},{80,64},{96,80},{112,96},{1... | collective-permute-start | bytes 147464 | tf_op jit(solution)/shard_map/ppermute | solution.py:703
  25.6 0.1 add_convert_fusion.ends
  25.7 3.6 %side_kernel.1 = (f32[8,13,4,8,640]{4,3,2,1,0:T(8,128)S(1)}, bf16[512,512]{1,0:T(8,128)(2,1)S(1)}, bf16[256,512]{1,0:T(8,128)(2,1)S(1)}) custom-call(f32[4]{0:T(128)S(1)} %add_convert_fusion.ends, f32[176,128]{1,0:T(8,128)S(1)} %collective-permute-done.from_right, f32[176,128]{1,0:T(8,128)S(1)} %collective-permute-done.1.from_left, ...), custom_call_target="tpu_custom_call" | custom-call | bytes 9000000 | tf_op jit(solution)/shard_map/side_kernel/pallas_call | solution.py:689
  29.3 0.0 collective-permute-done.4.corner_above
  29.4 0.0 collective-permute-done.5.corner_below
  29.4 0.0 collective-permute-done.2.rows_above
  29.4 0.0 collective-permute-done.3.rows_below
  29.4 4.2 %first_kernel.1 = (f32[2,13,4,8,640]{4,3,2,1,0:T(8,128)S(1)}, f32[12,4,8,640]{3,2,1,0:T(8,128)S(1)}, f32[8,2,8,640]{3,2,1,0:T(8,128)S(1)}, f32[2,2,8,640]{3,2,1,...) custom-call(f32[4]{0:T(128)S(1)} %add_convert_fusion.ends, ...), custom_call_target="tpu_custom_call" | custom-call | tf_op jit(solution)/shard_map/first_kernel/pallas_call | solution.py:689
  33.6 0.0 collective-permute-start.6
  33.6 2.9 %collective-permute-start.7 = (f32[2,2,8,640]{3,2,1,0:T(8,128)S(1)}, f32[2,2,8,640]{3,2,1,0:T(8,128)S(1)}, u32[]{:S(2)}, u32[]{:S(2)}) collective-permute-start(f32[2,2,8,640]{3,2,1,0:T(8,128)S(1)} %get-tuple-element.56), channel_id=1, source_target_pairs={{0,112},{16,0},{32,16},{48,32},{64,48},{80,64},{96,80},{112,96},{1... | collective-permute-start | bytes 245768 | tf_op jit(solution)/shard_map/ppermute | solution.py:703
  36.6 1.9 %levels_kernel.1 = (f32[12,12,2,8,640]{4,3,2,1,0:T(8,128)S(1)}, f32[12,12,1,8,640]{4,3,2,1,0:T(8,128)S(1)}) custom-call(f32[4]{0:T(128)S(1)} %add_convert_fusion.ends, f32[8,13,4,8,640]{4,3,2,1,0:T(8,128)S(1)} %get-tuple-element.42.main, f32[2,13,4,8,640]{4,3,2,1,0:T(8,128)S(1)} %get-tuple-element.50.near), custom_call_target="tpu_custom_call" | custom-call | bytes 10000000 | tf_op jit(solution)/shard_map/levels_kernel/pallas_call | solution.py:689
  38.5 0.2 collective-permute-done.6.above
  38.7 0.0 collective-permute-done.7.below
  38.7 1.3 %second_kernel.1 = (f32[12,2,8,640]{3,2,1,0:T(8,128)S(1)}, f32[12,2,8,640]{3,2,1,0:T(8,128)S(1)}, f32[8,1,8,640]{3,2,1,0:T(8,128)S(1)}, f32[3,1,8,640]{3,2,1,0:T...) custom-call(f32[12,12,2,8,640]{4,3,2,1,0:T(8,128)S(1)} %get-tuple-element.52.c1, ...), custom_call_target="tpu_custom_call" | custom-call | tf_op jit(solution)/shard_map/second_kernel/pallas_call | solution.py:689
  40.1 0.0 collective-permute-start.8
  40.1 3.0 %collective-permute-start.9 = (f32[3,1,8,640]{3,2,1,0:T(8,128)S(1)}, f32[3,1,8,640]{3,2,1,0:T(8,128)S(1)}, u32[]{:S(2)}, u32[]{:S(2)}) collective-permute-start(f32[3,1,8,640]{3,2,1,0:T(8,128)S(1)} %get-tuple-element.60), channel_id=1, source_target_pairs={{0,112},{16,0},{32,16},{48,32},{64,48},{80,64},{96,80},{112,96},{1... | collective-permute-start | bytes 184328 | tf_op jit(solution)/shard_map/ppermute | solution.py:703
  43.0 1.8 %far_coarse_kernel.1.far = f32[2,12,1,8,640]{4,3,2,1,0:T(8,128)S(1)} custom-call(f32[4]{0:T(128)S(1)} %add_convert_fusion.ends, f32[22,8,2048]{2,1,0:T(8,128)S(1)} %collective-permute-done.2.rows_above, f32[22,8,2048]{2,1,0:T(8,128)S(1)} %collective-permute-done.3.rows_below, f32[2,2,24,128]{3,2,1,0:T(8,128)S(1)} %collective-permute-done.4.corner_above, ...), custom_call_target="tpu_custom_call" | custom-call | bytes 7000000 | tf_op jit(solution)/shard_map/far_coarse_kernel/pallas_call | solution.py:689
  44.9 0.1 collective-permute-done.8.above
  44.9 0.0 collective-permute-done.9.below
  44.9 1.8 %third_kernel.1 = (f32[8,2,8,640]{3,2,1,0:T(8,128)S(1)}, f32[2,2,8,640]{3,2,1,0:T(8,128)S(1)}, f32[2,2,8,640]{3,2,1,0:T(8,128)S(1)}) custom-call(f32[12,12,1,8,640]{4,3,2,1,0:T(8,128)S(1)} %get-tuple-element.53.c2.main, f32[12,12,2,8,640]{4,3,2,1,0:T(8,128)S(1)} %get-tuple-element.52.c1, f32[2,12,1,8,640]{4,3,2,1,0:T(8,128)S(1)} %far_coarse_kernel.1.far, ...), custom_call_target="tpu_custom_call" | custom-call | tf_op jit(solution)/shard_map/third_kernel/pallas_call | solution.py:689
  46.8 0.0 collective-permute-start.10
  46.8 3.0 %collective-permute-start.11 = (f32[2,2,8,640]{3,2,1,0:T(8,128)S(1)}, f32[2,2,8,640]{3,2,1,0:T(8,128)S(1)}, u32[]{:S(2)}, u32[]{:S(2)}) collective-permute-start(f32[2,2,8,640]{3,2,1,0:T(8,128)S(1)} %get-tuple-element.64), channel_id=1, source_target_pairs={{0,112},{16,0},{32,16},{48,32},{64,48},{80,64},{96,80},{112,96},{1... | collective-permute-start | bytes 245768 | tf_op jit(solution)/shard_map/ppermute | solution.py:703
  49.8 2.1 %collective-permute-done.10.above = f32[2,2,8,640]{3,2,1,0:T(8,128)S(1)} collective-permute-done((f32[2,2,8,640]{3,2,1,0:T(8,128)S(1)}, f32[2,2,8,640]{3,2,1,0:T(8,128)S(1)}, u32[]{:S(2)}, u32[]{:S(2)}) %collective-permute-start.10) | collective-permute-done | bytes 81952 | tf_op jit(solution)/shard_map/ppermute | solution.py:703
  51.9 0.0 collective-permute-done.11.below
  51.9 1.5 %fourth_kernel.1 = (f32[8,4,8,640]{3,2,1,0:T(8,128)S(1)}, f32[3,4,8,640]{3,2,1,0:T(8,128)S(1)}, f32[3,4,8,640]{3,2,1,0:T(8,128)S(1)}) custom-call(f32[12,12,2,8,640]{4,3,2,1,0:T(8,128)S(1)} %get-tuple-element.52.c1, f32[8,13,4,8,640]{4,3,2,1,0:T(8,128)S(1)} %get-tuple-element.42.main, f32[12,2,8,640]{3,2,1,0:T(8,128)S(1)} %get-tuple-element.57.t1, ...), custom_call_target="tpu_custom_call" | custom-call | tf_op jit(solution)/shard_map/fourth_kernel/pallas_call | solution.py:689
  53.4 0.0 collective-permute-start.12
  53.4 3.0 %collective-permute-start.13 = (f32[3,4,8,640]{3,2,1,0:T(8,128)S(1)}, f32[3,4,8,640]{3,2,1,0:T(8,128)S(1)}, u32[]{:S(2)}, u32[]{:S(2)}) collective-permute-start(f32[3,4,8,640]{3,2,1,0:T(8,128)S(1)} %get-tuple-element.68), channel_id=1, source_target_pairs={{0,112},{16,0},{32,16},{48,32},{64,48},{80,64},{96,80},{112,96},{1... | collective-permute-start | bytes 737288 | tf_op jit(solution)/shard_map/ppermute | solution.py:703
  56.4 2.1 %far_kernel.1 = (f32[2,13,4,8,640]{4,3,2,1,0:T(8,128)S(1)}, bf16[512,512]{1,0:T(8,128)(2,1)S(1)}) custom-call(f32[4]{0:T(128)S(1)} %add_convert_fusion.ends, f32[22,8,2048]{2,1,0:T(8,128)S(1)} %collective-permute-done.2.rows_above, f32[22,8,2048]{2,1,0:T(8,128)S(1)} %collective-permute-done.3.rows_below, ...), custom_call_target="tpu_custom_call" | custom-call | bytes 8000000 | tf_op jit(solution)/shard_map/far_kernel/pallas_call | solution.py:689
  58.5 1.7 %collective-permute-done.12.above = f32[3,4,8,640]{3,2,1,0:T(8,128)S(1)} collective-permute-done((f32[3,4,8,640]{3,2,1,0:T(8,128)S(1)}, f32[3,4,8,640]{3,2,1,0:T(8,128)S(1)}, u32[]{:S(2)}, u32[]{:S(2)}) %collective-permute-start.12) | collective-permute-done | bytes 245792 | tf_op jit(solution)/shard_map/ppermute | solution.py:703
  60.2 0.0 collective-permute-done.13.below
  60.2 4.9 %fifth_kernel.1 = (f32[56,2048]{1,0:T(8,128)}, f32[56,2048]{1,0:T(8,128)}, f32[8,128]{1,0:T(8,128)S(1)}) custom-call(f32[8,13,4,8,640]{4,3,2,1,0:T(8,128)S(1)} %get-tuple-element.42.main, f32[2,13,4,8,640]{4,3,2,1,0:T(8,128)S(1)} %get-tuple-element.50.near, f32[2,13,4,8,640]{4,3,2,1,0:T(8,128)S(1)} %get-tuple-element.51.far, ...), custom_call_target="tpu_custom_call" | custom-call | tf_op jit(solution)/shard_map/fifth_kernel/pallas_call | solution.py:689
  65.2 0.1 fusion
  65.3 17.8 %all_to_all.6 = f32[128,1,128]{2,1,0:T(1,128)S(1)} all-to-all(f32[128,1,128]{2,1,0:T(1,128)S(1)} %broadcast_in_dim.2), channel_id=1, replica_groups=mesh['hull'=8,'blk'=16] {'hull','blk'}, dimensions={0} | all-to-all | bytes 131072 | tf_op jit(solution)/shard_map/all_to_all | solution.py:710
  83.1 0.5 multiply_sqrt_fusion
  (5 shorter events, 0.1 us)
Async XLA Ops:
  0.6 14.2 %copy-start = (f32[7,7,8,2048]{3,2,1,0:T(8,128)S(1)}, f32[7,7,8,2048]{3,2,1,0:T(8,128)}, u32[]{:S(2)}) copy-start(f32[7,7,8,2048]{3,2,1,0:T(8,128)} %param.5) | copy-start | bytes 9633796
  0.6 14.2 %copy-start.1 = (f32[4,7,8,2048]{3,2,1,0:T(8,128)S(1)}, f32[4,7,8,2048]{3,2,1,0:T(8,128)}, u32[]{:S(2)}) copy-start(f32[4,7,8,2048]{3,2,1,0:T(8,128)} %param.6) | copy-start | bytes 5505028
  0.7 14.2 %copy-start.2 = (f32[7,8,2048]{2,1,0:T(8,128)S(1)}, f32[7,8,2048]{2,1,0:T(8,128)}, u32[]{:S(2)}) copy-start(f32[7,8,2048]{2,1,0:T(8,128)} %param.4) | copy-start | bytes 1376260
  0.7 14.2 %copy-start.3 = (s32[8,2048]{1,0:T(8,128)S(1)}, s32[8,2048]{1,0:T(8,128)}, u32[]{:S(2)}) copy-start(s32[8,2048]{1,0:T(8,128)} %act.3) | copy-start | bytes 196612
  5.5 23.9 %collective-permute-start.2 = (f32[22,8,2048]{2,1,0:T(8,128)}, f32[22,8,2048]{2,1,0:T(8,128)S(1)}, u32[]{:S(2)}, u32[]{:S(2)}) collective-permute-start(f32[22,8,2048]{2,1,0:T(8,128)} %get-tuple-element.43), channel_id=1, source_target_pairs={{0,16},{16,32},{32,48},{48,64},{64,80},{80,96},{96,112},{112,0},{1... | collective-permute-start | bytes 4325384 | tf_op jit(solution)/shard_map/ppermute | solution.py:703
  5.5 23.8 %collective-permute-start.3 = (f32[22,8,2048]{2,1,0:T(8,128)}, f32[22,8,2048]{2,1,0:T(8,128)S(1)}, u32[]{:S(2)}, u32[]{:S(2)}) collective-permute-start(f32[22,8,2048]{2,1,0:T(8,128)} %get-tuple-element.44), channel_id=1, source_target_pairs={{0,112},{16,0},{32,16},{48,32},{64,48},{80,64},{96,80},{112,96},{1... | collective-permute-start | bytes 4325384 | tf_op jit(solution)/shard_map/ppermute | solution.py:703
  8.5 13.0 %collective-permute-start = (f32[176,128]{1,0:T(8,128)S(1)}, f32[176,128]{1,0:T(8,128)S(1)}, u32[]{:S(2)}, u32[]{:S(2)}) collective-permute-start(f32[176,128]{1,0:T(8,128)S(1)} %get-tuple-element.39), channel_id=1, source_target_pairs={{0,15},{1,0},{2,1},{3,2},{4,3},{5,4},{6,5},{7,6},{8,7},{9,8},{10,9... | collective-permute-start | bytes 270344 | tf_op jit(solution)/shard_map/ppermute | solution.py:703
  14.8 7.8 %collective-permute-start.1 = (f32[176,128]{1,0:T(8,128)S(1)}, f32[176,128]{1,0:T(8,128)S(1)}, u32[]{:S(2)}, u32[]{:S(2)}) collective-permute-start(f32[176,128]{1,0:T(8,128)S(1)} %get-tuple-element.40), channel_id=1, source_target_pairs={{0,1},{1,2},{2,3},{3,4},{4,5},{5,6},{6,7},{7,8},{8,9},{9,10},{10,1... | collective-permute-start | bytes 270344 | tf_op jit(solution)/shard_map/ppermute | solution.py:703
  22.7 6.7 %collective-permute-start.4 = (f32[2,2,24,128]{3,2,1,0:T(8,128)S(1)}, f32[2,2,24,128]{3,2,1,0:T(8,128)S(1)}, u32[]{:S(2)}, u32[]{:S(2)}) collective-permute-start(f32[2,2,24,128]{3,2,1,0:T(8,128)S(1)} %get-tuple-element.46), channel_id=1, source_target_pairs={{0,16},{16,32},{32,48},{48,64},{64,80},{80,96},{96,112},{112,0},{1... | collective-permute-start | bytes 147464 | tf_op jit(solution)/shard_map/ppermute | solution.py:703
  22.7 6.7 %collective-permute-start.5 = (f32[2,2,24,128]{3,2,1,0:T(8,128)S(1)}, f32[2,2,24,128]{3,2,1,0:T(8,128)S(1)}, u32[]{:S(2)}, u32[]{:S(2)}) collective-permute-start(f32[2,2,24,128]{3,2,1,0:T(8,128)S(1)} %get-tuple-element.47), channel_id=1, source_target_pairs={{0,112},{16,0},{32,16},{48,32},{64,48},{80,64},{96,80},{112,96},{1... | collective-permute-start | bytes 147464 | tf_op jit(solution)/shard_map/ppermute | solution.py:703
  33.6 5.1 %collective-permute-start.6 = (f32[2,2,8,640]{3,2,1,0:T(8,128)S(1)}, f32[2,2,8,640]{3,2,1,0:T(8,128)S(1)}, u32[]{:S(2)}, u32[]{:S(2)}) collective-permute-start(f32[2,2,8,640]{3,2,1,0:T(8,128)S(1)} %get-tuple-element.55), channel_id=1, source_target_pairs={{0,16},{16,32},{32,48},{48,64},{64,80},{80,96},{96,112},{112,0},{1... | collective-permute-start | bytes 245768 | tf_op jit(solution)/shard_map/ppermute | solution.py:703
  33.6 5.1 %collective-permute-start.7 = (f32[2,2,8,640]{3,2,1,0:T(8,128)S(1)}, f32[2,2,8,640]{3,2,1,0:T(8,128)S(1)}, u32[]{:S(2)}, u32[]{:S(2)}) collective-permute-start(f32[2,2,8,640]{3,2,1,0:T(8,128)S(1)} %get-tuple-element.56), channel_id=1, source_target_pairs={{0,112},{16,0},{32,16},{48,32},{64,48},{80,64},{96,80},{112,96},{1... | collective-permute-start | bytes 245768 | tf_op jit(solution)/shard_map/ppermute | solution.py:703
  40.1 4.9 %collective-permute-start.8 = (f32[3,1,8,640]{3,2,1,0:T(8,128)S(1)}, f32[3,1,8,640]{3,2,1,0:T(8,128)S(1)}, u32[]{:S(2)}, u32[]{:S(2)}) collective-permute-start(f32[3,1,8,640]{3,2,1,0:T(8,128)S(1)} %get-tuple-element.59), channel_id=1, source_target_pairs={{0,16},{16,32},{32,48},{48,64},{64,80},{80,96},{96,112},{112,0},{1... | collective-permute-start | bytes 184328 | tf_op jit(solution)/shard_map/ppermute | solution.py:703
  40.1 4.8 %collective-permute-start.9 = (f32[3,1,8,640]{3,2,1,0:T(8,128)S(1)}, f32[3,1,8,640]{3,2,1,0:T(8,128)S(1)}, u32[]{:S(2)}, u32[]{:S(2)}) collective-permute-start(f32[3,1,8,640]{3,2,1,0:T(8,128)S(1)} %get-tuple-element.60), channel_id=1, source_target_pairs={{0,112},{16,0},{32,16},{48,32},{64,48},{80,64},{96,80},{112,96},{1... | collective-permute-start | bytes 184328 | tf_op jit(solution)/shard_map/ppermute | solution.py:703
  46.8 5.1 %collective-permute-start.10 = (f32[2,2,8,640]{3,2,1,0:T(8,128)S(1)}, f32[2,2,8,640]{3,2,1,0:T(8,128)S(1)}, u32[]{:S(2)}, u32[]{:S(2)}) collective-permute-start(f32[2,2,8,640]{3,2,1,0:T(8,128)S(1)} %get-tuple-element.63), channel_id=1, source_target_pairs={{0,16},{16,32},{32,48},{48,64},{64,80},{80,96},{96,112},{112,0},{1... | collective-permute-start | bytes 245768 | tf_op jit(solution)/shard_map/ppermute | solution.py:703
  46.8 5.1 %collective-permute-start.11 = (f32[2,2,8,640]{3,2,1,0:T(8,128)S(1)}, f32[2,2,8,640]{3,2,1,0:T(8,128)S(1)}, u32[]{:S(2)}, u32[]{:S(2)}) collective-permute-start(f32[2,2,8,640]{3,2,1,0:T(8,128)S(1)} %get-tuple-element.64), channel_id=1, source_target_pairs={{0,112},{16,0},{32,16},{48,32},{64,48},{80,64},{96,80},{112,96},{1... | collective-permute-start | bytes 245768 | tf_op jit(solution)/shard_map/ppermute | solution.py:703
  53.4 6.9 %collective-permute-start.12 = (f32[3,4,8,640]{3,2,1,0:T(8,128)S(1)}, f32[3,4,8,640]{3,2,1,0:T(8,128)S(1)}, u32[]{:S(2)}, u32[]{:S(2)}) collective-permute-start(f32[3,4,8,640]{3,2,1,0:T(8,128)S(1)} %get-tuple-element.67), channel_id=1, source_target_pairs={{0,16},{16,32},{32,48},{48,64},{64,80},{80,96},{96,112},{112,0},{1... | collective-permute-start | bytes 737288 | tf_op jit(solution)/shard_map/ppermute | solution.py:703
  53.4 6.8 %collective-permute-start.13 = (f32[3,4,8,640]{3,2,1,0:T(8,128)S(1)}, f32[3,4,8,640]{3,2,1,0:T(8,128)S(1)}, u32[]{:S(2)}, u32[]{:S(2)}) collective-permute-start(f32[3,4,8,640]{3,2,1,0:T(8,128)S(1)} %get-tuple-element.68), channel_id=1, source_target_pairs={{0,112},{16,0},{32,16},{48,32},{64,48},{80,64},{96,80},{112,96},{1... | collective-permute-start | bytes 737288 | tf_op jit(solution)/shard_map/ppermute | solution.py:703
